TPU v7x, 32 devices: a whole 2x2x4 slice. The times are simulated.
32 devices in a mesh: dp: 4 (over y, core), ctx: 4 (over z), tp: 2 (over x).
Axes of the slice: x: 2, y: 2, z: 4, core: 2. Of those that a mesh axis runs over, the one named last changes fastest.
Arguments:
- tokens: bfloat16 [8192, 1536], P(('dp', 'ctx')), may hold values from -6 to 6
- cotangent: bfloat16 [8192, 1536], P(('dp', 'ctx')), may hold values from -6 to 6
- lengths: int32 [4, 4], P('dp'), may hold values from 1 to 1024, as said below
- block_order: int32 [4, 8, 4], P('dp'), may hold values from 0 to 3, each once within a row
- pre_gain: bfloat16 [1536], P(('dp', 'ctx')), may hold values from 0.5 to 1.5
- query_weight: bfloat16 [1536, 1536], P(('dp', 'ctx'), 'tp'), may hold values from -0.15625 to 0.15625
- key_weight: bfloat16 [1536, 768], P(('dp', 'ctx'), 'tp'), may hold values from -0.15625 to 0.15625
- value_weight: bfloat16 [1536, 768], P(('dp', 'ctx'), 'tp'), may hold values from -0.15625 to 0.15625
- output_weight: bfloat16 [1536, 1536], P(('dp', 'ctx'), 'tp'), may hold values from -2.5 to 2.5
- mid_gain: bfloat16 [1536], P(('dp', 'ctx')), may hold values from 0.5 to 1.5
- gate_weight: bfloat16 [1536, 4096], P(('dp', 'ctx'), 'tp'), may hold values from -0.15625 to 0.15625
- up_weight: bfloat16 [1536, 4096], P(('dp', 'ctx'), 'tp'), may hold values from -0.15625 to 0.15625
- down_weight: bfloat16 [1536, 4096], P(('dp', 'ctx'), 'tp'), may hold values from -0.09375 to 0.09375
Outputs:
- result: bfloat16 [8192, 1536], P(('dp', 'ctx'))
- token_gradient: bfloat16 [8192, 1536], P(('dp', 'ctx'))
- pre_gradient: float32 [1536], P(('dp', 'ctx'))
- query_gradient: float32 [1536, 1536], P(('dp', 'ctx'), 'tp')
- key_gradient: float32 [1536, 768], P(('dp', 'ctx'), 'tp')
- value_gradient: float32 [1536, 768], P(('dp', 'ctx'), 'tp')
- output_gradient: float32 [1536, 1536], P(('dp', 'ctx'), 'tp')
- mid_gradient: float32 [1536], P(('dp', 'ctx'))
- gate_gradient: float32 [1536, 4096], P(('dp', 'ctx'), 'tp')
- up_gradient: float32 [1536, 4096], P(('dp', 'ctx'), 'tp')
- down_gradient: float32 [1536, 4096], P(('dp', 'ctx'), 'tp')
Inputs may be any that keep to these rules, and one draw needn't show every extreme that they name: The lengths of a data index sum to 2048; the longest is max(1024, 1023).
All inputs are finite; a program needn't handle non-finite values.
Results may differ from a plain program's by a relative error of at most 0.019.
Values may be sent and summed in bfloat16 or wider, within the bound.
A program may use at most 192 MiB of HBM per device.

v0:
```python
import math

import jax
import jax.numpy as jnp
from jax import lax
from jax.sharding import PartitionSpec as P

HEAD_SIZE = 96
BLOCK = 64


epsilon = 1e-05
rotary_base = 100000.0
masked_score = -1e30


def times(left, right):
    return jnp.dot(left, right, preferred_element_type=jnp.float32)


def times_across(left, right):
    return lax.dot_general(
        left, right, (((1,), (1,)), ((), ())), preferred_element_type=jnp.float32
    )


def over_rows(left, right):
    return lax.dot_general(
        left, right, (((0,), (0,)), ((), ())), preferred_element_type=jnp.float32
    )


def places(lengths, block_order, count):
    rounds = block_order.shape[0]
    within = jnp.arange(rounds * BLOCK, dtype=jnp.int32)
    owner = jnp.repeat(block_order.T, BLOCK, axis=1)
    stream = (
        (owner + (within // BLOCK)[None, :] * count) * BLOCK + (within % BLOCK)[None, :]
    ).reshape(-1)
    ends = jnp.cumsum(lengths)
    starts = ends - lengths
    segment = jnp.sum((stream[:, None] >= ends[None, :]).astype(jnp.int32), axis=1)
    labels = jnp.arange(lengths.shape[0], dtype=jnp.int32)
    first = jnp.sum(jnp.where(segment[:, None] == labels[None, :], starts[None, :], 0), axis=1)
    return (segment, stream - first)


def angles(place):
    half = HEAD_SIZE // 2
    frequency = rotary_base ** (-(jnp.arange(half, dtype=jnp.float32) * 2.0 / HEAD_SIZE))
    turn = place.astype(jnp.float32)[:, None] * frequency[None, :]
    return (jnp.cos(turn), jnp.sin(turn))


def rotate(field, cosine, sine, sign):
    rows = field.shape[0]
    head_outputs = field.shape[1] // HEAD_SIZE
    half = HEAD_SIZE // 2
    shaped = field.reshape(rows, head_outputs, HEAD_SIZE)
    first = shaped[:, :, :half]
    second = shaped[:, :, half:]
    across = cosine[:, None, :]
    along = sign * sine[:, None, :]
    output = jnp.concatenate(
        [first * across - second * along, second * across + first * along], axis=2
    )
    return output.reshape(rows, head_outputs * HEAD_SIZE)


def norm_back(upstream, unit, scale, gain):
    inner = upstream * gain
    return scale * (inner - unit * jnp.mean(inner * unit, axis=1, keepdims=True))


def split_heads(field, groups):
    return field.reshape(field.shape[0], groups, field.shape[1] // (groups * HEAD_SIZE), HEAD_SIZE)


def block_scores(query_split, keys_block, query_segment, query_place, key_segment, key_place):
    groups = query_split.shape[1]
    key_split = keys_block.reshape(keys_block.shape[0], groups, HEAD_SIZE)
    raw = jnp.einsum(
        "nixv,wiv->ixnw", query_split, key_split, preferred_element_type=jnp.float32
    ) * HEAD_SIZE ** (-0.5)
    allowed = (query_segment[:, None] == key_segment[None, :]) & (
        key_place[None, :] <= query_place[:, None]
    )
    return (raw, allowed)


def attend(query_split, keys_all, values_all, query_segment, query_place, key_segment, key_place):
    length = keys_all.shape[0]
    step = math.gcd(length, 512)
    count = length // step
    rows, groups, ratio = (query_split.shape[0], query_split.shape[1], query_split.shape[2])
    width = keys_all.shape[1]
    blocks = (
        keys_all.reshape(count, step, width),
        values_all.reshape(count, step, width),
        key_segment.reshape(count, step),
        key_place.reshape(count, step),
    )

    def first_pass(carry, block):
        top, total = carry
        raw, allowed = block_scores(
            query_split, block[0], query_segment, query_place, block[2], block[3]
        )
        masked = jnp.where(allowed, raw, masked_score)
        new_top = jnp.maximum(top, jnp.max(masked, axis=3, keepdims=True))
        weights = jnp.where(allowed, jnp.exp(masked - new_top), 0.0)
        total = total * jnp.exp(top - new_top) + jnp.sum(weights, axis=3, keepdims=True)
        return ((new_top, total), None)

    begin = jnp.full((groups, ratio, rows, 1), masked_score, jnp.float32)
    (top, total), unused = lax.scan(first_pass, (begin, jnp.zeros_like(begin)), blocks)
    logsum = top + jnp.log(total)

    def second_pass(carry, block):
        raw, allowed = block_scores(
            query_split, block[0], query_segment, query_place, block[2], block[3]
        )
        softmax_lower = jnp.where(allowed, jnp.exp(raw - logsum), 0.0).astype(jnp.bfloat16)
        value_split = block[1].reshape(step, groups, HEAD_SIZE)
        return (
            carry
            + jnp.einsum(
                "omkw,woq->komq", softmax_lower, value_split, preferred_element_type=jnp.float32
            ),
            None,
        )

    attended_rows, unused = lax.scan(
        second_pass, jnp.zeros((rows, groups, ratio, HEAD_SIZE), jnp.float32), blocks
    )
    return (attended_rows, logsum)


def attend_back(
    query_split,
    head_gradients,
    delta,
    logsum,
    keys_all,
    values_all,
    query_segment,
    query_place,
    key_segment,
    key_place,
):
    length = keys_all.shape[0]
    step = math.gcd(length, 512)
    count = length // step
    rows, groups, ratio = (query_split.shape[0], query_split.shape[1], query_split.shape[2])
    width = keys_all.shape[1]
    scale = HEAD_SIZE ** (-0.5)
    blocks = (
        keys_all.reshape(count, step, width),
        values_all.reshape(count, step, width),
        key_segment.reshape(count, step),
        key_place.reshape(count, step),
    )

    def back_pass(carry, block):
        raw, allowed = block_scores(
            query_split, block[0], query_segment, query_place, block[2], block[3]
        )
        softmax_weights = jnp.where(allowed, jnp.exp(raw - logsum), 0.0)
        key_split = block[0].reshape(step, groups, HEAD_SIZE)
        value_split = block[1].reshape(step, groups, HEAD_SIZE)
        back_share = jnp.einsum(
            "nixv,wiv->ixnw", head_gradients, value_split, preferred_element_type=jnp.float32
        )
        score_gradients = (softmax_weights * (back_share - delta)).astype(jnp.bfloat16)
        carry = (
            carry
            + jnp.einsum(
                "omkw,woq->komq", score_gradients, key_split, preferred_element_type=jnp.float32
            )
            * scale
        )
        key_part = (
            jnp.einsum(
                "znyo,yznc->ozc", score_gradients, query_split, preferred_element_type=jnp.float32
            )
            * scale
        )
        value_part = jnp.einsum(
            "znyo,yznc->ozc",
            softmax_weights.astype(jnp.bfloat16),
            head_gradients,
            preferred_element_type=jnp.float32,
        )
        return (carry, (key_part.reshape(step, width), value_part.reshape(step, width)))

    back_queries, (key_parts, value_parts) = lax.scan(
        back_pass, jnp.zeros((rows, groups, ratio, HEAD_SIZE), jnp.float32), blocks
    )
    return (back_queries, key_parts.reshape(length, width), value_parts.reshape(length, width))


def body(
    tokens,
    cotangent,
    lengths,
    block_order,
    pre_gain,
    query_weight,
    key_weight,
    value_weight,
    output_weight,
    mid_gain,
    gate_weight,
    up_weight,
    down_weight,
):
    count = lax.axis_size("ctx")
    rows = tokens.shape[0]
    key_segment, key_place = places(lengths[0], block_order[0], count)
    offset = lax.axis_index("ctx") * rows
    query_segment = lax.dynamic_slice_in_dim(key_segment, offset, rows)
    query_place = lax.dynamic_slice_in_dim(key_place, offset, rows)
    gathered = (
        lax.all_gather(pre_gain, ("dp", "ctx"), axis=0, tiled=True),
        lax.all_gather(query_weight, ("dp", "ctx"), axis=0, tiled=True),
        lax.all_gather(key_weight, ("dp", "ctx"), axis=0, tiled=True),
        lax.all_gather(value_weight, ("dp", "ctx"), axis=0, tiled=True),
        lax.all_gather(output_weight, ("dp", "ctx"), axis=0, tiled=True),
        lax.all_gather(mid_gain, ("dp", "ctx"), axis=0, tiled=True),
        lax.all_gather(gate_weight, ("dp", "ctx"), axis=0, tiled=True),
        lax.all_gather(up_weight, ("dp", "ctx"), axis=0, tiled=True),
        lax.all_gather(down_weight, ("dp", "ctx"), axis=0, tiled=True),
    )
    (
        pre_all,
        query_full,
        key_full,
        value_full,
        output_full,
        mid_all,
        gate_full,
        up_full,
        down_full,
    ) = gathered
    pre_all = pre_all.astype(jnp.float32)
    mid_all = mid_all.astype(jnp.float32)
    groups = key_full.shape[1] // HEAD_SIZE
    inputs = tokens.astype(jnp.float32)
    pre_scale = lax.rsqrt(jnp.mean(inputs * inputs, axis=1, keepdims=True) + epsilon)
    pre_unit = inputs * pre_scale
    normed = (pre_unit * pre_all).astype(jnp.bfloat16)
    cosine, sine = angles(query_place)
    queries = rotate(times(normed, query_full), cosine, sine, 1.0).astype(jnp.bfloat16)
    keys = rotate(times(normed, key_full), cosine, sine, 1.0).astype(jnp.bfloat16)
    values = times(normed, value_full).astype(jnp.bfloat16)
    keys_all, values_all = (
        lax.all_gather(keys, "ctx", axis=0, tiled=True),
        lax.all_gather(values, "ctx", axis=0, tiled=True),
    )
    query_split = split_heads(queries, groups)
    attended_heads, logsum = attend(
        query_split, keys_all, values_all, query_segment, query_place, key_segment, key_place
    )
    attended_low = attended_heads.reshape(rows, -1).astype(jnp.bfloat16)
    branch = lax.psum(times_across(attended_low, output_full).astype(jnp.bfloat16), "tp").astype(
        jnp.float32
    )
    middle = inputs + branch
    mid_scale = lax.rsqrt(jnp.mean(middle * middle, axis=1, keepdims=True) + epsilon)
    mid_unit = middle * mid_scale
    mid_normed = (mid_unit * mid_all).astype(jnp.bfloat16)
    gate = times(mid_normed, gate_full)
    upward = times(mid_normed, up_full)
    sigmoid = jax.nn.sigmoid(gate)
    activated = gate * sigmoid
    mixed = (activated * upward).astype(jnp.bfloat16)
    feed = lax.psum(times_across(mixed, down_full).astype(jnp.bfloat16), "tp").astype(jnp.float32)
    result = (middle + feed).astype(jnp.bfloat16)
    upstream = cotangent.astype(jnp.float32)
    down_gradient = over_rows(cotangent, mixed)
    back_mixed = times(cotangent, down_full)
    back_gate = (back_mixed * upward * sigmoid * (1.0 + gate * (1.0 - sigmoid))).astype(
        jnp.bfloat16
    )
    back_up = (back_mixed * activated).astype(jnp.bfloat16)
    gate_gradient = over_rows(mid_normed, back_gate)
    up_gradient = over_rows(mid_normed, back_up)
    back_mid = lax.psum(
        (times_across(back_gate, gate_full) + times_across(back_up, up_full)).astype(jnp.bfloat16),
        "tp",
    ).astype(jnp.float32)
    mid_gradient = jnp.sum(back_mid * mid_unit, axis=0)
    back_middle = upstream + norm_back(back_mid, mid_unit, mid_scale, mid_all)
    back_branch = back_middle.astype(jnp.bfloat16)
    output_gradient = over_rows(back_branch, attended_low)
    back_attended = times(back_branch, output_full).astype(jnp.bfloat16)
    head_gradients = split_heads(back_attended, groups)
    delta = jnp.sum(head_gradients * attended_heads, axis=3).transpose(1, 2, 0)[..., None]
    back_queries, key_total, value_total = attend_back(
        query_split,
        head_gradients,
        delta,
        logsum,
        keys_all,
        values_all,
        query_segment,
        query_place,
        key_segment,
        key_place,
    )
    own_keys, own_values = (
        lax.psum_scatter(
            key_total.astype(jnp.bfloat16), "ctx", scatter_dimension=0, tiled=True
        ).astype(jnp.float32),
        lax.psum_scatter(
            value_total.astype(jnp.bfloat16), "ctx", scatter_dimension=0, tiled=True
        ).astype(jnp.float32),
    )
    query_cotangent = rotate(back_queries.reshape(rows, -1), cosine, sine, -1.0).astype(
        jnp.bfloat16
    )
    key_cotangent = rotate(own_keys, cosine, sine, -1.0).astype(jnp.bfloat16)
    value_cotangent = own_values.astype(jnp.bfloat16)
    query_gradient = over_rows(normed, query_cotangent)
    key_gradient = over_rows(normed, key_cotangent)
    value_gradient = over_rows(normed, value_cotangent)
    partial_normed = (
        times_across(query_cotangent, query_full)
        + times_across(key_cotangent, key_full)
        + times_across(value_cotangent, value_full)
    )
    back_normed = lax.psum(partial_normed.astype(jnp.bfloat16), "tp").astype(jnp.float32)
    pre_gradient = jnp.sum(back_normed * pre_unit, axis=0)
    token_gradient = (back_middle + norm_back(back_normed, pre_unit, pre_scale, pre_all)).astype(
        jnp.bfloat16
    )
    every = (
        lax.psum_scatter(pre_gradient, ("dp", "ctx"), scatter_dimension=0, tiled=True),
        lax.psum_scatter(query_gradient, ("dp", "ctx"), scatter_dimension=0, tiled=True),
        lax.psum_scatter(key_gradient, ("dp", "ctx"), scatter_dimension=0, tiled=True),
        lax.psum_scatter(value_gradient, ("dp", "ctx"), scatter_dimension=0, tiled=True),
        lax.psum_scatter(output_gradient, ("dp", "ctx"), scatter_dimension=0, tiled=True),
        lax.psum_scatter(mid_gradient, ("dp", "ctx"), scatter_dimension=0, tiled=True),
        lax.psum_scatter(gate_gradient, ("dp", "ctx"), scatter_dimension=0, tiled=True),
        lax.psum_scatter(up_gradient, ("dp", "ctx"), scatter_dimension=0, tiled=True),
        lax.psum_scatter(down_gradient, ("dp", "ctx"), scatter_dimension=0, tiled=True),
    )
    return (
        result,
        token_gradient,
        every[0],
        every[1],
        every[2],
        every[3],
        every[4],
        every[5],
        every[6],
        every[7],
        every[8],
    )


def solution(mesh):
    return jax.shard_map(
        body,
        mesh=mesh,
        in_specs=(
            P(("dp", "ctx"), None),
            P(("dp", "ctx"), None),
            P("dp", None),
            P("dp", None, None),
            P(("dp", "ctx")),
            P(("dp", "ctx"), "tp"),
            P(("dp", "ctx"), "tp"),
            P(("dp", "ctx"), "tp"),
            P(("dp", "ctx"), "tp"),
            P(("dp", "ctx")),
            P(("dp", "ctx"), "tp"),
            P(("dp", "ctx"), "tp"),
            P(("dp", "ctx"), "tp"),
        ),
        out_specs=(
            P(("dp", "ctx"), None),
            P(("dp", "ctx"), None),
            P(("dp", "ctx")),
            P(("dp", "ctx"), "tp"),
            P(("dp", "ctx"), "tp"),
            P(("dp", "ctx"), "tp"),
            P(("dp", "ctx"), "tp"),
            P(("dp", "ctx")),
            P(("dp", "ctx"), "tp"),
            P(("dp", "ctx"), "tp"),
            P(("dp", "ctx"), "tp"),
        ),
        check_vma=False,
    )
```

profile of v0, /device:TPU:0, one launch (start us, length us, event | category | flops | bytes accessed | tf_op | source)
XLA Modules:
  0.0 1557.3 jit_solution(2170138641546879265)
XLA Ops:
  14.9 36.5 %all-reduce.5 = (bf16[1536]{0:T(1024)(128)(2,1)S(1)}, bf16[1536]{0:T(1024)(128)(2,1)S(1)}) all-reduce(bf16[1536]{0:T(1024)(128)(2,1)S(1)} %dynamic-update-slice, bf16[1536]{0:T(1024)(128)(2,1)S(1)} %dynamic-update-slice.1), channel_id=1, replica_groups=mesh['dp'=4,'ctx'=4,'tp'=2] {'dp','ctx'}, use_global_device_ids=true, to_apply=%add | all-reduce | flops 3072 | bytes 12288
  59.0 32.3 %all-gather.10.cloned.1.call-done = bf16[1536,384]{1,0:T(8,128)(2,1)} async-done(((bf16[96,384]{1,0:T(8,128)(2,1)}), bf16[1536,384]{1,0:T(8,128)(2,1)}) %all-gather.10.cloned.1.call-update) | async-done | bytes 1179664 | tf_op jit(solution)/shard_map/all_gather | solution.py:227
  96.1 38.8 %all-gather.18.cloned.1.call-done = bf16[1536,768]{1,0:T(8,128)(2,1)} async-done(((bf16[96,768]{1,0:T(8,128)(2,1)}), bf16[1536,768]{1,0:T(8,128)(2,1)}) %all-gather.18.cloned.1.call-update) | async-done | bytes 2359312 | tf_op jit(solution)/shard_map/all_gather | solution.py:225
  138.4 34.4 %all-gather.16.cloned.1.call-done = bf16[2048,384]{0,1:T(8,128)(2,1)} async-done(((bf16[512,384]{0,1:T(8,128)(2,1)}), bf16[2048,384]{0,1:T(8,128)(2,1)}) %all-gather.16.cloned.1.call-update) | async-done | bytes 1572880 | tf_op jit(solution)/shard_map/all_gather | solution.py:257
  177.9 46.0 %while.39 = (s32[]{:T(128)}, f32[4,2,512,1]{2,1,0,3:T(2,128)S(1)}, f32[4,2,512,1]{2,1,0,3:T(2,128)S(1)}, s32[512]{0:T(512)S(1)}, s32[4,512]{1,0:T(4,128)}, /*ind...) while((s32[]{:T(128)}, f32[4,2,512,1]{2,1,0,3:T(2,128)S(1)}, ...), condition=%wide.region_7.8_spmd.clone, body=%wide.region_4.7_spmd.clone.sunk | while | flops 420237312 | bytes 19759232 | solution.py:116
  180.0 4.9 fusion.151
  191.5 4.9 fusion.151
  203.0 4.9 fusion.151
  214.5 4.9 fusion.151
  226.6 27.8 %while.40 = (s32[]{:T(128)}, f32[512,4,2,96]{0,3,2,1:T(8,128)}, bf16[4,512,384]{1,2,0:T(8,128)(2,1)}, s32[512]{0:T(512)S(1)}, s32[4,512]{1,0:T(4,128)}, /*index=...) while((s32[]{:T(128)}, f32[512,4,2,96]{0,3,2,1:T(8,128)}, ...), condition=%wide.region_9.10_spmd.clone, body=%wide.region_8.9_spmd.clone.sunk | while | flops 815267840 | bytes 6848647 | solution.py:133
  234.7 5.1 bitcast_add_fusion.7
  242.0 5.1 bitcast_add_fusion.7
  249.3 5.1 bitcast_add_fusion.7
  263.2 47.9 %all-reduce.11.cloned.1.call-done = bf16[512,1536]{1,0:T(8,128)(2,1)} async-done(((bf16[512,1536]{1,0:T(8,128)(2,1)}), bf16[512,1536]{1,0:T(8,128)(2,1)}) %all-reduce.11.cloned.1.call-update) | async-done | bytes 1572880 | tf_op jit(solution)/shard_map/psum | solution.py:265
  315.1 60.5 %all-gather.22.cloned.1.call-done = bf16[1536,2048]{1,0:T(8,128)(2,1)} async-done(((bf16[96,2048]{1,0:T(8,128)(2,1)}), bf16[1536,2048]{1,0:T(8,128)(2,1)}) %all-gather.22.cloned.1.call-update) | async-done | bytes 6291472 | tf_op jit(solution)/shard_map/all_gather | solution.py:230
  375.6 8.7 fusion.74
  384.3 54.3 %all-gather.24.cloned.1.call-done = bf16[1536,2048]{1,0:T(8,128)(2,1)} async-done(((bf16[96,2048]{1,0:T(8,128)(2,1)}), bf16[1536,2048]{1,0:T(8,128)(2,1)}) %all-gather.24.cloned.1.call-update) | async-done | bytes 6291472 | tf_op jit(solution)/shard_map/all_gather | solution.py:231
  438.7 8.7 fusion.75
  447.4 54.2 %all-gather.26.cloned.1.call-done = bf16[1536,2048]{1,0:T(8,128)(2,1)} async-done(((bf16[96,2048]{1,0:T(8,128)(2,1)}), bf16[1536,2048]{1,0:T(8,128)(2,1)}) %all-gather.26.cloned.1.call-update) | async-done | bytes 6291472 | tf_op jit(solution)/shard_map/all_gather | solution.py:232
  501.6 11.7 multiply_convert_fusion
  513.3 7.4 fusion.76
  525.5 50.2 %all-reduce.13.cloned.1.call-done = bf16[512,1536]{1,0:T(8,128)(2,1)} async-done(((bf16[512,1536]{1,0:T(8,128)(2,1)}), bf16[512,1536]{1,0:T(8,128)(2,1)}) %all-reduce.13.cloned.1.call-update) | async-done | bytes 1572880 | tf_op jit(solution)/shard_map/psum | solution.py:288
  579.6 4.7 convolution_convert_fusion.2
  588.0 92.0 %while.41 = (s32[]{:T(128)}, f32[512,4,2,96]{0,3,2,1:T(8,128)}, bf16[4,512,384]{2,1,0:T(8,128)(2,1)}, bf16[4,512,384]{2,1,0:T(8,128)(2,1)}, bf16[4,512,384]{1,2,...) while((s32[]{:T(128)}, f32[512,4,2,96]{0,3,2,1:T(8,128)}, ...), condition=%wide.region_17.18_spmd.clone, body=%wide.region_16.17_spmd.clone.sunk | while | flops 2036596736 | bytes 109380464 | solution.py:196
  598.1 6.1 fusion.168
  620.7 6.1 fusion.168
  643.9 6.1 fusion.168
  667.0 6.1 fusion.168
  675.3 4.7 bitcast_add_fusion.8
  681.1 8.1 convolution_convert_fusion
  694.3 21.2 %reduce-scatter.12.cloned.1.call-done = bf16[512,384]{1,0:T(8,128)(2,1)} async-done(((bf16[2048,384]{1,0:T(8,128)(2,1)}), bf16[512,384]{1,0:T(8,128)(2,1)}) %reduce-scatter.12.cloned.1.call-update) | async-done | bytes 393232 | tf_op jit(solution)/shard_map/reduce_scatter | solution.py:312
  716.8 5.0 convolution_add_fusion.1
  721.9 30.2 %reduce-scatter.14.cloned.1.call-done = bf16[512,384]{1,0:T(8,128)(2,1)} async-done(((bf16[2048,384]{1,0:T(8,128)(2,1)}), bf16[512,384]{1,0:T(8,128)(2,1)}) %reduce-scatter.14.cloned.1.call-update) | async-done | bytes 393232 | tf_op jit(solution)/shard_map/reduce_scatter | solution.py:315
  763.1 6.7 fusion.46
  770.5 4.9 fusion.62
  775.4 10.1 fusion.78
  785.6 10.1 fusion.79
  795.9 10.9 convolution_bitcast_fusion.1
  806.7 12.9 copy.117
  820.3 21.1 %all-reduce.15.cloned.1.call-done = (bf16[512,1536]{1,0:T(8,128)(2,1)}, bf16[512,1536]{1,0:T(8,128)(2,1)}) async-done(((bf16[512,1536]{1,0:T(8,128)(2,1)}, bf16[512,1536]{1,0:T(8,128)(2,1)}), (bf16[512,1536]{1,0:T(8,128)(2,1)}, bf16[512,1536]{1,0:T(8,128)(2,1)})) %all-reduce.15.cloned.1.call-update) | async-done | bytes 3145744 | tf_op jit(solution)/shard_map/psum | solution.py:277
  843.9 61.9 %all-reduce.4 = (f32[1536]{0:T(1024)S(1)}, f32[1536]{0:T(1024)S(1)}) all-reduce(f32[1536]{0:T(1024)S(1)} %get-tuple-element.512, f32[1536]{0:T(1024)S(1)} %copy-done.26), channel_id=4, replica_groups=mesh['dp'=4,'ctx'=4,'tp'=2] {'dp','ctx'}, use_global_device_ids=true, to_apply=%region_23.24.clone | all-reduce | flops 3072 | bytes 24576
  906.9 5.7 fusion.34
  912.7 62.6 %reduce-scatter.20.cloned.1.call-done = f32[96,384]{1,0:T(8,128)} async-done(((f32[1536,384]{1,0:T(8,128)}), f32[96,384]{1,0:T(8,128)}) %reduce-scatter.20.cloned.1.call-update) | async-done | bytes 147472 | tf_op jit(solution)/shard_map/reduce_scatter | solution.py:341
  975.3 79.4 %reduce-scatter.22.cloned.1.call-done = f32[96,768]{1,0:T(8,128)} async-done(((f32[1536,768]{1,0:T(8,128)}), f32[96,768]{1,0:T(8,128)}) %reduce-scatter.22.cloned.1.call-update) | async-done | bytes 294928 | tf_op jit(solution)/shard_map/reduce_scatter | solution.py:342
  1054.7 78.9 %reduce-scatter.16.cloned.1.call-done = f32[96,768]{1,0:T(8,128)} async-done(((f32[1536,768]{1,0:T(8,128)}), f32[96,768]{1,0:T(8,128)}) %reduce-scatter.16.cloned.1.call-update) | async-done | bytes 294928 | tf_op jit(solution)/shard_map/reduce_scatter | solution.py:339
  1133.6 138.9 %reduce-scatter.24.cloned.1.call-done = f32[96,2048]{1,0:T(8,128)} async-done(((f32[1536,2048]{1,0:T(8,128)}), f32[96,2048]{1,0:T(8,128)}) %reduce-scatter.24.cloned.1.call-update) | async-done | bytes 786448 | tf_op jit(solution)/shard_map/reduce_scatter | solution.py:344
  1272.4 138.8 %reduce-scatter.26.cloned.1.call-done = f32[96,2048]{1,0:T(8,128)} async-done(((f32[1536,2048]{1,0:T(8,128)}), f32[96,2048]{1,0:T(8,128)}) %reduce-scatter.26.cloned.1.call-update) | async-done | bytes 786448 | tf_op jit(solution)/shard_map/reduce_scatter | solution.py:345
  1411.3 139.0 %reduce-scatter.28.cloned.1.call-done = f32[96,2048]{1,0:T(8,128)} async-done(((f32[1536,2048]{1,0:T(8,128)}), f32[96,2048]{1,0:T(8,128)}) %reduce-scatter.28.cloned.1.call-update) | async-done | bytes 786448
  (321 shorter events, 179.3 us)
Async XLA Ops:
  7.2 48.0 %all-gather.14.cloned.1.call-start = ((), (), s32[]{:S(2)}) async-start(), calls=%async_computation.11 | async-start | bytes 1253376 | tf_op jit(solution)/shard_map/all_gather | solution.py:226
  7.9 83.4 %all-gather.10.cloned.1.call-start = ((), (), s32[]{:S(2)}) async-start(), calls=%async_computation.9 | async-start | bytes 1253376 | tf_op jit(solution)/shard_map/all_gather | solution.py:227
  8.7 126.2 %all-gather.18.cloned.1.call-start = ((), (), s32[]{:S(2)}) async-start(), calls=%async_computation.13 | async-start | bytes 2506752 | tf_op jit(solution)/shard_map/all_gather | solution.py:225
  9.4 163.4 %all-gather.16.cloned.1.call-start = ((), (), s32[]{:S(2)}) async-start(), calls=%async_computation.12 | async-start | bytes 1966080 | tf_op jit(solution)/shard_map/all_gather | solution.py:257
  51.3 83.5 %copy-start.19 = (f32[1536]{0:T(1024)}, f32[1536]{0:T(1024)S(1)}, u32[]{:S(2)}) copy-start(f32[1536]{0:T(1024)S(1)} %convert_element_type.123) | copy-start | bytes 18436
  54.1 80.8 %copy-start.23 = (f32[512]{0:T(512)}, f32[512]{0:T(512)S(1)}, u32[]{:S(2)}) copy-start(f32[512]{0:T(512)S(1)} %add_rsqrt_fusion.1) | copy-start | bytes 6148
  55.2 82.9 %copy-start.12 = (f32[512,48]{0,1:T(8,128)}, f32[512,48]{0,1:T(8,128)S(1)}, u32[]{:S(2)}) copy-start(f32[512,48]{0,1:T(8,128)S(1)} %get-tuple-element.613) | copy-start | bytes 294916
  55.2 36.1 %copy-start.2 = (bf16[512,1536]{1,0:T(8,128)(2,1)S(1)}, bf16[512,1536]{1,0:T(8,128)(2,1)}, u32[]{:S(2)}) copy-start(bf16[512,1536]{1,0:T(8,128)(2,1)} %param.19) | copy-start | bytes 4718596
  58.9 165.1 %all-gather.12.cloned.1.call-start = ((), (), s32[]{:S(2)}) async-start(), calls=%async_computation.10 | async-start | bytes 1966080 | tf_op jit(solution)/shard_map/all_gather | solution.py:258
  94.4 161.6 %all-gather.20.cloned.1.call-start = ((), (), s32[]{:S(2)}) async-start(), calls=%async_computation.14 | async-start | bytes 2506752 | tf_op jit(solution)/shard_map/all_gather | solution.py:228
  95.0 216.2 %all-reduce.11.cloned.1.call-start = ((), (), s32[]{:S(2)}) async-start(), calls=%async_computation.15 | async-start | bytes 3145728 | tf_op jit(solution)/shard_map/psum | solution.py:265
  254.4 6.1 copy-start.30
  255.9 4.6 copy-start.17
  260.6 115.0 %all-gather.22.cloned.1.call-start = ((), (), s32[]{:S(2)}) async-start(), calls=%async_computation.16 | async-start | bytes 6684672 | tf_op jit(solution)/shard_map/all_gather | solution.py:230
  261.3 177.3 %all-gather.24.cloned.1.call-start = ((), (), s32[]{:S(2)}) async-start(), calls=%async_computation.17 | async-start | bytes 6684672 | tf_op jit(solution)/shard_map/all_gather | solution.py:231
  262.1 239.5 %all-gather.26.cloned.1.call-start = ((), (), s32[]{:S(2)}) async-start(), calls=%async_computation.18 | async-start | bytes 6684672 | tf_op jit(solution)/shard_map/all_gather | solution.py:232
  262.6 313.0 %all-reduce.13.cloned.1.call-start = ((), (), s32[]{:S(2)}) async-start(), calls=%async_computation.19 | async-start | bytes 3145728 | tf_op jit(solution)/shard_map/psum | solution.py:288
  263.2 316.3 %copy-start.21 = (f32[1536]{0:T(1024)}, f32[1536]{0:T(1024)S(1)}, u32[]{:S(2)}) copy-start(f32[1536]{0:T(1024)S(1)} %convert_element_type.134) | copy-start | bytes 18436
  313.3 266.2 %copy-start.27 = (f32[512]{0:T(512)}, f32[512]{0:T(512)S(1)}, u32[]{:S(2)}) copy-start(f32[512]{0:T(512)S(1)} %add_rsqrt_fusion) | copy-start | bytes 6148
  513.3 7.4 copy-start.37
  513.3 7.4 copy-start.36
  513.3 7.4 copy-start.34
  525.4 190.1 %reduce-scatter.12.cloned.1.call-start = ((), (), s32[]{:S(2)}) async-start(), calls=%async_computation.20 | async-start | bytes 1966080 | tf_op jit(solution)/shard_map/reduce_scatter | solution.py:312
  579.5 4.8 copy-start.32
  588.0 4.8 copy-start.10
  610.6 4.8 copy-start.10
  614.1 4.4 copy-start
  629.1 4.7 copy-start.11
  633.8 4.8 copy-start.10
  652.2 4.7 copy-start.11
  656.9 4.8 copy-start.10
  675.3 4.7 copy-start.11
  680.1 72.1 %reduce-scatter.14.cloned.1.call-start = ((), (), s32[]{:S(2)}) async-start(), calls=%async_computation.21 | async-start | bytes 1966080 | tf_op jit(solution)/shard_map/reduce_scatter | solution.py:315
  680.8 160.6 %all-reduce.15.cloned.1.call-start = ((), (), s32[]{:S(2)}) async-start(), calls=%async_computation.29 | async-start | bytes 6291456 | tf_op jit(solution)/shard_map/psum | solution.py:277
  681.1 8.2 copy-start.3
  681.1 8.2 copy-start.13
  681.1 8.2 copy-start.16
  716.8 35.3 %copy-start.15 = (bf16[1536,384]{1,0:T(8,128)(2,1)S(1)}, bf16[1536,384]{1,0:T(8,128)(2,1)}, u32[]{:S(2)}) copy-start(bf16[1536,384]{1,0:T(8,128)(2,1)} %all-gather.10.cloned.1.call-done) | copy-start | bytes 3538948
  756.3 156.3 %reduce-scatter.18.cloned.1.call-start = ((), (), s32[]{:S(2)}) async-start(), calls=%async_computation.23 | async-start | bytes 2506752 | tf_op jit(solution)/shard_map/reduce_scatter | solution.py:340
  759.6 215.7 %reduce-scatter.20.cloned.1.call-start = ((), (), s32[]{:S(2)}) async-start(), calls=%async_computation.24 | async-start | bytes 2506752 | tf_op jit(solution)/shard_map/reduce_scatter | solution.py:341
  763.0 291.7 %reduce-scatter.22.cloned.1.call-start = ((), (), s32[]{:S(2)}) async-start(), calls=%async_computation.25 | async-start | bytes 5013504 | tf_op jit(solution)/shard_map/reduce_scatter | solution.py:342
  769.8 363.8 %reduce-scatter.16.cloned.1.call-start = ((), (), s32[]{:S(2)}) async-start(), calls=%async_computation.22 | async-start | bytes 5013504 | tf_op jit(solution)/shard_map/reduce_scatter | solution.py:339
  775.4 497.1 %reduce-scatter.24.cloned.1.call-start = ((), (), s32[]{:S(2)}) async-start(), calls=%async_computation.26 | async-start | bytes 13369344 | tf_op jit(solution)/shard_map/reduce_scatter | solution.py:344
  785.5 625.7 %reduce-scatter.26.cloned.1.call-start = ((), (), s32[]{:S(2)}) async-start(), calls=%async_computation.27 | async-start | bytes 13369344 | tf_op jit(solution)/shard_map/reduce_scatter | solution.py:345
  795.7 754.6 %reduce-scatter.28.cloned.1.call-start = ((), (), s32[]{:S(2)}) async-start(), calls=%async_computation.28 | async-start | bytes 13369344
  819.6 24.2 %copy-start.26 = (f32[1536]{0:T(1024)S(1)}, f32[1536]{0:T(1024)}, u32[]{:S(2)}) copy-start(f32[1536]{0:T(1024)} %get-tuple-element.510) | copy-start | bytes 18436
  819.6 87.3 %copy-start.28 = (f32[512]{0:T(512)S(1)}, f32[512]{0:T(512)}, u32[]{:S(2)}) copy-start(f32[512]{0:T(512)} %copy-done.27) | copy-start | bytes 6148
  819.6 87.3 %copy-start.33 = (f32[512]{0:T(512)S(1)}, f32[512]{0:T(512)}, u32[]{:S(2)}) copy-start(f32[512]{0:T(512)} %copy-done.32) | copy-start | bytes 6148
  (32 other events, 90.8 us)
Sparse Core Ops, SparseCore 0:
  10.3 41.2 all-gather.13
  53.9 37.3 all-gather.9
  93.6 41.1 all-gather.17
  136.9 35.8 all-gather.15
  174.8 35.9 all-gather.11
  212.9 41.1 all-gather.19
  260.7 50.4 all-reduce.10
  313.7 61.8 all-gather.21
  378.2 60.4 all-gather.23
  441.1 60.4 all-gather.25
  525.5 50.0 all-reduce.12
  680.2 35.2 reduce-scatter.11
  717.8 34.2 reduce-scatter.13
  756.4 84.9 all-reduce.14
  846.0 62.9 reduce-scatter.17
  913.3 61.9 reduce-scatter.19
  980.0 74.6 reduce-scatter.21
  1059.0 74.5 reduce-scatter.15
  1138.8 133.6 reduce-scatter.23
  1277.5 133.7 reduce-scatter.25
  1416.4 133.7 reduce-scatter.27
where the time goes:
time: 1560 us
  waiting for transfers between devices  1090 us (70%)
  matrix products  233 us (15%)
  blocking collectives  98.3 us (6%)
  local copies, waits for them, and re-layouts  70.7 us (5%)
  other arithmetic  47.8 us (3%)
  between operations  16.3 us (1%)
    unnamed x22, waiting for transfers between devices  144 us
    reduce_scatter x1, waiting for transfers between devices, body(): lax.psum_scatter(gate_gradient, ('dp', 'ctx'), scatter_dimension=0, tiled...  139 us
    reduce_scatter x1, waiting for transfers between devices, body(): lax.psum_scatter(up_gradient, ('dp', 'ctx'), scatter_dimension=0, tiled=T...  139 us
    unnamed x2, blocking collectives  98.3 us
    reduce_scatter x1, waiting for transfers between devices, body(): lax.psum_scatter(output_gradient, ('dp', 'ctx'), scatter_dimension=0, til...  79.4 us
    reduce_scatter x1, waiting for transfers between devices, body(): lax.psum_scatter(query_gradient, ('dp', 'ctx'), scatter_dimension=0, tile...  78.9 us
    reduce_scatter x1, waiting for transfers between devices, body(): lax.psum_scatter(value_gradient, ('dp', 'ctx'), scatter_dimension=0, tile...  62.6 us
    all_gather x1, waiting for transfers between devices, body(): lax.all_gather(gate_weight, ('dp', 'ctx'), axis=0, tiled=True)  60.5 us
  transfers between devices with their start and end apart: 21, of which 17 were waited for; matrix products, arithmetic and copies ran while one was open for 14% of the time, Pallas kernels for 0%

commit v1 on v0

v1 whole, which is shorter than its diff:
```python
import functools
import math

import jax
import jax.numpy as jnp
from jax import lax
from jax.experimental import pallas as pl
from jax.experimental.pallas import tpu as pltpu
from jax.sharding import PartitionSpec as P

HEAD_SIZE = 96
HALF = HEAD_SIZE // 2
BLOCK = 64
SPAN = 256
TILE = 512
LANES = 128

epsilon = 1e-05
rotary_base = 100000.0
masked_score = -1e30
SCALE = HEAD_SIZE**-0.5
SCALE2 = SCALE / math.log(2.0)

f32 = jnp.float32
bf16 = jnp.bfloat16
ROWS = ("dp", "ctx")
MIB = 2**20


def dot(left, right, contract):
    return lax.dot_general(
        left, right, ((contract[:1], contract[1:]), ((), ())), preferred_element_type=f32
    )


NN, NT, TN = (1, 0), (1, 1), (0, 0)


def cost(flops, moved):
    return pl.CostEstimate(flops=int(flops), bytes_accessed=int(moved), transcendentals=0)


def params(mib):
    return pltpu.CompilerParams(vmem_limit_bytes=mib * MIB)


def whole(shape):
    return pl.BlockSpec(shape, lambda *_: (0,) * len(shape))


SCALARS = pl.BlockSpec(memory_space=pltpu.SMEM)


def angles(place):
    frequency = rotary_base ** (-(jnp.arange(HALF, dtype=f32) * 2.0 / HEAD_SIZE))
    turn = place.astype(f32)[:, None] * frequency[None, :]
    return (jnp.cos(turn), jnp.sin(turn))


def own_places(starts, order, ctx, count):
    rounds = order.shape[0]
    within = jnp.arange(rounds * BLOCK, dtype=jnp.int32)
    owner = jnp.repeat(lax.dynamic_index_in_dim(order, ctx, 1, keepdims=False), BLOCK)
    stream = (owner + (within // BLOCK) * count) * BLOCK + within % BLOCK
    first = jnp.max(jnp.where(starts[None, :] <= stream[:, None], starts[None, :], 0), axis=1)
    return stream - first


def turned(head, cosine, sine, sign):
    first, second = head[:, :HALF], head[:, HALF:]
    along = sine if sign > 0 else -sine
    return jnp.concatenate(
        [first * cosine - second * along, second * cosine + first * along], axis=1
    )


def project_kernel(x_ref, gain_ref, cos_ref, sin_ref, w_ref, q_ref, kv_ref, normed_ref):
    step = pl.program_id(0)
    tile = w_ref.shape[1]

    @pl.when(step == 0)
    def _():
        x = x_ref[...].astype(f32)
        scale = lax.rsqrt(jnp.mean(x * x, axis=1, keepdims=True) + epsilon)
        normed_ref[...] = (x * scale * gain_ref[0:1, :]).astype(bf16)

    out = dot(normed_ref[...], w_ref[...], NN)

    def rotated(ref):
        for h in range(tile // HEAD_SIZE):
            lanes = slice(h * HEAD_SIZE, (h + 1) * HEAD_SIZE)
            ref[:, lanes] = turned(out[:, lanes], cos_ref[...], sin_ref[...], 1).astype(bf16)

    @pl.when(step < 2)
    def _():
        rotated(q_ref)

    @pl.when(step == 2)
    def _():
        rotated(kv_ref)

    @pl.when(step == 3)
    def _():
        kv_ref[...] = out.astype(bf16)


def project(x, gains, cosine, sine, weights, q_cols):
    rows, width = x.shape
    tile = q_cols // 2
    return pl.pallas_call(
        project_kernel,
        grid=(4,),
        in_specs=[
            whole(x.shape),
            whole(gains.shape),
            whole(cosine.shape),
            whole(sine.shape),
            pl.BlockSpec((width, tile), lambda j: (0, j)),
        ],
        out_specs=[
            pl.BlockSpec((rows, tile), lambda j: (0, jnp.minimum(j, 1))),
            pl.BlockSpec((rows, tile), lambda j: (0, jnp.maximum(j - 2, 0))),
            whole((rows, width)),
        ],
        out_shape=[
            jax.ShapeDtypeStruct((rows, q_cols), bf16),
            jax.ShapeDtypeStruct((rows, q_cols), bf16),
            jax.ShapeDtypeStruct((rows, width), bf16),
        ],
        compiler_params=params(40),
        cost_estimate=cost(2 * rows * width * 4 * tile, 2 * width * 4 * tile),
        name="project",
    )(x, gains, cosine, sine, weights)


def gather_stream(order, ctx, pieces, k_ref, v_ref):
    count, groups = len(pieces), k_ref.shape[0]
    width = groups * HEAD_SIZE

    def fill(i, unused):
        source = pl.ds(pl.multiple_of(i * BLOCK, BLOCK), BLOCK)
        for k, piece in enumerate(pieces):
            block = i * count + order[i, lax.rem(ctx - k + count, count)]
            target = pl.ds(pl.multiple_of(block * BLOCK, BLOCK), BLOCK)
            for g in range(groups):
                lanes = slice(g * HEAD_SIZE, (g + 1) * HEAD_SIZE)
                k_ref[g, target, :] = piece[source, lanes]
                v_ref[g, target, :] = piece[
                    source, width + g * HEAD_SIZE : width + (g + 1) * HEAD_SIZE
                ]
        return unused

    lax.fori_loop(0, order.shape[0], fill, 0)


def reach(starts, first):
    low = jnp.int32(0)
    for j in range(starts.shape[0]):
        low = jnp.where(starts[j] <= first, starts[j], low)
    return low


def row_limits(starts, first, lanes):
    row = first + lax.rem(lax.broadcasted_iota(jnp.int32, (1, lanes), 1), BLOCK)
    low = jnp.zeros((1, lanes), jnp.int32)
    for j in range(starts.shape[0]):
        low = jnp.where(row >= starts[j], starts[j], low)
    return row, low


def stacked(ref, rows, group, ratio):
    return jnp.concatenate(
        [
            ref[rows, (group * ratio + h) * HEAD_SIZE : (group * ratio + h + 1) * HEAD_SIZE]
            for h in range(ratio)
        ],
        axis=0,
    )


def attend_kernel(count, order, starts, place, q_ref, *refs):
    pieces = refs[:count]
    low_ref, att_ref, sum_ref, k_ref, v_ref = refs[count:]
    groups = k_ref.shape[0]
    ratio = q_ref.shape[1] // (groups * HEAD_SIZE)
    lanes = ratio * BLOCK
    ctx = place[0]
    gather_stream(order, ctx, pieces, k_ref, v_ref)

    def one(i, unused):
        first = (i * count + order[i, ctx]) * BLOCK
        row, low = row_limits(starts, first, lanes)
        begin = reach(starts, first) // SPAN
        end = (first + BLOCK - 1) // SPAN + 1
        rows = pl.ds(pl.multiple_of(i * BLOCK, BLOCK), BLOCK)
        queries = [stacked(q_ref, rows, g, ratio) for g in range(groups)]

        def chunk(c, carry):
            keys = pl.ds(pl.multiple_of(c * SPAN, SPAN), SPAN)
            index = c * SPAN + lax.broadcasted_iota(jnp.int32, (SPAN, lanes), 0)
            allowed = (index <= row) & (index >= low)
            new = []
            for g in range(groups):
                top, total, out = carry[g]
                raw = dot(k_ref[g, keys, :], queries[g], NT) * SCALE2
                raw = jnp.where(allowed, raw, masked_score)
                new_top = jnp.maximum(top, jnp.max(raw, axis=0, keepdims=True))
                weights = jnp.where(allowed, jnp.exp2(raw - new_top), 0.0)
                back = jnp.exp2(top - new_top)
                total = total * back + jnp.sum(weights, axis=0, keepdims=True)
                out = out * back + dot(v_ref[g, keys, :], weights.astype(bf16), TN)
                new.append((new_top, total, out))
            return tuple(new)

        blank = (
            jnp.full((1, lanes), masked_score, f32),
            jnp.zeros((1, lanes), f32),
            jnp.zeros((HEAD_SIZE, lanes), f32),
        )
        result = lax.fori_loop(begin, end, chunk, (blank,) * groups)
        for g in range(groups):
            top, total, out = result[g]
            out = out / total
            att_ref[i * groups + g] = out
            sum_ref[pl.ds(i * groups + g, 1), :] = top + jnp.log2(total)
            flat = out.T.astype(bf16)
            for h in range(ratio):
                head = g * ratio + h
                low_ref[rows, head * HEAD_SIZE : (head + 1) * HEAD_SIZE] = flat[
                    h * BLOCK : (h + 1) * BLOCK
                ]
        return unused

    lax.fori_loop(0, order.shape[0], one, 0)


def attend(order, starts, place, queries, pieces):
    count, rows = len(pieces), queries.shape[0]
    groups = pieces[0].shape[1] // (2 * HEAD_SIZE)
    ratio = queries.shape[1] // (groups * HEAD_SIZE)
    rounds, lanes = order.shape[0], ratio * BLOCK
    return pl.pallas_call(
        functools.partial(attend_kernel, count),
        in_specs=[SCALARS] * 3 + [pl.BlockSpec(memory_space=pltpu.VMEM)] * (1 + count),
        out_specs=[pl.BlockSpec(memory_space=pltpu.VMEM)] * 3,
        out_shape=[
            jax.ShapeDtypeStruct(queries.shape, bf16),
            jax.ShapeDtypeStruct((rounds * groups, HEAD_SIZE, lanes), f32),
            jax.ShapeDtypeStruct((rounds * groups, lanes), f32),
        ],
        scratch_shapes=[pltpu.VMEM((groups, count * rows, HEAD_SIZE), bf16)] * 2,
        compiler_params=params(40),
        cost_estimate=cost(8e9, 1e7),
        name="attend",
    )(order, starts, place, queries, *pieces)


def attend_back_kernel(count, order, starts, place, q_ref, d_ref, att_ref, sum_ref, cos_ref, sin_ref, *refs):
    pieces = refs[:count]
    qc_ref = refs[count]
    outs = refs[count + 1 : 2 * count + 1]
    k_ref, v_ref, dk_ref, dv_ref = refs[2 * count + 1 :]
    groups = k_ref.shape[0]
    ratio = q_ref.shape[1] // (groups * HEAD_SIZE)
    lanes = ratio * BLOCK
    width = groups * HEAD_SIZE
    ctx = place[0]
    gather_stream(order, ctx, pieces, k_ref, v_ref)
    dk_ref[...] = jnp.zeros_like(dk_ref)
    dv_ref[...] = jnp.zeros_like(dv_ref)

    def one(i, unused):
        first = (i * count + order[i, ctx]) * BLOCK
        row, low = row_limits(starts, first, lanes)
        begin = reach(starts, first) // SPAN
        end = (first + BLOCK - 1) // SPAN + 1
        rows = pl.ds(pl.multiple_of(i * BLOCK, BLOCK), BLOCK)
        queries = [stacked(q_ref, rows, g, ratio) for g in range(groups)]
        slopes = [stacked(d_ref, rows, g, ratio) for g in range(groups)]
        sums, deltas = [], []
        for g in range(groups):
            sums.append(sum_ref[pl.ds(i * groups + g, 1), :])
            across = slopes[g].astype(f32).T
            deltas.append(jnp.sum(across * att_ref[i * groups + g], axis=0, keepdims=True))

        def chunk(c, carry):
            keys = pl.ds(pl.multiple_of(c * SPAN, SPAN), SPAN)
            index = c * SPAN + lax.broadcasted_iota(jnp.int32, (SPAN, lanes), 0)
            allowed = (index <= row) & (index >= low)
            new = []
            for g in range(groups):
                key, value = k_ref[g, keys, :], v_ref[g, keys, :]
                raw = dot(key, queries[g], NT) * SCALE2
                share = jnp.where(allowed, jnp.exp2(jnp.minimum(raw - sums[g], 0.0)), 0.0)
                back_share = dot(value, slopes[g], NT)
                back = (share * (back_share - deltas[g])).astype(bf16)
                dv_ref[g, keys, :] += dot(share.astype(bf16), slopes[g], NN)
                dk_ref[g, keys, :] += dot(back, queries[g], NN)
                new.append(carry[g] + dot(key, back, TN))
            return tuple(new)

        blank = jnp.zeros((HEAD_SIZE, lanes), f32)
        result = lax.fori_loop(begin, end, chunk, (blank,) * groups)
        cosine, sine = cos_ref[rows, :], sin_ref[rows, :]
        for g in range(groups):
            flat = result[g].T * SCALE
            for h in range(ratio):
                head = g * ratio + h
                qc_ref[rows, head * HEAD_SIZE : (head + 1) * HEAD_SIZE] = turned(
                    flat[h * BLOCK : (h + 1) * BLOCK], cosine, sine, -1
                ).astype(bf16)
        return unused

    lax.fori_loop(0, order.shape[0], one, 0)

    def spread(i, unused):
        target = pl.ds(pl.multiple_of(i * BLOCK, BLOCK), BLOCK)
        for k, out in enumerate(outs):
            block = i * count + order[i, lax.rem(ctx - k + count, count)]
            source = pl.ds(pl.multiple_of(block * BLOCK, BLOCK), BLOCK)
            for g in range(groups):
                out[target, g * HEAD_SIZE : (g + 1) * HEAD_SIZE] = (
                    dk_ref[g, source, :] * SCALE
                ).astype(bf16)
                out[target, width + g * HEAD_SIZE : width + (g + 1) * HEAD_SIZE] = dv_ref[
                    g, source, :
                ].astype(bf16)
        return unused

    lax.fori_loop(0, order.shape[0], spread, 0)


def attend_back(order, starts, place, queries, slopes, att, sums, cosine, sine, pieces):
    count, rows = len(pieces), queries.shape[0]
    groups = pieces[0].shape[1] // (2 * HEAD_SIZE)
    keys = (groups, count * rows, HEAD_SIZE)
    return pl.pallas_call(
        functools.partial(attend_back_kernel, count),
        in_specs=[SCALARS] * 3 + [pl.BlockSpec(memory_space=pltpu.VMEM)] * (6 + count),
        out_specs=[pl.BlockSpec(memory_space=pltpu.VMEM)] * (1 + count),
        out_shape=[jax.ShapeDtypeStruct(queries.shape, bf16)]
        + [jax.ShapeDtypeStruct(pieces[0].shape, bf16)] * count,
        scratch_shapes=[pltpu.VMEM(keys, bf16)] * 2 + [pltpu.VMEM(keys, f32)] * 2,
        compiler_params=params(56),
        cost_estimate=cost(16e9, 2e7),
        name="attend_back",
    )(order, starts, place, queries, slopes, att, sums, cosine, sine, *pieces)


def output_kernel(a_ref, w_ref, o_ref):
    o_ref[...] = dot(a_ref[...], w_ref[...], NT).astype(bf16)


def output_product(attended, weights, column, features):
    rows, inner = attended.shape
    return pl.pallas_call(
        output_kernel,
        grid=(2,),
        in_specs=[
            whole(attended.shape),
            pl.BlockSpec((features // 2, inner), lambda j: (j, column)),
        ],
        out_specs=pl.BlockSpec((rows, features // 2), lambda j: (0, j)),
        out_shape=jax.ShapeDtypeStruct((rows, features), bf16),
        compiler_params=params(40),
        cost_estimate=cost(2 * rows * inner * features, 2 * inner * features),
        name="output_product",
    )(attended, weights)


def feed_kernel(
    x_ref, mine_ref, other_ref, gain_ref, cot_ref, gate_ref, up_ref, down_ref,
    middle_ref, normed_ref, mixed_ref, bg_ref, bu_ref, back_ref, total_ref,
):
    step = pl.program_id(0)

    @pl.when(step == 0)
    def _():
        middle = (
            x_ref[...].astype(f32) + mine_ref[...].astype(f32) + other_ref[...].astype(f32)
        )
        middle_ref[...] = middle
        scale = lax.rsqrt(jnp.mean(middle * middle, axis=1, keepdims=True) + epsilon)
        normed_ref[...] = (middle * scale * gain_ref[1:2, :]).astype(bf16)

    gate = dot(normed_ref[...], gate_ref[...], NN)
    upward = dot(normed_ref[...], up_ref[...], NN)
    back_mixed = dot(cot_ref[...], down_ref[...], NN)
    sigmoid = 1.0 / (1.0 + jnp.exp(-gate))
    activated = gate * sigmoid
    mixed_ref[...] = (activated * upward).astype(bf16)
    back_gate = (back_mixed * upward * sigmoid * (1.0 + gate * (1.0 - sigmoid))).astype(bf16)
    back_up = (back_mixed * activated).astype(bf16)
    bg_ref[...] = back_gate
    bu_ref[...] = back_up
    part = dot(back_gate, gate_ref[...], NT) + dot(back_up, up_ref[...], NT)

    @pl.when(step == 0)
    def _():
        total_ref[...] = part

    @pl.when(step > 0)
    def _():
        total_ref[...] += part

    @pl.when(step == pl.num_programs(0) - 1)
    def _():
        back_ref[...] = total_ref[...].astype(bf16)


def feed_forward(x, mine, other, gains, cotangent, weights, hidden):
    rows, width = x.shape
    steps = hidden // TILE
    tile_of = lambda which: pl.BlockSpec((width, TILE), lambda j: (0, which * steps + j))
    rows_of = pl.BlockSpec((rows, TILE), lambda j: (0, j))
    full = whole((rows, width))
    return pl.pallas_call(
        feed_kernel,
        grid=(steps,),
        in_specs=[full, full, full, whole(gains.shape), full]
        + [tile_of(0), tile_of(1), tile_of(2)],
        out_specs=[full, full, rows_of, rows_of, rows_of, full],
        out_shape=[
            jax.ShapeDtypeStruct((rows, width), f32),
            jax.ShapeDtypeStruct((rows, width), bf16),
            jax.ShapeDtypeStruct((rows, hidden), bf16),
            jax.ShapeDtypeStruct((rows, hidden), bf16),
            jax.ShapeDtypeStruct((rows, hidden), bf16),
            jax.ShapeDtypeStruct((rows, width), bf16),
        ],
        scratch_shapes=[pltpu.VMEM((rows, width), f32)],
        compiler_params=params(56),
        cost_estimate=cost(10 * rows * width * hidden, 6 * width * hidden),
        name="feed_forward",
    )(x, mine, other, gains, cotangent, weights, weights, weights)


def down_kernel(mixed_ref, w_ref, o_ref):
    o_ref[...] = dot(mixed_ref[...], w_ref[...], NT).astype(bf16)


def down_product(mixed, weights, column):
    rows, hidden = mixed.shape
    width = weights.shape[0]
    return pl.pallas_call(
        down_kernel,
        grid=(3,),
        in_specs=[
            whole(mixed.shape),
            pl.BlockSpec((width // 3, hidden), lambda j: (j, column)),
        ],
        out_specs=pl.BlockSpec((rows, width // 3), lambda j: (0, j)),
        out_shape=jax.ShapeDtypeStruct((rows, width), bf16),
        compiler_params=params(40),
        cost_estimate=cost(2 * rows * width * hidden, 2 * width * hidden),
        name="down_product",
    )(mixed, weights)


def middle_kernel(cot_ref, mine_ref, other_ref, middle_ref, gain_ref, w_ref, bm_ref, bb_ref, ba_ref, grad_ref):
    middle = middle_ref[...]
    scale = lax.rsqrt(jnp.mean(middle * middle, axis=1, keepdims=True) + epsilon)
    unit = middle * scale
    back = mine_ref[...].astype(f32) + other_ref[...].astype(f32)
    grad_ref[...] = jnp.sum(back * unit, axis=0, keepdims=True)
    inner = back * gain_ref[1:2, :]
    out = cot_ref[...].astype(f32) + scale * (
        inner - unit * jnp.mean(inner * unit, axis=1, keepdims=True)
    )
    bm_ref[...] = out
    low = out.astype(bf16)
    bb_ref[...] = low
    ba_ref[...] = dot(low, w_ref[...], NN).astype(bf16)


def middle_back(cotangent, mine, other, middle, gains, weights, column, inner):
    rows, width = middle.shape
    full = whole((rows, width))
    return pl.pallas_call(
        middle_kernel,
        grid=(1,),
        in_specs=[full, full, full, full, whole(gains.shape)]
        + [pl.BlockSpec((width, inner), lambda j: (0, column))],
        out_specs=[full, full, whole((rows, inner)), whole((1, width))],
        out_shape=[
            jax.ShapeDtypeStruct((rows, width), f32),
            jax.ShapeDtypeStruct((rows, width), bf16),
            jax.ShapeDtypeStruct((rows, inner), bf16),
            jax.ShapeDtypeStruct((1, width), f32),
        ],
        compiler_params=params(56),
        cost_estimate=cost(2 * rows * width * inner, 1.5e7),
        name="middle_back",
    )(cotangent, mine, other, middle, gains, weights)


def inputs_kernel(count, x_ref, qc_ref, cos_ref, sin_ref, w_ref, *refs):
    parts = refs[:count]
    cot_ref, back_ref, grad_ref = refs[count:]
    half = qc_ref.shape[1] // 2
    cot_ref[:, : 2 * half] = qc_ref[...]
    total = parts[0][...].astype(f32)
    for part in parts[1:]:
        total += part[...].astype(f32)
    for h in range(half // HEAD_SIZE):
        lanes = slice(h * HEAD_SIZE, (h + 1) * HEAD_SIZE)
        there = slice(2 * half + h * HEAD_SIZE, 2 * half + (h + 1) * HEAD_SIZE)
        cot_ref[:, there] = turned(total[:, lanes], cos_ref[...], sin_ref[...], -1).astype(bf16)
    cot_ref[:, 3 * half :] = total[:, half:].astype(bf16)
    back = dot(cot_ref[...], w_ref[...], NT)
    back_ref[...] = back.astype(bf16)
    x = x_ref[...].astype(f32)
    unit = x * lax.rsqrt(jnp.mean(x * x, axis=1, keepdims=True) + epsilon)
    grad_ref[...] = jnp.sum(back * unit, axis=0, keepdims=True)


def inputs_back(x, qc, cosine, sine, weights, parts):
    rows, width = x.shape
    inner = 2 * qc.shape[1]
    full = whole((rows, width))
    return pl.pallas_call(
        functools.partial(inputs_kernel, len(parts)),
        grid=(1,),
        in_specs=[full, whole(qc.shape), whole(cosine.shape), whole(sine.shape)]
        + [pl.BlockSpec((width, inner), lambda j: (0, 0))]
        + [whole(parts[0].shape)] * len(parts),
        out_specs=[whole((rows, inner)), full, whole((1, width))],
        out_shape=[
            jax.ShapeDtypeStruct((rows, inner), bf16),
            jax.ShapeDtypeStruct((rows, width), bf16),
            jax.ShapeDtypeStruct((1, width), f32),
        ],
        compiler_params=params(56),
        cost_estimate=cost(2 * rows * width * inner, 1.5e7),
        name="inputs_back",
    )(x, qc, cosine, sine, weights, *parts)


def final_kernel(bm_ref, mine_ref, other_ref, x_ref, gain_ref, o_ref):
    x = x_ref[...].astype(f32)
    scale = lax.rsqrt(jnp.mean(x * x, axis=1, keepdims=True) + epsilon)
    unit = x * scale
    inner = (mine_ref[...].astype(f32) + other_ref[...].astype(f32)) * gain_ref[0:1, :]
    out = bm_ref[...] + scale * (inner - unit * jnp.mean(inner * unit, axis=1, keepdims=True))
    o_ref[...] = out.astype(bf16)


def final_back(back_middle, mine, other, x, gains):
    rows, width = x.shape
    block = pl.BlockSpec((rows // 4, width), lambda j: (j, 0))
    return pl.pallas_call(
        final_kernel,
        grid=(4,),
        in_specs=[block] * 4 + [whole(gains.shape)],
        out_specs=block,
        out_shape=jax.ShapeDtypeStruct((rows, width), bf16),
        compiler_params=params(40),
        cost_estimate=cost(1e6, 1e7),
        name="final_back",
    )(back_middle, mine, other, x, gains)


def relative(field, pairs, ctxs):
    dp, ctx = lax.axis_index("dp"), lax.axis_index("ctx")
    shaped = field.reshape((pairs, 2, ctxs, -1) + field.shape[1:])
    for axis, shift in ((0, dp // 2 + 1), (1, dp % 2 + 1), (2, ctx + 1)):
        shaped = jnp.roll(shaped, -shift, axis)
    return shaped.swapaxes(0, 1).reshape(field.shape)


def gradient_kernel(pairs, ctxs, place, a_ref, b_ref, send_ref, keep_ref):
    width = a_ref.shape[1]
    section = width // (2 * pairs)
    piece = section // ctxs
    for c, out in ((1, send_ref), (0, keep_ref)):
        for y in range(pairs):
            pair = lax.rem(place[0] + y + 1, pairs)
            core = lax.rem(place[1] + c, 2)
            lanes = pl.ds(pl.multiple_of((pair * 2 + core) * section, LANES), section)
            result = dot(a_ref[:, lanes], b_ref[...], TN).astype(bf16)
            for z in range(ctxs):
                far = lax.rem(z + ctxs - place[2] - 1 + ctxs, ctxs)
                rows = pl.ds(pl.multiple_of(y * section + far * piece, piece), piece)
                out[rows, :] = result[z * piece : (z + 1) * piece]


def gradient(a, b, pairs, ctxs):
    rows, width = a.shape
    columns = b.shape[1]
    section = width // (2 * pairs)
    if section % LANES or (section // ctxs) % 32:
        ordered = relative(dot(a, b, TN).astype(bf16), pairs, ctxs)
        return ordered[: width // 2], ordered[width // 2 :]
    dp, ctx = lax.axis_index("dp"), lax.axis_index("ctx")
    place = jnp.stack([dp // 2, dp % 2, ctx]).astype(jnp.int32)
    tile = TILE if columns % TILE == 0 else columns // 2
    block = pl.BlockSpec((width // 2, tile), lambda j: (0, j))
    return pl.pallas_call(
        functools.partial(gradient_kernel, pairs, ctxs),
        grid=(columns // tile,),
        in_specs=[SCALARS, whole(a.shape), pl.BlockSpec((rows, tile), lambda j: (0, j))],
        out_specs=[block, block],
        out_shape=[jax.ShapeDtypeStruct((width // 2, columns), bf16)] * 2,
        compiler_params=params(40),
        cost_estimate=cost(2 * rows * width * columns, 2 * width * columns),
        name="gradient",
    )(place, a, b)


def shifted(field, axis, steps, stride=1):
    count = lax.axis_size(axis)
    return lax.ppermute(
        field, axis, [(i, (i + steps * stride) % count) for i in range(count)]
    )


def other_core(field):
    return lax.ppermute(field, "dp", [(i, i ^ 1) for i in range(lax.axis_size("dp"))])


def sum_to_owner(send, keep, pairs, ctxs):
    columns = send.shape[1]
    got = other_core(send).reshape(pairs, -1, columns)
    keep = keep.reshape(pairs, -1, columns)
    total = got[-1].astype(f32) + keep[-1].astype(f32)
    for y in range(1, pairs):
        part = (got[y - 1].astype(f32) + keep[y - 1].astype(f32)).astype(bf16)
        total = total + shifted(part, "dp", y, 2).astype(f32)
    total = total.reshape(ctxs, -1, columns)
    result = total[-1]
    for z in range(1, ctxs):
        result = result + shifted(total[z - 1].astype(bf16), "ctx", z).astype(f32)
    return result


def swapped(field):
    count = lax.axis_size("tp")
    return lax.ppermute(field, "tp", [(i, count - 1 - i) for i in range(count)])


def body(
    tokens,
    cotangent,
    lengths,
    block_order,
    pre_gain,
    query_weight,
    key_weight,
    value_weight,
    output_weight,
    mid_gain,
    gate_weight,
    up_weight,
    down_weight,
):
    ctxs = lax.axis_size("ctx")
    pairs = lax.axis_size("dp") // 2
    ctx = lax.axis_index("ctx")
    order = block_order[0]
    ends = jnp.cumsum(lengths[0]).astype(jnp.int32)
    starts = ends - lengths[0]
    place = jnp.stack([ctx]).astype(jnp.int32)
    q_cols = query_weight.shape[1]
    features = tokens.shape[1]
    hidden = gate_weight.shape[1]

    gain_columns = jnp.pad(jnp.stack([pre_gain, mid_gain], axis=1), ((0, 0), (0, LANES - 2)))
    first = lax.all_gather(
        jnp.concatenate([query_weight, key_weight, value_weight, gain_columns], axis=1),
        ROWS, axis=0, tiled=True,
    )
    second = lax.all_gather(
        jnp.concatenate([gate_weight, up_weight, down_weight, output_weight], axis=1),
        ROWS, axis=0, tiled=True,
    )
    output_column = 3 * hidden // q_cols
    gains = first[:, 2 * q_cols : 2 * q_cols + 8].T.astype(f32)

    cosine, sine = angles(own_places(starts, order, ctx, ctxs))
    queries, kv, normed = project(tokens, gains, cosine, sine, first, q_cols)
    pieces = [kv] + [shifted(kv, "ctx", k) for k in range(1, ctxs)]
    attended_low, att, sums = attend(order, starts, place, queries, pieces)
    branch = output_product(attended_low, second, output_column, features)
    middle, mid_normed, mixed, back_gate, back_up, back_part = feed_forward(
        tokens, branch, swapped(branch), gains, cotangent, second, hidden
    )
    back_other = swapped(back_part)
    gate_parts = gradient(mid_normed, back_gate, pairs, ctxs)
    up_parts = gradient(mid_normed, back_up, pairs, ctxs)
    down_parts = gradient(cotangent, mixed, pairs, ctxs)
    feed = down_product(mixed, second, 2)
    result = (middle + feed.astype(f32) + swapped(feed).astype(f32)).astype(bf16)

    back_middle, back_branch, back_attended, mid_grad = middle_back(
        cotangent, back_part, back_other, middle, gains, second, output_column, q_cols
    )
    output_parts = gradient(back_branch, attended_low, pairs, ctxs)
    back = attend_back(
        order, starts, place, queries, back_attended, att, sums, cosine, sine, pieces
    )
    own_parts = [back[1]] + [shifted(back[1 + k], "ctx", -k) for k in range(1, ctxs)]
    cot, normed_part, pre_grad = inputs_back(tokens, back[0], cosine, sine, first, own_parts)
    normed_other = swapped(normed_part)
    qkv_parts = gradient(normed, cot, pairs, ctxs)
    token_gradient = final_back(back_middle, normed_part, normed_other, tokens, gains)

    tp = lax.axis_index("tp")
    mid_once = jnp.where(tp == 0, mid_grad, 0.0)
    pair = jnp.concatenate([pre_grad, mid_once], axis=0).astype(bf16)
    pair = jnp.pad(pair, ((0, 6), (0, 0))).T
    ordered = relative(pair, pairs, ctxs)
    gain_sums = sum_to_owner(ordered[: features // 2], ordered[features // 2 :], pairs, ctxs)
    gain_sums = gain_sums + swapped(gain_sums)

    gate_gradient = sum_to_owner(*gate_parts, pairs, ctxs)
    up_gradient = sum_to_owner(*up_parts, pairs, ctxs)
    down_gradient = sum_to_owner(*down_parts, pairs, ctxs)
    output_gradient = sum_to_owner(*output_parts, pairs, ctxs)
    qkv_gradient = sum_to_owner(*qkv_parts, pairs, ctxs)
    return (
        result,
        token_gradient,
        gain_sums[:, 0],
        qkv_gradient[:, :q_cols],
        qkv_gradient[:, q_cols : q_cols + q_cols // 2],
        qkv_gradient[:, q_cols + q_cols // 2 :],
        output_gradient,
        gain_sums[:, 1],
        gate_gradient,
        up_gradient,
        down_gradient,
    )


def solution(mesh):
    rows, split = P(ROWS, None), P(ROWS, "tp")
    return jax.shard_map(
        body,
        mesh=mesh,
        in_specs=(rows, rows, P("dp", None), P("dp", None, None), P(ROWS))
        + (split,) * 4
        + (P(ROWS),)
        + (split,) * 3,
        out_specs=(rows, rows, P(ROWS)) + (split,) * 4 + (P(ROWS),) + (split,) * 3,
        check_vma=False,
    )
```

time: 1560 us -> 740 us (0.47)
  waiting for transfers between devices: 1090 us -> 427 us
  matrix products: 233 us -> 0 us
  Pallas kernels: 0 us -> 152 us
  blocking collectives: 98.3 us -> 0 us
  starting transfers between devices: 2.45 us -> 74.2 us
  local copies, waits for them, and re-layouts: 70.7 us -> 28 us
    reduce_scatter x8 -> x0, waiting for transfers between devices: 550 us -> none  [the longest x1 139 us: body(): lax.psum_scatter(gate_gradient, ('dp', 'ctx'), scatter_dimension=0, tiled...]
    ppermute x0 -> x41, waiting for transfers between devices: none -> 308 us  [the longest x30 249 us: shifted(): lax.ppermute(field, axis, [(i, (i + steps * stride) % count) for i in ran...]
    dot_general x49 -> x0, matrix products: 233 us -> none  [the longest x7 48.5 us: over_rows(): lax.dot_general(left, right, (((0,), (0,)), ((), ())), preferred_element_...]
    all_gather x9 -> x2, waiting for transfers between devices: 275 us -> 120 us  [the longest x1 64.4 us: body(): lax.all_gather(jnp.concatenate([gate_weight, up_weight, down_weight, outp...]
    pallas_call x0 -> x14, Pallas kernels: none -> 152 us  [the longest x1 37 us: attend_back(): pl.pallas_call(functools.partial(attend_back_kernel, count), in_specs=[SC...]
    unnamed x22 -> x2, waiting for transfers between devices: 144 us -> 0.03 us
    psum x3 -> x0, waiting for transfers between devices: 119 us -> none  [the longest x1 50.2 us: body(): lax.psum((times_across(back_gate, gate_full) + times_across(back_up, up_f...]
    unnamed x2 -> x0, blocking collectives: 98.3 us -> none
  transfers between devices with their start and end apart: 21 -> 43, of which waited for: 17 -> 19; matrix products, arithmetic and copies ran while one was open for 14% -> 5% of each run, Pallas kernels for 0% -> 16%
where the time goes in v1:
time: 740 us; the launch traced here: 735 us
  waiting for transfers between devices  427 us (58%)
  Pallas kernels  152 us (21%)
  starting transfers between devices  74.2 us (10%)
  other arithmetic  39.2 us (5%)
  local copies, waits for them, and re-layouts  28 us (4%)
  between operations  15 us (2%)
    ppermute x30, waiting for transfers between devices, shifted(): lax.ppermute(field, axis, [(i, (i + steps * stride) % count) for i in ran...  249 us
    ppermute x30, starting transfers between devices, shifted(): lax.ppermute(field, axis, [(i, (i + steps * stride) % count) for i in ran...  67.2 us
    all_gather x1, waiting for transfers between devices, body(): lax.all_gather(jnp.concatenate([gate_weight, up_weight, down_weight, outp...  64.4 us
    ppermute x5, waiting for transfers between devices, swapped(): return lax.ppermute(field, 'tp', [(i, count - 1 - i) for i in range(count)])  57.4 us
    all_gather x1, waiting for transfers between devices, body(): lax.all_gather(jnp.concatenate([query_weight, key_weight, value_weight, g...  55.1 us
    pallas_call x1, Pallas kernels, attend_back(): pl.pallas_call(functools.partial(attend_back_kernel, count), in_specs=[SC...  37 us
    pallas_call x1, Pallas kernels, feed_forward(): pl.pallas_call(feed_kernel, grid=(steps,), in_specs=[full, full, full, wh...  28.1 us
    pallas_call x5, Pallas kernels, gradient(): pl.pallas_call(functools.partial(gradient_kernel, pairs, ctxs), grid=(col...  24.8 us
  transfers between devices with their start and end apart: 43, of which 19 were waited for; matrix products, arithmetic and copies ran while one was open for 5% of the time, Pallas kernels for 16%

profile of v1, /device:TPU:0, one launch (start us, length us, event | category | flops | bytes accessed | tf_op | source)
XLA Modules:
  0.0 735.0 jit_solution(3359252345923048512)
XLA Ops:
  9.8 2.5 pad_maximum_fusion
  13.8 55.1 %all-gather.3.cloned.1.call-done.w_ref = bf16[1536,1664]{1,0:T(8,128)(2,1)} async-done(((bf16[96,1664]{1,0:T(8,128)(2,1)}), bf16[1536,1664]{1,0:T(8,128)(2,1)}) %all-gather.3.cloned.1.call-update) | async-done | bytes 5111824 | tf_op jit(solution)/shard_map/all_gather | solution.py:668
  70.2 2.5 copy-done.4
  72.6 12.3 %project.1 = (bf16[512,768]{1,0:T(8,128)(2,1)S(1)}, bf16[512,768]{1,0:T(8,128)(2,1)S(1)}, bf16[512,1536]{1,0:T(8,128)(2,1)S(1)}) custom-call(bf16[512,1536]{1,0:T(8,128)(2,1)S(1)} %copy-done, f32[8,1536]{1,0:T(8,128)S(1)} %convert_bitcast_fusion.gain_ref, f32[512,48]{1,0:T(8,128)S(1)} %get-tuple-element.116.cos_ref, ...), custom_call_target="tpu_custom_call" | custom-call | flops 2415919104 | bytes 4718592 | tf_op jit(solution)/shard_map/project/pallas_call | solution.py:110
  89.5 2.5 collective-permute-start.2
  92.1 25.5 %collective-permute-done.refs_1_ = bf16[512,768]{1,0:T(8,128)(2,1)S(1)} collective-permute-done((bf16[512,768]{1,0:T(8,128)(2,1)S(1)}, bf16[512,768]{1,0:T(8,128)(2,1)S(1)}, u32[]{:S(2)}, u32[]{:S(2)}) %collective-permute-start) | collective-permute-done | bytes 786464 | tf_op jit(solution)/shard_map/ppermute | solution.py:612
  117.6 33.6 %collective-permute-done.1.refs_2_ = bf16[512,768]{1,0:T(8,128)(2,1)S(1)} collective-permute-done((bf16[512,768]{1,0:T(8,128)(2,1)S(1)}, bf16[512,768]{1,0:T(8,128)(2,1)S(1)}, u32[]{:S(2)}, u32[]{:S(2)}) %collective-permute-start.1) | collective-permute-done | bytes 786464 | tf_op jit(solution)/shard_map/ppermute | solution.py:612
  152.1 4.4 collective-permute-done.2.refs_3_
  158.8 19.5 %attend.1 = (bf16[512,768]{1,0:T(8,128)(2,1)S(1)}, f32[32,96,128]{2,1,0:T(8,128)S(1)}, f32[32,128]{1,0:T(8,128)S(1)}) custom-call(s32[8,4]{1,0:T(8,128)S(1)} %copy.37.order, s32[4]{0:T(128)S(1)} %bitcast_subtract_fusion.1.starts, s32[1]{0:T(128)} %bitcast.4.place, bf16[512,768]{1,0:T(8,128)(2,1)S(1)} %copy-done.35, ...), custom_call_target="tpu_custom_call" | custom-call | flops 8000000000 | bytes 10000000 | tf_op jit(solution)/shard_map/attend/pallas_call | solution.py:242
  180.7 64.4 %all-gather.5.cloned.1.call-done.w_ref.gate_ref.up_ref.down_ref = bf16[1536,6912]{1,0:T(8,128)(2,1)} async-done(((bf16[96,6912]{1,0:T(8,128)(2,1)}), bf16[1536,6912]{1,0:T(8,128)(2,1)}) %all-gather.5.cloned.1.call-update) | async-done | bytes 21233680 | tf_op jit(solution)/shard_map/all_gather | solution.py:672
  245.1 3.0 output_product.1.mine_ref
  249.7 29.4 %collective-permute-done.3.other_ref = bf16[512,1536]{1,0:T(8,128)(2,1)S(1)} collective-permute-done((bf16[512,1536]{1,0:T(8,128)(2,1)S(1)}, bf16[512,1536]{1,0:T(8,128)(2,1)S(1)}, u32[]{:S(2)}, u32[]{:S(2)}) %collective-permute-start.3) | collective-permute-done | bytes 1572896 | tf_op jit(solution)/shard_map/ppermute | solution.py:638
  280.2 28.1 %feed_forward.1 = (f32[512,1536]{1,0:T(8,128)}, bf16[512,1536]{1,0:T(8,128)(2,1)}, bf16[512,2048]{1,0:T(8,128)(2,1)}, bf16[512,2048]{1,0:T(8,128)(2,1)}, bf16[51...) custom-call(bf16[512,1536]{1,0:T(8,128)(2,1)} %x_ref.7, bf16[512,1536]{1,0:T(8,128)(2,1)} %copy-done.2, ...), custom_call_target="tpu_custom_call" | custom-call | flops 16106127360 | bytes 18874368 | tf_op jit(solution)/shard_map/feed_forward/pallas_call | solution.py:417
  311.6 5.8 down_product.1
  318.0 28.0 %collective-permute-done.5.other_ref = bf16[512,1536]{1,0:T(8,128)(2,1)S(1)} collective-permute-done((bf16[512,1536]{1,0:T(8,128)(2,1)}, bf16[512,1536]{1,0:T(8,128)(2,1)S(1)}, u32[]{:S(2)}, u32[]{:S(2)}) %collective-permute-start.5) | collective-permute-done | bytes 1572896 | tf_op jit(solution)/shard_map/ppermute | solution.py:638
  347.1 8.4 %middle_back.1 = (f32[512,1536]{1,0:T(8,128)}, bf16[512,1536]{1,0:T(8,128)(2,1)}, bf16[512,768]{1,0:T(8,128)(2,1)}, f32[1,1536]{1,0:T(1,128)}) custom-call(bf16[512,1536]{1,0:T(8,128)(2,1)} %a_ref.1, bf16[512,1536]{1,0:T(8,128)(2,1)} %get-tuple-element.50.mine_ref, bf16[512,1536]{1,0:T(8,128)(2,1)} %copy-done.39, f32[512,1536]{1,0:T(8,128)} %get-tuple-element.48.middle_ref, ...), custom_call_target="tpu_custom_call" | custom-call | flops 1207959552 | bytes 15000000 | tf_op jit(solution)/shard_map/middle_back/pallas_call | solution.py:479
  355.5 37.0 %attend_back.1 = (bf16[512,768]{1,0:T(8,128)(2,1)}, bf16[512,768]{1,0:T(8,128)(2,1)}, bf16[512,768]{1,0:T(8,128)(2,1)}, bf16[512,768]{1,0:T(8,128)(2,1)}, bf16[512,768]{1,0:T(8,128)(2,1)}) custom-call(s32[8,4]{1,0:T(8,128)} %copy-done.21, s32[4]{0:T(128)} %copy-done.31, s32[1]{0:T(128)} %bitcast.4.place, bf16[512,768]{1,0:T(8,128)(2,1)} %copy-done.34, ...), custom_call_target="tpu_custom_call" | custom-call | flops 16000000000 | bytes 20000000 | tf_op jit(solution)/shard_map/attend_back/pallas_call | solution.py:337
  392.5 12.9 %collective-permute-start.7 = (bf16[512,768]{1,0:T(8,128)(2,1)}, bf16[512,768]{1,0:T(8,128)(2,1)S(1)}, u32[]{:S(2)}, u32[]{:S(2)}) collective-permute-start(bf16[512,768]{1,0:T(8,128)(2,1)} %get-tuple-element.58), channel_id=1, source_target_pairs={{0,4},{2,6},{4,0},{6,2},{1,5},{3,7},{5,1},{7,3},{8,12},{10,14},{12... | collective-permute-start | bytes 2359304 | tf_op jit(solution)/shard_map/ppermute | solution.py:612
  405.4 5.7 gradient.7
  412.8 5.7 gradient.8
  420.8 49.5 %collective-permute-done.7.refs_2_ = bf16[512,768]{1,0:T(8,128)(2,1)S(1)} collective-permute-done((bf16[512,768]{1,0:T(8,128)(2,1)}, bf16[512,768]{1,0:T(8,128)(2,1)S(1)}, u32[]{:S(2)}, u32[]{:S(2)}) %collective-permute-start.7) | collective-permute-done | bytes 786464 | tf_op jit(solution)/shard_map/ppermute | solution.py:612
  471.4 9.7 %inputs_back.1 = (bf16[512,1536]{1,0:T(8,128)(2,1)}, bf16[512,1536]{1,0:T(8,128)(2,1)}, f32[1,1536]{1,0:T(1,128)}) custom-call(bf16[512,1536]{1,0:T(8,128)(2,1)} %x_ref.7, bf16[512,768]{1,0:T(8,128)(2,1)} %get-tuple-element.55.qc_ref, f32[512,48]{1,0:T(8,128)} %copy-done.16, f32[512,48]{1,0:T(8,128)} %copy-done.15, ...), custom_call_target="tpu_custom_call" | custom-call | flops 2415919104 | bytes 15000000 | tf_op jit(solution)/shard_map/inputs_back/pallas_call | solution.py:521
  483.5 2.1 collective-permute-start.11
  488.1 3.4 gradient.6
  494.4 5.7 gradient.9
  502.3 3.3 add_convert_fusion.3
  507.6 4.3 gradient.5
  514.5 3.3 add_convert_fusion.2
  517.8 10.3 %collective-permute-done.22 = bf16[384,768]{1,0:T(8,128)(2,1)S(1)} collective-permute-done((bf16[384,768]{1,0:T(8,128)(2,1)S(1)}, bf16[384,768]{1,0:T(8,128)(2,1)S(1)}, u32[]{:S(2)}, u32[]{:S(2)}) %collective-permute-start.22) | collective-permute-done | bytes 589856 | tf_op jit(solution)/shard_map/ppermute | solution.py:612
  529.7 2.8 collective-permute-start.25
  532.5 3.3 add_convert_fusion.1
  538.0 3.4 add_convert_fusion
  541.4 5.3 collective-permute-done.24
  549.5 2.8 final_back.1
  555.5 10.2 %collective-permute-done.27 = bf16[384,2048]{1,0:T(8,128)(2,1)} collective-permute-done((bf16[384,2048]{1,0:T(8,128)(2,1)}, bf16[384,2048]{1,0:T(8,128)(2,1)}, u32[]{:S(2)}, u32[]{:S(2)}) %collective-permute-start.27) | collective-permute-done | bytes 1572896 | tf_op jit(solution)/shard_map/ppermute | solution.py:612
  565.7 2.9 fusion.38
  568.8 2.8 collective-permute-start.30
  571.8 27.6 %collective-permute-done.32 = bf16[384,2048]{1,0:T(8,128)(2,1)} collective-permute-done((bf16[384,2048]{1,0:T(8,128)(2,1)}, bf16[384,2048]{1,0:T(8,128)(2,1)}, u32[]{:S(2)}, u32[]{:S(2)}) %collective-permute-start.32) | collective-permute-done | bytes 1572896 | tf_op jit(solution)/shard_map/ppermute | solution.py:612
  600.9 2.9 fusion.37
  604.0 29.1 %collective-permute-done.37 = bf16[384,2048]{1,0:T(8,128)(2,1)} collective-permute-done((bf16[384,2048]{1,0:T(8,128)(2,1)}, bf16[384,2048]{1,0:T(8,128)(2,1)}, u32[]{:S(2)}, u32[]{:S(2)}) %collective-permute-start.37) | collective-permute-done | bytes 1572896 | tf_op jit(solution)/shard_map/ppermute | solution.py:612
  633.1 2.8 collective-permute-start.35
  635.9 2.9 fusion.36
  645.5 14.7 %collective-permute-start.39 = (bf16[96,2048]{1,0:T(8,128)(2,1)S(1)}, bf16[96,2048]{1,0:T(8,128)(2,1)S(1)}, u32[]{:S(2)}, u32[]{:S(2)}) collective-permute-start(bf16[96,2048]{1,0:T(8,128)(2,1)S(1)} %get-tuple-element.93), channel_id=1, source_target_pairs={{0,4},{2,6},{4,0},{6,2},{1,5},{3,7},{5,1},{7,3},{8,12},{10,14},{12... | collective-permute-start | bytes 1179656 | tf_op jit(solution)/shard_map/ppermute | solution.py:612
  660.1 23.6 %collective-permute-done.34 = bf16[96,2048]{1,0:T(8,128)(2,1)S(1)} collective-permute-done((bf16[96,2048]{1,0:T(8,128)(2,1)S(1)}, bf16[96,2048]{1,0:T(8,128)(2,1)S(1)}, u32[]{:S(2)}, u32[]{:S(2)}) %collective-permute-start.34) | collective-permute-done | bytes 393248 | tf_op jit(solution)/shard_map/ppermute | solution.py:612
  686.7 3.9 collective-permute-start.20
  692.1 5.0 collective-permute-start.18
  697.0 20.5 %collective-permute-done.39 = bf16[96,2048]{1,0:T(8,128)(2,1)S(1)} collective-permute-done((bf16[96,2048]{1,0:T(8,128)(2,1)S(1)}, bf16[96,2048]{1,0:T(8,128)(2,1)S(1)}, u32[]{:S(2)}, u32[]{:S(2)}) %collective-permute-start.39) | collective-permute-done | bytes 393248 | tf_op jit(solution)/shard_map/ppermute | solution.py:612
  718.6 7.5 %collective-permute-done.19 = bf16[96,1536]{1,0:T(8,128)(2,1)S(1)} collective-permute-done((bf16[96,1536]{1,0:T(8,128)(2,1)S(1)}, bf16[96,1536]{1,0:T(8,128)(2,1)S(1)}, u32[]{:S(2)}, u32[]{:S(2)}) %collective-permute-start.19) | collective-permute-done | bytes 294944 | tf_op jit(solution)/shard_map/ppermute | solution.py:612
  (209 shorter events, 68.1 us)
Async XLA Ops:
  7.2 61.8 %all-gather.3.cloned.1.call-start = ((), (), s32[]{:S(2)}) async-start(), calls=%async_computation | async-start | bytes 5431296 | tf_op jit(solution)/shard_map/all_gather | solution.py:668
  9.8 235.3 %all-gather.5.cloned.1.call-start = ((), (), s32[]{:S(2)}) async-start(), calls=%async_computation.1 | async-start | bytes 22560768 | tf_op jit(solution)/shard_map/all_gather | solution.py:672
  13.8 71.1 %copy-start.15 = (f32[512,48]{1,0:T(8,128)}, f32[512,48]{1,0:T(8,128)S(1)}, u32[]{:S(2)}) copy-start(f32[512,48]{1,0:T(8,128)S(1)} %get-tuple-element.115.sin_ref) | copy-start | bytes 294916
  13.8 71.1 %copy-start.16 = (f32[512,48]{1,0:T(8,128)}, f32[512,48]{1,0:T(8,128)S(1)}, u32[]{:S(2)}) copy-start(f32[512,48]{1,0:T(8,128)S(1)} %get-tuple-element.116.cos_ref) | copy-start | bytes 294916
  87.1 91.3 %copy-start.27 = (bf16[512,768]{1,0:T(8,128)(2,1)}, bf16[512,768]{1,0:T(8,128)(2,1)S(1)}, u32[]{:S(2)}) copy-start(bf16[512,768]{1,0:T(8,128)(2,1)S(1)} %get-tuple-element.46.refs_0_) | copy-start | bytes 2359300
  87.1 30.6 %collective-permute-start = (bf16[512,768]{1,0:T(8,128)(2,1)S(1)}, bf16[512,768]{1,0:T(8,128)(2,1)S(1)}, u32[]{:S(2)}, u32[]{:S(2)}) collective-permute-start(bf16[512,768]{1,0:T(8,128)(2,1)S(1)} %get-tuple-element.46.refs_0_), channel_id=1, source_target_pairs={{0,2},{2,4},{4,6},{6,0},{1,3},{3,5},{5,7},{7,1},{8,10},{10,12},{12... | collective-permute-start | bytes 2359304 | tf_op jit(solution)/shard_map/ppermute | solution.py:612
  88.6 62.6 %collective-permute-start.1 = (bf16[512,768]{1,0:T(8,128)(2,1)S(1)}, bf16[512,768]{1,0:T(8,128)(2,1)S(1)}, u32[]{:S(2)}, u32[]{:S(2)}) collective-permute-start(bf16[512,768]{1,0:T(8,128)(2,1)S(1)} %get-tuple-element.46.refs_0_), channel_id=1, source_target_pairs={{0,4},{2,6},{4,0},{6,2},{1,5},{3,7},{5,1},{7,3},{8,12},{10,14},{12... | collective-permute-start | bytes 2359304 | tf_op jit(solution)/shard_map/ppermute | solution.py:612
  89.5 67.0 %collective-permute-start.2 = (bf16[512,768]{1,0:T(8,128)(2,1)S(1)}, bf16[512,768]{1,0:T(8,128)(2,1)}, u32[]{:S(2)}, u32[]{:S(2)}) collective-permute-start(bf16[512,768]{1,0:T(8,128)(2,1)S(1)} %get-tuple-element.46.refs_0_), channel_id=1, source_target_pairs={{0,6},{2,0},{4,2},{6,4},{1,7},{3,1},{5,3},{7,5},{8,14},{10,8},{12,... | collective-permute-start | bytes 2359304 | tf_op jit(solution)/shard_map/ppermute | solution.py:612
  92.1 86.3 %copy-start.21 = (s32[8,4]{1,0:T(8,128)}, s32[8,4]{1,0:T(8,128)S(1)}, u32[]{:S(2)}) copy-start(s32[8,4]{1,0:T(8,128)S(1)} %copy.37.order) | copy-start | bytes 388
  180.7 67.4 %copy-start.17 = (bf16[512,768]{1,0:T(8,128)(2,1)}, bf16[512,768]{1,0:T(8,128)(2,1)S(1)}, u32[]{:S(2)}) copy-start(bf16[512,768]{1,0:T(8,128)(2,1)S(1)} %get-tuple-element.47.a_ref.b_ref) | copy-start | bytes 2359300
  248.1 30.9 %collective-permute-start.3 = (bf16[512,1536]{1,0:T(8,128)(2,1)S(1)}, bf16[512,1536]{1,0:T(8,128)(2,1)S(1)}, u32[]{:S(2)}, u32[]{:S(2)}) collective-permute-start(bf16[512,1536]{1,0:T(8,128)(2,1)S(1)} %output_product.1.mine_ref), channel_id=1, source_target_pairs={{0,1},{1,0},{2,3},{3,2},{4,5},{5,4},{6,7},{7,6},{8,9},{9,8},{10,11... | collective-permute-start | bytes 4718600 | tf_op jit(solution)/shard_map/ppermute | solution.py:638
  308.4 37.6 %collective-permute-start.5 = (bf16[512,1536]{1,0:T(8,128)(2,1)}, bf16[512,1536]{1,0:T(8,128)(2,1)S(1)}, u32[]{:S(2)}, u32[]{:S(2)}) collective-permute-start(bf16[512,1536]{1,0:T(8,128)(2,1)} %get-tuple-element.50.mine_ref), channel_id=1, source_target_pairs={{0,1},{1,0},{2,3},{3,2},{4,5},{5,4},{6,7},{7,6},{8,9},{9,8},{10,11... | collective-permute-start | bytes 4718600 | tf_op jit(solution)/shard_map/ppermute | solution.py:638
  317.4 175.3 %collective-permute-start.4 = (bf16[512,1536]{1,0:T(8,128)(2,1)S(1)}, bf16[512,1536]{1,0:T(8,128)(2,1)}, u32[]{:S(2)}, u32[]{:S(2)}) collective-permute-start(bf16[512,1536]{1,0:T(8,128)(2,1)S(1)} %down_product.1), channel_id=1, source_target_pairs={{0,1},{1,0},{2,3},{3,2},{4,5},{5,4},{6,7},{7,6},{8,9},{9,8},{10,11... | collective-permute-start | bytes 4718600 | tf_op jit(solution)/shard_map/ppermute | solution.py:638
  392.5 27.7 %collective-permute-start.6 = (bf16[512,768]{1,0:T(8,128)(2,1)}, bf16[512,768]{1,0:T(8,128)(2,1)S(1)}, u32[]{:S(2)}, u32[]{:S(2)}) collective-permute-start(bf16[512,768]{1,0:T(8,128)(2,1)} %get-tuple-element.57), channel_id=1, source_target_pairs={{0,6},{2,0},{4,2},{6,4},{1,7},{3,1},{5,3},{7,5},{8,14},{10,8},{12,... | collective-permute-start | bytes 2359304 | tf_op jit(solution)/shard_map/ppermute | solution.py:612
  392.5 77.7 %collective-permute-start.7 = (bf16[512,768]{1,0:T(8,128)(2,1)}, bf16[512,768]{1,0:T(8,128)(2,1)S(1)}, u32[]{:S(2)}, u32[]{:S(2)}) collective-permute-start(bf16[512,768]{1,0:T(8,128)(2,1)} %get-tuple-element.58), channel_id=1, source_target_pairs={{0,4},{2,6},{4,0},{6,2},{1,5},{3,7},{5,1},{7,3},{8,12},{10,14},{12... | collective-permute-start | bytes 2359304 | tf_op jit(solution)/shard_map/ppermute | solution.py:612
  405.4 64.9 %collective-permute-start.8 = (bf16[512,768]{1,0:T(8,128)(2,1)}, bf16[512,768]{1,0:T(8,128)(2,1)S(1)}, u32[]{:S(2)}, u32[]{:S(2)}) collective-permute-start(bf16[512,768]{1,0:T(8,128)(2,1)} %get-tuple-element.59), channel_id=1, source_target_pairs={{0,2},{2,4},{4,6},{6,0},{1,3},{3,5},{5,7},{7,1},{8,10},{10,12},{12... | collective-permute-start | bytes 2359304 | tf_op jit(solution)/shard_map/ppermute | solution.py:612
  412.8 101.8 %collective-permute-start.26 = (bf16[768,2048]{1,0:T(8,128)(2,1)}, bf16[768,2048]{1,0:T(8,128)(2,1)}, u32[]{:S(2)}, u32[]{:S(2)}) collective-permute-start(bf16[768,2048]{1,0:T(8,128)(2,1)} %get-tuple-element.72), channel_id=1, source_target_pairs={{0,8},{8,0},{16,24},{24,16},{1,9},{9,1},{17,25},{25,17},{2,10},{10... | collective-permute-start | bytes 9437192 | tf_op jit(solution)/shard_map/ppermute | solution.py:618
  420.2 109.5 %collective-permute-start.31 = (bf16[768,2048]{1,0:T(8,128)(2,1)}, bf16[768,2048]{1,0:T(8,128)(2,1)}, u32[]{:S(2)}, u32[]{:S(2)}) collective-permute-start(bf16[768,2048]{1,0:T(8,128)(2,1)} %get-tuple-element.75), channel_id=1, source_target_pairs={{0,8},{8,0},{16,24},{24,16},{1,9},{9,1},{17,25},{25,17},{2,10},{10... | collective-permute-start | bytes 9437192 | tf_op jit(solution)/shard_map/ppermute | solution.py:618
  482.3 1.2 collective-permute-start.10
  483.5 9.1 %collective-permute-start.11 = (bf16[384,8]{0,1:T(8,128)(2,1)S(1)}, bf16[384,8]{0,1:T(8,128)(2,1)S(1)}, u32[]{:S(2)}, u32[]{:S(2)}) collective-permute-start(bf16[384,8]{0,1:T(8,128)(2,1)S(1)} %add_convert_fusion.6), channel_id=1, source_target_pairs={{0,16},{8,24},{16,0},{24,8},{1,17},{9,25},{17,1},{25,9},{2,18},{10... | collective-permute-start | bytes 18440 | tf_op jit(solution)/shard_map/ppermute | solution.py:612
  492.5 20.1 %collective-permute-start.21 = (bf16[768,768]{1,0:T(8,128)(2,1)}, bf16[768,768]{1,0:T(8,128)(2,1)}, u32[]{:S(2)}, u32[]{:S(2)}) collective-permute-start(bf16[768,768]{1,0:T(8,128)(2,1)} %get-tuple-element.68), channel_id=1, source_target_pairs={{0,8},{8,0},{16,24},{24,16},{1,9},{9,1},{17,25},{25,17},{2,10},{10... | collective-permute-start | bytes 3538952 | tf_op jit(solution)/shard_map/ppermute | solution.py:618
  492.6 7.4 %collective-permute-start.14 = (bf16[96,8]{0,1:T(8,128)(2,1)S(1)}, bf16[96,8]{0,1:T(8,128)(2,1)S(1)}, u32[]{:S(2)}, u32[]{:S(2)}) collective-permute-start(bf16[96,8]{0,1:T(8,128)(2,1)S(1)} %get-tuple-element.111), channel_id=1, source_target_pairs={{0,6},{2,0},{4,2},{6,4},{1,7},{3,1},{5,3},{7,5},{8,14},{10,8},{12,... | collective-permute-start | bytes 4616 | tf_op jit(solution)/shard_map/ppermute | solution.py:612
  492.7 7.9 %collective-permute-start.13 = (bf16[96,8]{0,1:T(8,128)(2,1)S(1)}, bf16[96,8]{0,1:T(8,128)(2,1)S(1)}, u32[]{:S(2)}, u32[]{:S(2)}) collective-permute-start(bf16[96,8]{0,1:T(8,128)(2,1)S(1)} %get-tuple-element.112), channel_id=1, source_target_pairs={{0,4},{2,6},{4,0},{6,2},{1,5},{3,7},{5,1},{7,3},{8,12},{10,14},{12... | collective-permute-start | bytes 4616 | tf_op jit(solution)/shard_map/ppermute | solution.py:612
  500.1 35.8 %collective-permute-start.36 = (bf16[768,2048]{1,0:T(8,128)(2,1)}, bf16[768,2048]{1,0:T(8,128)(2,1)}, u32[]{:S(2)}, u32[]{:S(2)}) collective-permute-start(bf16[768,2048]{1,0:T(8,128)(2,1)} %get-tuple-element.77), channel_id=1, source_target_pairs={{0,8},{8,0},{16,24},{24,16},{1,9},{9,1},{17,25},{25,17},{2,10},{10... | collective-permute-start | bytes 9437192 | tf_op jit(solution)/shard_map/ppermute | solution.py:618
  500.6 5.4 collective-permute-start.12
  506.1 5.9 collective-permute-start.15
  511.9 37.5 %collective-permute-start.9 = (bf16[512,1536]{1,0:T(8,128)(2,1)S(1)}, bf16[512,1536]{1,0:T(8,128)(2,1)S(1)}, u32[]{:S(2)}, u32[]{:S(2)}) collective-permute-start(bf16[512,1536]{1,0:T(8,128)(2,1)S(1)} %copy-done.12), channel_id=1, source_target_pairs={{0,1},{1,0},{2,3},{3,2},{4,5},{5,4},{6,7},{7,6},{8,9},{9,8},{10,11... | collective-permute-start | bytes 4718600 | tf_op jit(solution)/shard_map/ppermute | solution.py:638
  513.8 14.3 %collective-permute-start.22 = (bf16[384,768]{1,0:T(8,128)(2,1)S(1)}, bf16[384,768]{1,0:T(8,128)(2,1)S(1)}, u32[]{:S(2)}, u32[]{:S(2)}) collective-permute-start(bf16[384,768]{1,0:T(8,128)(2,1)S(1)} %add_convert_fusion.5), channel_id=1, source_target_pairs={{0,16},{8,24},{16,0},{24,8},{1,17},{9,25},{17,1},{25,9},{2,18},{10... | collective-permute-start | bytes 1769480 | tf_op jit(solution)/shard_map/ppermute | solution.py:612
  514.5 37.7 %collective-permute-start.16 = (bf16[768,1536]{1,0:T(8,128)(2,1)S(1)}, bf16[768,1536]{1,0:T(8,128)(2,1)}, u32[]{:S(2)}, u32[]{:S(2)}) collective-permute-start(bf16[768,1536]{1,0:T(8,128)(2,1)S(1)} %get-tuple-element.65), channel_id=1, source_target_pairs={{0,8},{8,0},{16,24},{24,16},{1,9},{9,1},{17,25},{25,17},{2,10},{10... | collective-permute-start | bytes 7077896 | tf_op jit(solution)/shard_map/ppermute | solution.py:618
  528.1 37.6 %collective-permute-start.27 = (bf16[384,2048]{1,0:T(8,128)(2,1)}, bf16[384,2048]{1,0:T(8,128)(2,1)}, u32[]{:S(2)}, u32[]{:S(2)}) collective-permute-start(bf16[384,2048]{1,0:T(8,128)(2,1)} %add_convert_fusion.2), channel_id=1, source_target_pairs={{0,16},{8,24},{16,0},{24,8},{1,17},{9,25},{17,1},{25,9},{2,18},{10... | collective-permute-start | bytes 4718600 | tf_op jit(solution)/shard_map/ppermute | solution.py:612
  529.7 6.3 collective-permute-start.25
  535.9 10.8 %collective-permute-start.24 = (bf16[96,768]{1,0:T(8,128)(2,1)S(1)}, bf16[96,768]{1,0:T(8,128)(2,1)S(1)}, u32[]{:S(2)}, u32[]{:S(2)}) collective-permute-start(bf16[96,768]{1,0:T(8,128)(2,1)S(1)} %get-tuple-element.105), channel_id=1, source_target_pairs={{0,4},{2,6},{4,0},{6,2},{1,5},{3,7},{5,1},{7,3},{8,12},{10,14},{12... | collective-permute-start | bytes 442376 | tf_op jit(solution)/shard_map/ppermute | solution.py:612
  536.0 12.2 %collective-permute-start.23 = (bf16[96,768]{1,0:T(8,128)(2,1)S(1)}, bf16[96,768]{1,0:T(8,128)(2,1)S(1)}, u32[]{:S(2)}, u32[]{:S(2)}) collective-permute-start(bf16[96,768]{1,0:T(8,128)(2,1)S(1)} %get-tuple-element.103), channel_id=1, source_target_pairs={{0,2},{2,4},{4,6},{6,0},{1,3},{3,5},{5,7},{7,1},{8,10},{10,12},{12... | collective-permute-start | bytes 442376 | tf_op jit(solution)/shard_map/ppermute | solution.py:612
  546.6 52.8 %collective-permute-start.32 = (bf16[384,2048]{1,0:T(8,128)(2,1)}, bf16[384,2048]{1,0:T(8,128)(2,1)}, u32[]{:S(2)}, u32[]{:S(2)}) collective-permute-start(bf16[384,2048]{1,0:T(8,128)(2,1)} %add_convert_fusion.1), channel_id=1, source_target_pairs={{0,16},{8,24},{16,0},{24,8},{1,17},{9,25},{17,1},{25,9},{2,18},{10... | collective-permute-start | bytes 4718600 | tf_op jit(solution)/shard_map/ppermute | solution.py:612
  548.3 84.9 %collective-permute-start.37 = (bf16[384,2048]{1,0:T(8,128)(2,1)}, bf16[384,2048]{1,0:T(8,128)(2,1)}, u32[]{:S(2)}, u32[]{:S(2)}) collective-permute-start(bf16[384,2048]{1,0:T(8,128)(2,1)} %add_convert_fusion), channel_id=1, source_target_pairs={{0,16},{8,24},{16,0},{24,8},{1,17},{9,25},{17,1},{25,9},{2,18},{10... | collective-permute-start | bytes 4718600 | tf_op jit(solution)/shard_map/ppermute | solution.py:612
  553.8 131.0 %collective-permute-start.17 = (bf16[384,1536]{1,0:T(8,128)(2,1)S(1)}, bf16[384,1536]{1,0:T(8,128)(2,1)S(1)}, u32[]{:S(2)}, u32[]{:S(2)}) collective-permute-start(bf16[384,1536]{1,0:T(8,128)(2,1)S(1)} %add_convert_fusion.4), channel_id=1, source_target_pairs={{0,16},{8,24},{16,0},{24,8},{1,17},{9,25},{17,1},{25,9},{2,18},{10... | collective-permute-start | bytes 3538952 | tf_op jit(solution)/shard_map/ppermute | solution.py:612
  568.8 70.1 %collective-permute-start.30 = (bf16[96,2048]{1,0:T(8,128)(2,1)S(1)}, bf16[96,2048]{1,0:T(8,128)(2,1)S(1)}, u32[]{:S(2)}, u32[]{:S(2)}) collective-permute-start(bf16[96,2048]{1,0:T(8,128)(2,1)S(1)} %get-tuple-element.98), channel_id=1, source_target_pairs={{0,6},{2,0},{4,2},{6,4},{1,7},{3,1},{5,3},{7,5},{8,14},{10,8},{12,... | collective-permute-start | bytes 1179656 | tf_op jit(solution)/shard_map/ppermute | solution.py:612
  571.6 67.6 %collective-permute-start.29 = (bf16[96,2048]{1,0:T(8,128)(2,1)S(1)}, bf16[96,2048]{1,0:T(8,128)(2,1)S(1)}, u32[]{:S(2)}, u32[]{:S(2)}) collective-permute-start(bf16[96,2048]{1,0:T(8,128)(2,1)S(1)} %get-tuple-element.99), channel_id=1, source_target_pairs={{0,4},{2,6},{4,0},{6,2},{1,5},{3,7},{5,1},{7,3},{8,12},{10,14},{12... | collective-permute-start | bytes 1179656 | tf_op jit(solution)/shard_map/ppermute | solution.py:612
  599.4 41.7 %collective-permute-start.28 = (bf16[96,2048]{1,0:T(8,128)(2,1)S(1)}, bf16[96,2048]{1,0:T(8,128)(2,1)S(1)}, u32[]{:S(2)}, u32[]{:S(2)}) collective-permute-start(bf16[96,2048]{1,0:T(8,128)(2,1)S(1)} %get-tuple-element.97), channel_id=1, source_target_pairs={{0,2},{2,4},{4,6},{6,0},{1,3},{3,5},{5,7},{7,1},{8,10},{10,12},{12... | collective-permute-start | bytes 1179656 | tf_op jit(solution)/shard_map/ppermute | solution.py:612
  633.1 12.3 %collective-permute-start.35 = (bf16[96,2048]{1,0:T(8,128)(2,1)S(1)}, bf16[96,2048]{1,0:T(8,128)(2,1)S(1)}, u32[]{:S(2)}, u32[]{:S(2)}) collective-permute-start(bf16[96,2048]{1,0:T(8,128)(2,1)S(1)} %get-tuple-element.95), channel_id=1, source_target_pairs={{0,6},{2,0},{4,2},{6,4},{1,7},{3,1},{5,3},{7,5},{8,14},{10,8},{12,... | collective-permute-start | bytes 1179656 | tf_op jit(solution)/shard_map/ppermute | solution.py:612
  638.9 44.8 %collective-permute-start.34 = (bf16[96,2048]{1,0:T(8,128)(2,1)S(1)}, bf16[96,2048]{1,0:T(8,128)(2,1)S(1)}, u32[]{:S(2)}, u32[]{:S(2)}) collective-permute-start(bf16[96,2048]{1,0:T(8,128)(2,1)S(1)} %get-tuple-element.96), channel_id=1, source_target_pairs={{0,4},{2,6},{4,0},{6,2},{1,5},{3,7},{5,1},{7,3},{8,12},{10,14},{12... | collective-permute-start | bytes 1179656 | tf_op jit(solution)/shard_map/ppermute | solution.py:612
  639.2 44.6 %collective-permute-start.33 = (bf16[96,2048]{1,0:T(8,128)(2,1)S(1)}, bf16[96,2048]{1,0:T(8,128)(2,1)S(1)}, u32[]{:S(2)}, u32[]{:S(2)}) collective-permute-start(bf16[96,2048]{1,0:T(8,128)(2,1)S(1)} %get-tuple-element.94), channel_id=1, source_target_pairs={{0,2},{2,4},{4,6},{6,0},{1,3},{3,5},{5,7},{7,1},{8,10},{10,12},{12... | collective-permute-start | bytes 1179656 | tf_op jit(solution)/shard_map/ppermute | solution.py:612
  641.1 50.9 %collective-permute-start.40 = (bf16[96,2048]{1,0:T(8,128)(2,1)S(1)}, bf16[96,2048]{1,0:T(8,128)(2,1)S(1)}, u32[]{:S(2)}, u32[]{:S(2)}) collective-permute-start(bf16[96,2048]{1,0:T(8,128)(2,1)S(1)} %get-tuple-element.92), channel_id=1, source_target_pairs={{0,6},{2,0},{4,2},{6,4},{1,7},{3,1},{5,3},{7,5},{8,14},{10,8},{12,... | collective-permute-start | bytes 1179656 | tf_op jit(solution)/shard_map/ppermute | solution.py:612
  645.5 72.1 %collective-permute-start.39 = (bf16[96,2048]{1,0:T(8,128)(2,1)S(1)}, bf16[96,2048]{1,0:T(8,128)(2,1)S(1)}, u32[]{:S(2)}, u32[]{:S(2)}) collective-permute-start(bf16[96,2048]{1,0:T(8,128)(2,1)S(1)} %get-tuple-element.93), channel_id=1, source_target_pairs={{0,4},{2,6},{4,0},{6,2},{1,5},{3,7},{5,1},{7,3},{8,12},{10,14},{12... | collective-permute-start | bytes 1179656 | tf_op jit(solution)/shard_map/ppermute | solution.py:612
  683.8 33.8 %collective-permute-start.38 = (bf16[96,2048]{1,0:T(8,128)(2,1)S(1)}, bf16[96,2048]{1,0:T(8,128)(2,1)S(1)}, u32[]{:S(2)}, u32[]{:S(2)}) collective-permute-start(bf16[96,2048]{1,0:T(8,128)(2,1)S(1)} %get-tuple-element.91), channel_id=1, source_target_pairs={{0,2},{2,4},{4,6},{6,0},{1,3},{3,5},{5,7},{7,1},{8,10},{10,12},{12... | collective-permute-start | bytes 1179656 | tf_op jit(solution)/shard_map/ppermute | solution.py:612
  686.7 31.9 %collective-permute-start.20 = (bf16[96,1536]{1,0:T(8,128)(2,1)S(1)}, bf16[96,1536]{1,0:T(8,128)(2,1)S(1)}, u32[]{:S(2)}, u32[]{:S(2)}) collective-permute-start(bf16[96,1536]{1,0:T(8,128)(2,1)S(1)} %get-tuple-element.101), channel_id=1, source_target_pairs={{0,6},{2,0},{4,2},{6,4},{1,7},{3,1},{5,3},{7,5},{8,14},{10,8},{12,... | collective-permute-start | bytes 884744 | tf_op jit(solution)/shard_map/ppermute | solution.py:612
  690.5 35.6 %collective-permute-start.19 = (bf16[96,1536]{1,0:T(8,128)(2,1)S(1)}, bf16[96,1536]{1,0:T(8,128)(2,1)S(1)}, u32[]{:S(2)}, u32[]{:S(2)}) collective-permute-start(bf16[96,1536]{1,0:T(8,128)(2,1)S(1)} %get-tuple-element.102), channel_id=1, source_target_pairs={{0,4},{2,6},{4,0},{6,2},{1,5},{3,7},{5,1},{7,3},{8,12},{10,14},{12... | collective-permute-start | bytes 884744 | tf_op jit(solution)/shard_map/ppermute | solution.py:612
  692.1 34.1 %collective-permute-start.18 = (bf16[96,1536]{1,0:T(8,128)(2,1)S(1)}, bf16[96,1536]{1,0:T(8,128)(2,1)S(1)}, u32[]{:S(2)}, u32[]{:S(2)}) collective-permute-start(bf16[96,1536]{1,0:T(8,128)(2,1)S(1)} %get-tuple-element.100), channel_id=1, source_target_pairs={{0,2},{2,4},{4,6},{6,0},{1,3},{3,5},{5,7},{7,1},{8,10},{10,12},{12... | collective-permute-start | bytes 884744 | tf_op jit(solution)/shard_map/ppermute | solution.py:612
  (42 other events, 450.7 us)
Sparse Core Ops, SparseCore 0:
  10.9 58.0 all-gather.2
  71.1 173.9 all-gather.4

commit v2 on v1

--- a/solution.py
+++ b/solution.py
@@ -131,6 +131,126 @@
         cost_estimate=cost(2 * rows * width * 4 * tile, 2 * width * 4 * tile),
         name="project",
     )(x, gains, cosine, sine, weights)
+
+
+MESH = pl.DeviceIdType.MESH
+
+
+def gather_project_kernel(
+    shard_ref, x_ref, cos_ref, sin_ref,
+    full_ref, q_ref, kv_ref, normed_ref, gain_ref,
+    w_ref, z_send, z_recv, y_send, y_recv, c_send, c_recv, k_send, k_recv, local,
+):
+    ctxs = lax.axis_size("ctx")
+    dp, ctx, tp = lax.axis_index("dp"), lax.axis_index("ctx"), lax.axis_index("tp")
+    far, core = (lax.rem(dp + 2, 4), ctx, tp), (dp + 1 - 2 * lax.rem(dp, 2), ctx, tp)
+    after, before = (dp, lax.rem(ctx + 1, ctxs), tp), (dp, lax.rem(ctx + ctxs - 1, ctxs), tp)
+    barrier = pltpu.get_barrier_semaphore()
+    for device in (after, before, far, core):
+        pl.semaphore_signal(barrier, inc=1, device_id=device, device_id_type=MESH)
+    pl.semaphore_wait(barrier, 4)
+    piece = shard_ref.shape[0]
+
+    def block(pair, steps):
+        owner = pair * ctxs + lax.rem(ctx - steps + ctxs, ctxs)
+        return w_ref.at[pl.ds(pl.multiple_of(owner * piece, piece), piece)]
+
+    def send(source, target, device, sent, got):
+        copy = pltpu.make_async_remote_copy(source, target, sent, got, device, MESH)
+        copy.start()
+        return copy
+
+    copies, y_copies, c_copies, z_copies = [], [], [], []
+    for s in range(ctxs):
+        place = block(dp, s)
+        source = place if s else shard_ref
+        if s:
+            z_copies[s - 1].wait_recv()
+        if s < ctxs - 1:
+            z_copies.append(send(source, place, after, z_send.at[s], z_recv.at[s]))
+        y_copies.append(send(source, place, far, y_send.at[s], y_recv.at[s]))
+        c_copies.append(send(source, place, core, c_send.at[s], c_recv.at[s]))
+        if s == 0:
+            own = pltpu.make_async_copy(shard_ref, place, local.at[0])
+            own.start()
+            x = x_ref[...].astype(f32)
+            unit = x * lax.rsqrt(jnp.mean(x * x, axis=1, keepdims=True) + epsilon)
+    for s in range(ctxs):
+        y_copies[s].wait_recv()
+        place = block(far[0], s)
+        c_copies.append(send(place, place, core, c_send.at[ctxs + s], c_recv.at[ctxs + s]))
+    own.wait()
+    for copy in c_copies:
+        copy.wait_recv()
+    full = pltpu.make_async_copy(w_ref, full_ref, local.at[1])
+    full.start()
+
+    q_cols = q_ref.shape[1]
+    tile = q_cols // 2
+    gains = w_ref[:, 2 * q_cols : 2 * q_cols + LANES].astype(f32).T[:8]
+    gain_ref[...] = gains
+    normed_ref[...] = (unit * gains[0:1]).astype(bf16)
+
+    def rotated(out, store):
+        for h in range(tile // HEAD_SIZE):
+            lanes = slice(h * HEAD_SIZE, (h + 1) * HEAD_SIZE)
+            store(lanes, turned(out[:, lanes], cos_ref[...], sin_ref[...], 1).astype(bf16))
+
+    def key_store(lanes, value):
+        kv_ref[0, :, lanes] = value
+
+    def product(step):
+        return dot(normed_ref[...], w_ref[:, step * tile : (step + 1) * tile], NN)
+
+    rotated(product(2), key_store)
+    kv_ref[0, :, tile:] = product(3).astype(bf16)
+    k_copies = [send(kv_ref.at[0], kv_ref.at[1], after, k_send.at[0], k_recv.at[0])]
+
+    for step in range(2):
+
+        def query_store(lanes, value):
+            q_ref[:, step * tile + lanes.start : step * tile + lanes.stop] = value
+
+        rotated(product(step), query_store)
+    for s in range(1, ctxs):
+        k_copies[s - 1].wait_recv()
+        if s < ctxs - 1:
+            k_copies.append(
+                send(kv_ref.at[s], kv_ref.at[s + 1], after, k_send.at[s], k_recv.at[s])
+            )
+    for copy in z_copies + y_copies + c_copies + k_copies:
+        copy.wait_send()
+    full.wait()
+
+
+def gather_project(shard, x, cosine, sine, q_cols, ctxs):
+    rows, width = x.shape
+    columns = shard.shape[1]
+    vmem = pl.BlockSpec(memory_space=pltpu.VMEM)
+    sems = lambda n: pltpu.SemaphoreType.DMA((n,))
+    return pl.pallas_call(
+        gather_project_kernel,
+        in_specs=[vmem] * 4,
+        out_specs=[pl.BlockSpec(memory_space=pl.ANY)] + [vmem] * 4,
+        out_shape=[
+            jax.ShapeDtypeStruct((width, columns), bf16),
+            jax.ShapeDtypeStruct((rows, q_cols), bf16),
+            jax.ShapeDtypeStruct((ctxs, rows, q_cols), bf16),
+            jax.ShapeDtypeStruct((rows, width), bf16),
+            jax.ShapeDtypeStruct((8, width), f32),
+        ],
+        scratch_shapes=[pltpu.VMEM((width, columns), bf16)]
+        + [sems(ctxs - 1)] * 2
+        + [sems(ctxs)] * 2
+        + [sems(2 * ctxs)] * 2
+        + [sems(ctxs - 1)] * 2
+        + [sems(2)],
+        compiler_params=pltpu.CompilerParams(
+            vmem_limit_bytes=48 * MIB, collective_id=0, has_side_effects=True
+        ),
+        cost_estimate=cost(2 * rows * width * 2 * q_cols, 1e8),
+        name="gather_project",
+    )(shard, x, cosine, sine)
 
 
 def gather_stream(order, ctx, pieces, k_ref, v_ref):
@@ -665,22 +785,26 @@
     hidden = gate_weight.shape[1]
 
     gain_columns = jnp.pad(jnp.stack([pre_gain, mid_gain], axis=1), ((0, 0), (0, LANES - 2)))
-    first = lax.all_gather(
-        jnp.concatenate([query_weight, key_weight, value_weight, gain_columns], axis=1),
-        ROWS, axis=0, tiled=True,
+    shard = jnp.concatenate(
+        [query_weight, key_weight, value_weight, gain_columns, output_weight], axis=1
     )
     second = lax.all_gather(
-        jnp.concatenate([gate_weight, up_weight, down_weight, output_weight], axis=1),
-        ROWS, axis=0, tiled=True,
-    )
-    output_column = 3 * hidden // q_cols
-    gains = first[:, 2 * q_cols : 2 * q_cols + 8].T.astype(f32)
-
+        jnp.concatenate([gate_weight, up_weight, down_weight], axis=1), ROWS, axis=0, tiled=True
+    )
     cosine, sine = angles(own_places(starts, order, ctx, ctxs))
-    queries, kv, normed = project(tokens, gains, cosine, sine, first, q_cols)
-    pieces = [kv] + [shifted(kv, "ctx", k) for k in range(1, ctxs)]
+    if pairs == 2 and shard.shape[0] % 16 == 0:
+        first, queries, kv, normed, gains = gather_project(
+            shard, tokens, cosine, sine, q_cols, ctxs
+        )
+        pieces = [kv[k] for k in range(ctxs)]
+    else:
+        first = lax.all_gather(shard, ROWS, axis=0, tiled=True)
+        gains = first[:, 2 * q_cols : 2 * q_cols + 8].T.astype(f32)
+        queries, kv, normed = project(tokens, gains, cosine, sine, first, q_cols)
+        pieces = [kv] + [shifted(kv, "ctx", k) for k in range(1, ctxs)]
+    output_weights = first[:, 2 * q_cols + LANES :]
     attended_low, att, sums = attend(order, starts, place, queries, pieces)
-    branch = output_product(attended_low, second, output_column, features)
+    branch = output_product(attended_low, output_weights, 0, features)
     middle, mid_normed, mixed, back_gate, back_up, back_part = feed_forward(
         tokens, branch, swapped(branch), gains, cotangent, second, hidden
     )
@@ -692,7 +816,7 @@
     result = (middle + feed.astype(f32) + swapped(feed).astype(f32)).astype(bf16)
 
     back_middle, back_branch, back_attended, mid_grad = middle_back(
-        cotangent, back_part, back_other, middle, gains, second, output_column, q_cols
+        cotangent, back_part, back_other, middle, gains, output_weights, 0, q_cols
     )
     output_parts = gradient(back_branch, attended_low, pairs, ctxs)
     back = attend_back(

time: 740 us -> 686 us (0.927)
  waiting for transfers between devices: 427 us -> 244 us
  Pallas kernels: 152 us -> 294 us
    pallas_call x1, Pallas kernels: 12.3 us -> 153 us  [gather_project(): pl.pallas_call(gather_project_kernel, in_specs=[vmem] * 4, out_specs=[pl....]
    all_gather x2 -> x1, waiting for transfers between devices: 120 us -> 0.01 us  [body(): lax.all_gather(jnp.concatenate([gate_weight, up_weight, down_weight], axi...]
    ppermute x30 -> x27, waiting for transfers between devices: 249 us -> 181 us  [shifted(): lax.ppermute(field, axis, [(i, (i + steps * stride) % count) for i in ran...]
    ppermute x30 -> x27, starting transfers between devices: 67.2 us -> 58 us  [shifted(): lax.ppermute(field, axis, [(i, (i + steps * stride) % count) for i in ran...]
    ppermute x6, starting transfers between devices: 1.15 us -> 9.97 us  [other_core(): lax.ppermute(field, 'dp', [(i, i ^ 1) for i in range(lax.axis_size('dp'))])]
    unnamed x96 -> x108, local copies, waits for them, and re-layouts: 23.9 us -> 15.9 us
  transfers between devices with their start and end apart: 43 -> 39, of which waited for: 19 -> 15; matrix products, arithmetic and copies ran while one was open for 5% -> 5% of each run, Pallas kernels for 16% -> 39%
where the time goes in v2:
time: 686 us; the launch traced here: 683 us
  Pallas kernels  294 us (43%)
  waiting for transfers between devices  244 us (36%)
  starting transfers between devices  73.8 us (11%)
  other arithmetic  34.1 us (5%)
  local copies, waits for them, and re-layouts  22 us (3%)
  between operations  15.2 us (2%)
    ppermute x27, waiting for transfers between devices, shifted(): lax.ppermute(field, axis, [(i, (i + steps * stride) % count) for i in ran...  181 us
    pallas_call x1, Pallas kernels, gather_project(): pl.pallas_call(gather_project_kernel, in_specs=[vmem] * 4, out_specs=[pl....  153 us
    ppermute x5, waiting for transfers between devices, swapped(): return lax.ppermute(field, 'tp', [(i, count - 1 - i) for i in range(count)])  61.8 us
    ppermute x27, starting transfers between devices, shifted(): lax.ppermute(field, axis, [(i, (i + steps * stride) % count) for i in ran...  58 us
    pallas_call x1, Pallas kernels, attend_back(): pl.pallas_call(functools.partial(attend_back_kernel, count), in_specs=[SC...  38.7 us
    pallas_call x1, Pallas kernels, feed_forward(): pl.pallas_call(feed_kernel, grid=(steps,), in_specs=[full, full, full, wh...  28.7 us
    pallas_call x5, Pallas kernels, gradient(): pl.pallas_call(functools.partial(gradient_kernel, pairs, ctxs), grid=(col...  24.8 us
    pallas_call x1, Pallas kernels, attend(): pl.pallas_call(functools.partial(attend_kernel, count), in_specs=[SCALARS...  20.4 us
  transfers between devices with their start and end apart: 39, of which 15 were waited for; matrix products, arithmetic and copies ran while one was open for 5% of the time, Pallas kernels for 39%

profile of v2, /device:TPU:0, one launch (start us, length us, event | category | flops | bytes accessed | tf_op | source)
XLA Modules:
  0.0 682.9 jit_solution(3723590346926503758)
XLA Ops:
  7.3 2.5 pad_maximum_fusion
  11.7 153.0 %gather_project.1 = (bf16[1536,2432]{1,0:T(8,128)(2,1)}, bf16[512,768]{1,0:T(8,128)(2,1)S(1)}, bf16[4,512,768]{2,1,0:T(8,128)(2,1)}, bf16[512,1536]{1,0:T(8,128)(2,1)S(1)}, f32[8,1536]{1,0:T(8,128)S(1)}) custom-call(bf16[96,2432]{1,0:T(8,128)(2,1)S(1)} %constant_dynamic-update-slice_fusion.shard_ref, bf16[512,1536]{1,0:T(8,128)(2,1)S(1)} %copy-done.1, ...), custom_call_target="tpu_custom_call" | custom-call | flops 2415919104 | bytes 100000000 | tf_op jit(solution)/shard_map/gather_project/pallas_call | solution.py:231
  165.3 2.7 slice.254.w_ref
  169.2 20.4 %attend.1 = (bf16[512,768]{1,0:T(8,128)(2,1)S(1)}, f32[32,96,128]{2,1,0:T(8,128)S(1)}, f32[32,128]{1,0:T(8,128)S(1)}) custom-call(s32[8,4]{1,0:T(8,128)S(1)} %copy.32.order, s32[4]{0:T(128)S(1)} %bitcast_subtract_fusion.1.starts, s32[1]{0:T(128)} %bitcast.4.place, bf16[512,768]{1,0:T(8,128)(2,1)S(1)} %get-tuple-element.47.q_ref, ...), custom_call_target="tpu_custom_call" | custom-call | flops 8000000000 | bytes 10000000 | tf_op jit(solution)/shard_map/attend/pallas_call | solution.py:362
  189.6 1.7 output_product.1.mine_ref
  194.1 34.2 %collective-permute-done.other_ref = bf16[512,1536]{1,0:T(8,128)(2,1)S(1)} collective-permute-done((bf16[512,1536]{1,0:T(8,128)(2,1)S(1)}, bf16[512,1536]{1,0:T(8,128)(2,1)S(1)}, u32[]{:S(2)}, u32[]{:S(2)}) %collective-permute-start) | collective-permute-done | bytes 1572896 | tf_op jit(solution)/shard_map/ppermute | solution.py:758
  229.4 28.7 %feed_forward.1 = (f32[512,1536]{1,0:T(8,128)}, bf16[512,1536]{1,0:T(8,128)(2,1)}, bf16[512,2048]{1,0:T(8,128)(2,1)}, bf16[512,2048]{1,0:T(8,128)(2,1)}, bf16[51...) custom-call(bf16[512,1536]{1,0:T(8,128)(2,1)} %x_ref.7, bf16[512,1536]{1,0:T(8,128)(2,1)} %copy-done.4, ...), custom_call_target="tpu_custom_call" | custom-call | flops 16106127360 | bytes 18874368 | tf_op jit(solution)/shard_map/feed_forward/pallas_call | solution.py:537
  261.3 5.8 down_product.1
  267.7 27.6 %collective-permute-done.2.other_ref = bf16[512,1536]{1,0:T(8,128)(2,1)S(1)} collective-permute-done((bf16[512,1536]{1,0:T(8,128)(2,1)}, bf16[512,1536]{1,0:T(8,128)(2,1)S(1)}, u32[]{:S(2)}, u32[]{:S(2)}) %collective-permute-start.2) | collective-permute-done | bytes 1572896 | tf_op jit(solution)/shard_map/ppermute | solution.py:758
  296.5 8.4 %middle_back.1 = (f32[512,1536]{1,0:T(8,128)}, bf16[512,1536]{1,0:T(8,128)(2,1)}, bf16[512,768]{1,0:T(8,128)(2,1)}, f32[1,1536]{1,0:T(1,128)}) custom-call(bf16[512,1536]{1,0:T(8,128)(2,1)} %a_ref.1, bf16[512,1536]{1,0:T(8,128)(2,1)} %get-tuple-element.54.mine_ref, bf16[512,1536]{1,0:T(8,128)(2,1)} %copy-done.39, f32[512,1536]{1,0:T(8,128)} %get-tuple-element.52.middle_ref, ...), custom_call_target="tpu_custom_call" | custom-call | flops 1207959552 | bytes 15000000 | tf_op jit(solution)/shard_map/middle_back/pallas_call | solution.py:599
  304.9 38.7 %attend_back.1 = (bf16[512,768]{1,0:T(8,128)(2,1)}, bf16[512,768]{1,0:T(8,128)(2,1)}, bf16[512,768]{1,0:T(8,128)(2,1)}, bf16[512,768]{1,0:T(8,128)(2,1)}, bf16[512,768]{1,0:T(8,128)(2,1)}) custom-call(s32[8,4]{1,0:T(8,128)} %copy-done.25, s32[4]{0:T(128)} %copy-done.31, s32[1]{0:T(128)} %bitcast.4.place, bf16[512,768]{1,0:T(8,128)(2,1)} %copy-done.34, ...), custom_call_target="tpu_custom_call" | custom-call | flops 16000000000 | bytes 20000000 | tf_op jit(solution)/shard_map/attend_back/pallas_call | solution.py:457
  343.6 4.8 collective-permute-start.3
  349.0 5.9 gradient.7
  356.6 2.2 collective-permute-start.23
  358.8 5.7 gradient.8
  366.3 2.6 collective-permute-start.28
  368.9 39.4 %collective-permute-done.4.refs_2_ = bf16[512,768]{1,0:T(8,128)(2,1)S(1)} collective-permute-done((bf16[512,768]{1,0:T(8,128)(2,1)}, bf16[512,768]{1,0:T(8,128)(2,1)S(1)}, u32[]{:S(2)}, u32[]{:S(2)}) %collective-permute-start.4) | collective-permute-done | bytes 786464 | tf_op jit(solution)/shard_map/ppermute | solution.py:732
  409.2 9.8 %inputs_back.1 = (bf16[512,1536]{1,0:T(8,128)(2,1)}, bf16[512,1536]{1,0:T(8,128)(2,1)}, f32[1,1536]{1,0:T(1,128)}) custom-call(bf16[512,1536]{1,0:T(8,128)(2,1)} %x_ref.7, bf16[512,768]{1,0:T(8,128)(2,1)} %get-tuple-element.59.qc_ref, f32[512,48]{1,0:T(8,128)} %copy-done.16, f32[512,48]{1,0:T(8,128)} %copy-done.15, ...), custom_call_target="tpu_custom_call" | custom-call | flops 2415919104 | bytes 15000000 | tf_op jit(solution)/shard_map/inputs_back/pallas_call | solution.py:641
  420.1 5.0 collective-permute-start.7
  425.9 7.9 %collective-permute-start.8 = (bf16[384,8]{0,1:T(8,128)(2,1)S(1)}, bf16[384,8]{0,1:T(8,128)(2,1)S(1)}, u32[]{:S(2)}, u32[]{:S(2)}) collective-permute-start(bf16[384,8]{0,1:T(8,128)(2,1)S(1)} %add_convert_fusion.6), channel_id=1, source_target_pairs={{0,16},{8,24},{16,0},{24,8},{1,17},{9,25},{17,1},{25,9},{2,18},{10... | collective-permute-start | bytes 18440 | tf_op jit(solution)/shard_map/ppermute | solution.py:732
  436.4 3.3 gradient.6
  443.2 5.7 gradient.9
  449.1 1.8 collective-permute-start.9
  450.9 3.3 add_convert_fusion.3
  455.9 4.1 gradient.5
  462.7 3.2 add_convert_fusion.2
  465.9 10.7 %collective-permute-done.19 = bf16[384,768]{1,0:T(8,128)(2,1)S(1)} collective-permute-done((bf16[384,768]{1,0:T(8,128)(2,1)S(1)}, bf16[384,768]{1,0:T(8,128)(2,1)S(1)}, u32[]{:S(2)}, u32[]{:S(2)}) %collective-permute-start.19) | collective-permute-done | bytes 589856 | tf_op jit(solution)/shard_map/ppermute | solution.py:732
  478.2 2.5 collective-permute-start.22
  480.7 3.2 add_convert_fusion.1
  486.1 3.4 add_convert_fusion
  489.5 5.3 collective-permute-done.21
  497.6 2.8 final_back.1
  502.2 12.0 %collective-permute-done.24 = bf16[384,2048]{1,0:T(8,128)(2,1)} collective-permute-done((bf16[384,2048]{1,0:T(8,128)(2,1)}, bf16[384,2048]{1,0:T(8,128)(2,1)}, u32[]{:S(2)}, u32[]{:S(2)}) %collective-permute-start.24) | collective-permute-done | bytes 1572896 | tf_op jit(solution)/shard_map/ppermute | solution.py:732
  514.3 2.9 fusion.36
  517.3 2.2 collective-permute-start.27
  520.1 27.9 %collective-permute-done.29 = bf16[384,2048]{1,0:T(8,128)(2,1)} collective-permute-done((bf16[384,2048]{1,0:T(8,128)(2,1)}, bf16[384,2048]{1,0:T(8,128)(2,1)}, u32[]{:S(2)}, u32[]{:S(2)}) %collective-permute-start.29) | collective-permute-done | bytes 1572896 | tf_op jit(solution)/shard_map/ppermute | solution.py:732
  549.2 2.9 fusion.35
  552.3 29.4 %collective-permute-done.34 = bf16[384,2048]{1,0:T(8,128)(2,1)} collective-permute-done((bf16[384,2048]{1,0:T(8,128)(2,1)}, bf16[384,2048]{1,0:T(8,128)(2,1)}, u32[]{:S(2)}, u32[]{:S(2)}) %collective-permute-start.34) | collective-permute-done | bytes 1572896 | tf_op jit(solution)/shard_map/ppermute | solution.py:732
  581.7 2.2 collective-permute-start.32
  583.9 2.9 fusion.34
  589.1 2.2 collective-permute-start.37
  592.4 5.0 collective-permute-done.32
  597.4 11.5 %collective-permute-start.36 = (bf16[96,2048]{1,0:T(8,128)(2,1)S(1)}, bf16[96,2048]{1,0:T(8,128)(2,1)S(1)}, u32[]{:S(2)}, u32[]{:S(2)}) collective-permute-start(bf16[96,2048]{1,0:T(8,128)(2,1)S(1)} %get-tuple-element.101), channel_id=1, source_target_pairs={{0,4},{2,6},{4,0},{6,2},{1,5},{3,7},{5,1},{7,3},{8,12},{10,14},{12... | collective-permute-start | bytes 1179656 | tf_op jit(solution)/shard_map/ppermute | solution.py:732
  608.9 23.3 %collective-permute-done.31 = bf16[96,2048]{1,0:T(8,128)(2,1)S(1)} collective-permute-done((bf16[96,2048]{1,0:T(8,128)(2,1)S(1)}, bf16[96,2048]{1,0:T(8,128)(2,1)S(1)}, u32[]{:S(2)}, u32[]{:S(2)}) %collective-permute-start.31) | collective-permute-done | bytes 393248 | tf_op jit(solution)/shard_map/ppermute | solution.py:732
  633.8 3.9 collective-permute-start.17
  638.3 7.0 %collective-permute-start.15 = (bf16[96,1536]{1,0:T(8,128)(2,1)S(1)}, bf16[96,1536]{1,0:T(8,128)(2,1)S(1)}, u32[]{:S(2)}, u32[]{:S(2)}) collective-permute-start(bf16[96,1536]{1,0:T(8,128)(2,1)S(1)} %get-tuple-element.108), channel_id=1, source_target_pairs={{0,2},{2,4},{4,6},{6,0},{1,3},{3,5},{5,7},{7,1},{8,10},{10,12},{12... | collective-permute-start | bytes 884744 | tf_op jit(solution)/shard_map/ppermute | solution.py:732
  645.3 20.5 %collective-permute-done.36 = bf16[96,2048]{1,0:T(8,128)(2,1)S(1)} collective-permute-done((bf16[96,2048]{1,0:T(8,128)(2,1)S(1)}, bf16[96,2048]{1,0:T(8,128)(2,1)S(1)}, u32[]{:S(2)}, u32[]{:S(2)}) %collective-permute-start.36) | collective-permute-done | bytes 393248 | tf_op jit(solution)/shard_map/ppermute | solution.py:732
  666.9 7.1 %collective-permute-done.16 = bf16[96,1536]{1,0:T(8,128)(2,1)S(1)} collective-permute-done((bf16[96,1536]{1,0:T(8,128)(2,1)S(1)}, bf16[96,1536]{1,0:T(8,128)(2,1)S(1)}, u32[]{:S(2)}, u32[]{:S(2)}) %collective-permute-start.16) | collective-permute-done | bytes 294944 | tf_op jit(solution)/shard_map/ppermute | solution.py:732
  (213 shorter events, 48.4 us)
Async XLA Ops:
  7.3 221.0 %all-gather.2.cloned.1.call-start = ((), (), s32[]{:S(2)}) async-start(), calls=%async_computation | async-start | bytes 20054016 | tf_op jit(solution)/shard_map/all_gather | solution.py:791
  9.9 159.2 %copy-start.25 = (s32[8,4]{1,0:T(8,128)}, s32[8,4]{1,0:T(8,128)S(1)}, u32[]{:S(2)}) copy-start(s32[8,4]{1,0:T(8,128)S(1)} %copy.32.order) | copy-start | bytes 388
  11.7 153.0 %copy-start.15 = (f32[512,48]{1,0:T(8,128)}, f32[512,48]{1,0:T(8,128)S(1)}, u32[]{:S(2)}) copy-start(f32[512,48]{1,0:T(8,128)S(1)} %get-tuple-element.123.sin_ref) | copy-start | bytes 294916
  11.7 153.0 %copy-start.16 = (f32[512,48]{1,0:T(8,128)}, f32[512,48]{1,0:T(8,128)S(1)}, u32[]{:S(2)}) copy-start(f32[512,48]{1,0:T(8,128)S(1)} %get-tuple-element.124.cos_ref) | copy-start | bytes 294916
  168.1 21.5 %copy-start = (bf16[1536,768]{1,0:T(8,128)(2,1)}, bf16[1536,768]{1,0:T(8,128)(2,1)S(1)}, u32[]{:S(2)}) copy-start(bf16[1536,768]{1,0:T(8,128)(2,1)S(1)} %slice.254.w_ref) | copy-start | bytes 7077892
  169.1 20.5 %copy-start.19 = (bf16[512,768]{1,0:T(8,128)(2,1)}, bf16[512,768]{1,0:T(8,128)(2,1)S(1)}, u32[]{:S(2)}) copy-start(bf16[512,768]{1,0:T(8,128)(2,1)S(1)} %get-tuple-element.95.refs_3_) | copy-start | bytes 2359300
  169.1 20.5 %copy-start.20 = (bf16[512,768]{1,0:T(8,128)(2,1)}, bf16[512,768]{1,0:T(8,128)(2,1)S(1)}, u32[]{:S(2)}) copy-start(bf16[512,768]{1,0:T(8,128)(2,1)S(1)} %get-tuple-element.96.refs_2_) | copy-start | bytes 2359300
  192.6 35.7 %collective-permute-start = (bf16[512,1536]{1,0:T(8,128)(2,1)S(1)}, bf16[512,1536]{1,0:T(8,128)(2,1)S(1)}, u32[]{:S(2)}, u32[]{:S(2)}) collective-permute-start(bf16[512,1536]{1,0:T(8,128)(2,1)S(1)} %output_product.1.mine_ref), channel_id=1, source_target_pairs={{0,1},{1,0},{2,3},{3,2},{4,5},{5,4},{6,7},{7,6},{8,9},{9,8},{10,11... | collective-permute-start | bytes 4718600 | tf_op jit(solution)/shard_map/ppermute | solution.py:758
  258.1 37.2 %collective-permute-start.2 = (bf16[512,1536]{1,0:T(8,128)(2,1)}, bf16[512,1536]{1,0:T(8,128)(2,1)S(1)}, u32[]{:S(2)}, u32[]{:S(2)}) collective-permute-start(bf16[512,1536]{1,0:T(8,128)(2,1)} %get-tuple-element.54.mine_ref), channel_id=1, source_target_pairs={{0,1},{1,0},{2,3},{3,2},{4,5},{5,4},{6,7},{7,6},{8,9},{9,8},{10,11... | collective-permute-start | bytes 4718600 | tf_op jit(solution)/shard_map/ppermute | solution.py:758
  267.2 173.7 %collective-permute-start.1 = (bf16[512,1536]{1,0:T(8,128)(2,1)S(1)}, bf16[512,1536]{1,0:T(8,128)(2,1)}, u32[]{:S(2)}, u32[]{:S(2)}) collective-permute-start(bf16[512,1536]{1,0:T(8,128)(2,1)S(1)} %down_product.1), channel_id=1, source_target_pairs={{0,1},{1,0},{2,3},{3,2},{4,5},{5,4},{6,7},{7,6},{8,9},{9,8},{10,11... | collective-permute-start | bytes 4718600 | tf_op jit(solution)/shard_map/ppermute | solution.py:758
  304.9 44.1 %copy-start.27 = (bf16[512,2048]{1,0:T(8,128)(2,1)S(1)}, bf16[512,2048]{1,0:T(8,128)(2,1)}, u32[]{:S(2)}) copy-start(bf16[512,2048]{1,0:T(8,128)(2,1)} %get-tuple-element.75.b_ref) | copy-start | bytes 6291460
  304.9 44.1 %copy-start.28 = (bf16[512,1536]{1,0:T(8,128)(2,1)S(1)}, bf16[512,1536]{1,0:T(8,128)(2,1)}, u32[]{:S(2)}) copy-start(bf16[512,1536]{1,0:T(8,128)(2,1)} %get-tuple-element.74.a_ref) | copy-start | bytes 4718596
  343.6 22.7 %collective-permute-start.3 = (bf16[512,768]{1,0:T(8,128)(2,1)}, bf16[512,768]{1,0:T(8,128)(2,1)S(1)}, u32[]{:S(2)}, u32[]{:S(2)}) collective-permute-start(bf16[512,768]{1,0:T(8,128)(2,1)} %get-tuple-element.61), channel_id=1, source_target_pairs={{0,6},{2,0},{4,2},{6,4},{1,7},{3,1},{5,3},{7,5},{8,14},{10,8},{12,... | collective-permute-start | bytes 2359304 | tf_op jit(solution)/shard_map/ppermute | solution.py:732
  348.4 59.9 %collective-permute-start.4 = (bf16[512,768]{1,0:T(8,128)(2,1)}, bf16[512,768]{1,0:T(8,128)(2,1)S(1)}, u32[]{:S(2)}, u32[]{:S(2)}) collective-permute-start(bf16[512,768]{1,0:T(8,128)(2,1)} %get-tuple-element.62), channel_id=1, source_target_pairs={{0,4},{2,6},{4,0},{6,2},{1,5},{3,7},{5,1},{7,3},{8,12},{10,14},{12... | collective-permute-start | bytes 2359304 | tf_op jit(solution)/shard_map/ppermute | solution.py:732
  348.4 59.9 %collective-permute-start.5 = (bf16[512,768]{1,0:T(8,128)(2,1)}, bf16[512,768]{1,0:T(8,128)(2,1)}, u32[]{:S(2)}, u32[]{:S(2)}) collective-permute-start(bf16[512,768]{1,0:T(8,128)(2,1)} %get-tuple-element.63), channel_id=1, source_target_pairs={{0,2},{2,4},{4,6},{6,0},{1,3},{3,5},{5,7},{7,1},{8,10},{10,12},{12... | collective-permute-start | bytes 2359304 | tf_op jit(solution)/shard_map/ppermute | solution.py:732
  356.6 106.1 %collective-permute-start.23 = (bf16[768,2048]{1,0:T(8,128)(2,1)}, bf16[768,2048]{1,0:T(8,128)(2,1)}, u32[]{:S(2)}, u32[]{:S(2)}) collective-permute-start(bf16[768,2048]{1,0:T(8,128)(2,1)} %get-tuple-element.76), channel_id=1, source_target_pairs={{0,8},{8,0},{16,24},{24,16},{1,9},{9,1},{17,25},{25,17},{2,10},{10... | collective-permute-start | bytes 9437192 | tf_op jit(solution)/shard_map/ppermute | solution.py:738
  366.3 42.0 %copy-start.41 = (bf16[512,768]{1,0:T(8,128)(2,1)}, bf16[512,768]{1,0:T(8,128)(2,1)S(1)}, u32[]{:S(2)}) copy-start(bf16[512,768]{1,0:T(8,128)(2,1)S(1)} %collective-permute-done.3.refs_1_) | copy-start | bytes 2359300
  366.3 111.9 %collective-permute-start.28 = (bf16[768,2048]{1,0:T(8,128)(2,1)}, bf16[768,2048]{1,0:T(8,128)(2,1)}, u32[]{:S(2)}, u32[]{:S(2)}) collective-permute-start(bf16[768,2048]{1,0:T(8,128)(2,1)} %get-tuple-element.79), channel_id=1, source_target_pairs={{0,8},{8,0},{16,24},{24,16},{1,9},{9,1},{17,25},{25,17},{2,10},{10... | collective-permute-start | bytes 9437192 | tf_op jit(solution)/shard_map/ppermute | solution.py:738
  420.1 5.8 collective-permute-start.7
  425.9 14.9 %collective-permute-start.8 = (bf16[384,8]{0,1:T(8,128)(2,1)S(1)}, bf16[384,8]{0,1:T(8,128)(2,1)S(1)}, u32[]{:S(2)}, u32[]{:S(2)}) collective-permute-start(bf16[384,8]{0,1:T(8,128)(2,1)S(1)} %add_convert_fusion.6), channel_id=1, source_target_pairs={{0,16},{8,24},{16,0},{24,8},{1,17},{9,25},{17,1},{25,9},{2,18},{10... | collective-permute-start | bytes 18440 | tf_op jit(solution)/shard_map/ppermute | solution.py:732
  440.7 20.1 %collective-permute-start.18 = (bf16[768,768]{1,0:T(8,128)(2,1)}, bf16[768,768]{1,0:T(8,128)(2,1)}, u32[]{:S(2)}, u32[]{:S(2)}) collective-permute-start(bf16[768,768]{1,0:T(8,128)(2,1)} %get-tuple-element.72), channel_id=1, source_target_pairs={{0,8},{8,0},{16,24},{24,16},{1,9},{9,1},{17,25},{25,17},{2,10},{10... | collective-permute-start | bytes 3538952 | tf_op jit(solution)/shard_map/ppermute | solution.py:738
  440.9 8.0 %collective-permute-start.11 = (bf16[96,8]{0,1:T(8,128)(2,1)S(1)}, bf16[96,8]{0,1:T(8,128)(2,1)S(1)}, u32[]{:S(2)}, u32[]{:S(2)}) collective-permute-start(bf16[96,8]{0,1:T(8,128)(2,1)S(1)} %get-tuple-element.119), channel_id=1, source_target_pairs={{0,6},{2,0},{4,2},{6,4},{1,7},{3,1},{5,3},{7,5},{8,14},{10,8},{12,... | collective-permute-start | bytes 4616 | tf_op jit(solution)/shard_map/ppermute | solution.py:732
  440.9 8.2 %collective-permute-start.10 = (bf16[96,8]{0,1:T(8,128)(2,1)S(1)}, bf16[96,8]{0,1:T(8,128)(2,1)S(1)}, u32[]{:S(2)}, u32[]{:S(2)}) collective-permute-start(bf16[96,8]{0,1:T(8,128)(2,1)S(1)} %get-tuple-element.120), channel_id=1, source_target_pairs={{0,4},{2,6},{4,0},{6,2},{1,5},{3,7},{5,1},{7,3},{8,12},{10,14},{12... | collective-permute-start | bytes 4616 | tf_op jit(solution)/shard_map/ppermute | solution.py:732
  448.9 35.1 %collective-permute-start.33 = (bf16[768,2048]{1,0:T(8,128)(2,1)}, bf16[768,2048]{1,0:T(8,128)(2,1)}, u32[]{:S(2)}, u32[]{:S(2)}) collective-permute-start(bf16[768,2048]{1,0:T(8,128)(2,1)} %get-tuple-element.81), channel_id=1, source_target_pairs={{0,8},{8,0},{16,24},{24,16},{1,9},{9,1},{17,25},{25,17},{2,10},{10... | collective-permute-start | bytes 9437192 | tf_op jit(solution)/shard_map/ppermute | solution.py:738
  449.1 5.4 collective-permute-start.9
  454.6 5.3 collective-permute-start.12
  460.0 37.6 %collective-permute-start.6 = (bf16[512,1536]{1,0:T(8,128)(2,1)S(1)}, bf16[512,1536]{1,0:T(8,128)(2,1)S(1)}, u32[]{:S(2)}, u32[]{:S(2)}) collective-permute-start(bf16[512,1536]{1,0:T(8,128)(2,1)S(1)} %copy-done.12), channel_id=1, source_target_pairs={{0,1},{1,0},{2,3},{3,2},{4,5},{5,4},{6,7},{7,6},{8,9},{9,8},{10,11... | collective-permute-start | bytes 4718600 | tf_op jit(solution)/shard_map/ppermute | solution.py:758
  462.0 14.6 %collective-permute-start.19 = (bf16[384,768]{1,0:T(8,128)(2,1)S(1)}, bf16[384,768]{1,0:T(8,128)(2,1)S(1)}, u32[]{:S(2)}, u32[]{:S(2)}) collective-permute-start(bf16[384,768]{1,0:T(8,128)(2,1)S(1)} %add_convert_fusion.5), channel_id=1, source_target_pairs={{0,16},{8,24},{16,0},{24,8},{1,17},{9,25},{17,1},{25,9},{2,18},{10... | collective-permute-start | bytes 1769480 | tf_op jit(solution)/shard_map/ppermute | solution.py:732
  462.7 37.8 %collective-permute-start.13 = (bf16[768,1536]{1,0:T(8,128)(2,1)S(1)}, bf16[768,1536]{1,0:T(8,128)(2,1)S(1)}, u32[]{:S(2)}, u32[]{:S(2)}) collective-permute-start(bf16[768,1536]{1,0:T(8,128)(2,1)S(1)} %get-tuple-element.69), channel_id=1, source_target_pairs={{0,8},{8,0},{16,24},{24,16},{1,9},{9,1},{17,25},{25,17},{2,10},{10... | collective-permute-start | bytes 7077896 | tf_op jit(solution)/shard_map/ppermute | solution.py:738
  476.6 37.6 %collective-permute-start.24 = (bf16[384,2048]{1,0:T(8,128)(2,1)}, bf16[384,2048]{1,0:T(8,128)(2,1)}, u32[]{:S(2)}, u32[]{:S(2)}) collective-permute-start(bf16[384,2048]{1,0:T(8,128)(2,1)} %add_convert_fusion.2), channel_id=1, source_target_pairs={{0,16},{8,24},{16,0},{24,8},{1,17},{9,25},{17,1},{25,9},{2,18},{10... | collective-permute-start | bytes 4718600 | tf_op jit(solution)/shard_map/ppermute | solution.py:732
  478.2 6.2 collective-permute-start.22
  484.0 10.8 %collective-permute-start.21 = (bf16[96,768]{1,0:T(8,128)(2,1)S(1)}, bf16[96,768]{1,0:T(8,128)(2,1)S(1)}, u32[]{:S(2)}, u32[]{:S(2)}) collective-permute-start(bf16[96,768]{1,0:T(8,128)(2,1)S(1)} %get-tuple-element.113), channel_id=1, source_target_pairs={{0,4},{2,6},{4,0},{6,2},{1,5},{3,7},{5,1},{7,3},{8,12},{10,14},{12... | collective-permute-start | bytes 442376 | tf_op jit(solution)/shard_map/ppermute | solution.py:732
  484.5 11.8 %collective-permute-start.20 = (bf16[96,768]{1,0:T(8,128)(2,1)S(1)}, bf16[96,768]{1,0:T(8,128)(2,1)S(1)}, u32[]{:S(2)}, u32[]{:S(2)}) collective-permute-start(bf16[96,768]{1,0:T(8,128)(2,1)S(1)} %get-tuple-element.111), channel_id=1, source_target_pairs={{0,2},{2,4},{4,6},{6,0},{1,3},{3,5},{5,7},{7,1},{8,10},{10,12},{12... | collective-permute-start | bytes 442376 | tf_op jit(solution)/shard_map/ppermute | solution.py:732
  494.8 53.2 %collective-permute-start.29 = (bf16[384,2048]{1,0:T(8,128)(2,1)}, bf16[384,2048]{1,0:T(8,128)(2,1)}, u32[]{:S(2)}, u32[]{:S(2)}) collective-permute-start(bf16[384,2048]{1,0:T(8,128)(2,1)} %add_convert_fusion.1), channel_id=1, source_target_pairs={{0,16},{8,24},{16,0},{24,8},{1,17},{9,25},{17,1},{25,9},{2,18},{10... | collective-permute-start | bytes 4718600 | tf_op jit(solution)/shard_map/ppermute | solution.py:732
  496.3 85.4 %collective-permute-start.34 = (bf16[384,2048]{1,0:T(8,128)(2,1)}, bf16[384,2048]{1,0:T(8,128)(2,1)}, u32[]{:S(2)}, u32[]{:S(2)}) collective-permute-start(bf16[384,2048]{1,0:T(8,128)(2,1)} %add_convert_fusion), channel_id=1, source_target_pairs={{0,16},{8,24},{16,0},{24,8},{1,17},{9,25},{17,1},{25,9},{2,18},{10... | collective-permute-start | bytes 4718600 | tf_op jit(solution)/shard_map/ppermute | solution.py:732
  500.7 132.5 %collective-permute-start.14 = (bf16[384,1536]{1,0:T(8,128)(2,1)S(1)}, bf16[384,1536]{1,0:T(8,128)(2,1)S(1)}, u32[]{:S(2)}, u32[]{:S(2)}) collective-permute-start(bf16[384,1536]{1,0:T(8,128)(2,1)S(1)} %add_convert_fusion.4), channel_id=1, source_target_pairs={{0,16},{8,24},{16,0},{24,8},{1,17},{9,25},{17,1},{25,9},{2,18},{10... | collective-permute-start | bytes 3538952 | tf_op jit(solution)/shard_map/ppermute | solution.py:732
  517.3 69.6 %collective-permute-start.27 = (bf16[96,2048]{1,0:T(8,128)(2,1)S(1)}, bf16[96,2048]{1,0:T(8,128)(2,1)S(1)}, u32[]{:S(2)}, u32[]{:S(2)}) collective-permute-start(bf16[96,2048]{1,0:T(8,128)(2,1)S(1)} %get-tuple-element.106), channel_id=1, source_target_pairs={{0,6},{2,0},{4,2},{6,4},{1,7},{3,1},{5,3},{7,5},{8,14},{10,8},{12,... | collective-permute-start | bytes 1179656 | tf_op jit(solution)/shard_map/ppermute | solution.py:732
  519.6 67.9 %collective-permute-start.26 = (bf16[96,2048]{1,0:T(8,128)(2,1)S(1)}, bf16[96,2048]{1,0:T(8,128)(2,1)S(1)}, u32[]{:S(2)}, u32[]{:S(2)}) collective-permute-start(bf16[96,2048]{1,0:T(8,128)(2,1)S(1)} %get-tuple-element.107), channel_id=1, source_target_pairs={{0,4},{2,6},{4,0},{6,2},{1,5},{3,7},{5,1},{7,3},{8,12},{10,14},{12... | collective-permute-start | bytes 1179656 | tf_op jit(solution)/shard_map/ppermute | solution.py:732
  548.0 41.2 %collective-permute-start.25 = (bf16[96,2048]{1,0:T(8,128)(2,1)S(1)}, bf16[96,2048]{1,0:T(8,128)(2,1)S(1)}, u32[]{:S(2)}, u32[]{:S(2)}) collective-permute-start(bf16[96,2048]{1,0:T(8,128)(2,1)S(1)} %get-tuple-element.105), channel_id=1, source_target_pairs={{0,2},{2,4},{4,6},{6,0},{1,3},{3,5},{5,7},{7,1},{8,10},{10,12},{12... | collective-permute-start | bytes 1179656 | tf_op jit(solution)/shard_map/ppermute | solution.py:732
  581.7 15.7 %collective-permute-start.32 = (bf16[96,2048]{1,0:T(8,128)(2,1)S(1)}, bf16[96,2048]{1,0:T(8,128)(2,1)S(1)}, u32[]{:S(2)}, u32[]{:S(2)}) collective-permute-start(bf16[96,2048]{1,0:T(8,128)(2,1)S(1)} %get-tuple-element.103), channel_id=1, source_target_pairs={{0,6},{2,0},{4,2},{6,4},{1,7},{3,1},{5,3},{7,5},{8,14},{10,8},{12,... | collective-permute-start | bytes 1179656 | tf_op jit(solution)/shard_map/ppermute | solution.py:732
  586.9 45.2 %collective-permute-start.31 = (bf16[96,2048]{1,0:T(8,128)(2,1)S(1)}, bf16[96,2048]{1,0:T(8,128)(2,1)S(1)}, u32[]{:S(2)}, u32[]{:S(2)}) collective-permute-start(bf16[96,2048]{1,0:T(8,128)(2,1)S(1)} %get-tuple-element.104), channel_id=1, source_target_pairs={{0,4},{2,6},{4,0},{6,2},{1,5},{3,7},{5,1},{7,3},{8,12},{10,14},{12... | collective-permute-start | bytes 1179656 | tf_op jit(solution)/shard_map/ppermute | solution.py:732
  587.5 44.7 %collective-permute-start.30 = (bf16[96,2048]{1,0:T(8,128)(2,1)S(1)}, bf16[96,2048]{1,0:T(8,128)(2,1)S(1)}, u32[]{:S(2)}, u32[]{:S(2)}) collective-permute-start(bf16[96,2048]{1,0:T(8,128)(2,1)S(1)} %get-tuple-element.102), channel_id=1, source_target_pairs={{0,2},{2,4},{4,6},{6,0},{1,3},{3,5},{5,7},{7,1},{8,10},{10,12},{12... | collective-permute-start | bytes 1179656 | tf_op jit(solution)/shard_map/ppermute | solution.py:732
  589.1 49.2 %collective-permute-start.37 = (bf16[96,2048]{1,0:T(8,128)(2,1)S(1)}, bf16[96,2048]{1,0:T(8,128)(2,1)S(1)}, u32[]{:S(2)}, u32[]{:S(2)}) collective-permute-start(bf16[96,2048]{1,0:T(8,128)(2,1)S(1)} %get-tuple-element.100), channel_id=1, source_target_pairs={{0,6},{2,0},{4,2},{6,4},{1,7},{3,1},{5,3},{7,5},{8,14},{10,8},{12,... | collective-permute-start | bytes 1179656 | tf_op jit(solution)/shard_map/ppermute | solution.py:732
  597.4 68.5 %collective-permute-start.36 = (bf16[96,2048]{1,0:T(8,128)(2,1)S(1)}, bf16[96,2048]{1,0:T(8,128)(2,1)S(1)}, u32[]{:S(2)}, u32[]{:S(2)}) collective-permute-start(bf16[96,2048]{1,0:T(8,128)(2,1)S(1)} %get-tuple-element.101), channel_id=1, source_target_pairs={{0,4},{2,6},{4,0},{6,2},{1,5},{3,7},{5,1},{7,3},{8,12},{10,14},{12... | collective-permute-start | bytes 1179656 | tf_op jit(solution)/shard_map/ppermute | solution.py:732
  632.1 33.7 %collective-permute-start.35 = (bf16[96,2048]{1,0:T(8,128)(2,1)S(1)}, bf16[96,2048]{1,0:T(8,128)(2,1)S(1)}, u32[]{:S(2)}, u32[]{:S(2)}) collective-permute-start(bf16[96,2048]{1,0:T(8,128)(2,1)S(1)} %get-tuple-element.99), channel_id=1, source_target_pairs={{0,2},{2,4},{4,6},{6,0},{1,3},{3,5},{5,7},{7,1},{8,10},{10,12},{12... | collective-permute-start | bytes 1179656 | tf_op jit(solution)/shard_map/ppermute | solution.py:732
  633.8 33.2 %collective-permute-start.17 = (bf16[96,1536]{1,0:T(8,128)(2,1)S(1)}, bf16[96,1536]{1,0:T(8,128)(2,1)S(1)}, u32[]{:S(2)}, u32[]{:S(2)}) collective-permute-start(bf16[96,1536]{1,0:T(8,128)(2,1)S(1)} %get-tuple-element.109), channel_id=1, source_target_pairs={{0,6},{2,0},{4,2},{6,4},{1,7},{3,1},{5,3},{7,5},{8,14},{10,8},{12,... | collective-permute-start | bytes 884744 | tf_op jit(solution)/shard_map/ppermute | solution.py:732
  637.6 36.4 %collective-permute-start.16 = (bf16[96,1536]{1,0:T(8,128)(2,1)S(1)}, bf16[96,1536]{1,0:T(8,128)(2,1)S(1)}, u32[]{:S(2)}, u32[]{:S(2)}) collective-permute-start(bf16[96,1536]{1,0:T(8,128)(2,1)S(1)} %get-tuple-element.110), channel_id=1, source_target_pairs={{0,4},{2,6},{4,0},{6,2},{1,5},{3,7},{5,1},{7,3},{8,12},{10,14},{12... | collective-permute-start | bytes 884744 | tf_op jit(solution)/shard_map/ppermute | solution.py:732
  638.3 35.7 %collective-permute-start.15 = (bf16[96,1536]{1,0:T(8,128)(2,1)S(1)}, bf16[96,1536]{1,0:T(8,128)(2,1)S(1)}, u32[]{:S(2)}, u32[]{:S(2)}) collective-permute-start(bf16[96,1536]{1,0:T(8,128)(2,1)S(1)} %get-tuple-element.108), channel_id=1, source_target_pairs={{0,2},{2,4},{4,6},{6,0},{1,3},{3,5},{5,7},{7,1},{8,10},{10,12},{12... | collective-permute-start | bytes 884744 | tf_op jit(solution)/shard_map/ppermute | solution.py:732
  (43 other events, 209.5 us)
Sparse Core Ops, SparseCore 0:
  9.9 185.7 all-gather.1

commit v3 on v2

--- a/solution.py
+++ b/solution.py
@@ -57,13 +57,12 @@
     return (jnp.cos(turn), jnp.sin(turn))
 
 
-def own_places(starts, order, ctx, count):
-    rounds = order.shape[0]
-    within = jnp.arange(rounds * BLOCK, dtype=jnp.int32)
-    owner = jnp.repeat(lax.dynamic_index_in_dim(order, ctx, 1, keepdims=False), BLOCK)
-    stream = (owner + (within // BLOCK) * count) * BLOCK + within % BLOCK
-    first = jnp.max(jnp.where(starts[None, :] <= stream[:, None], starts[None, :], 0), axis=1)
-    return stream - first
+def streams(order, ctx):
+    rounds, count = order.shape
+    owners = order[:, lax.rem(ctx - jnp.arange(count) + count, count)].T
+    blocks = owners + (jnp.arange(rounds, dtype=jnp.int32) * count)[None, :]
+    within = jnp.arange(BLOCK, dtype=jnp.int32)
+    return (blocks[:, :, None] * BLOCK + within).reshape(count, rounds * BLOCK).astype(jnp.int32)
 
 
 def turned(head, cosine, sine, sign):
@@ -467,6 +466,588 @@
     )(order, starts, place, queries, slopes, att, sums, cosine, sine, *pieces)
 
 
+SIDE = 256
+
+
+def tile_bias(qi_ref, ki_ref, k, q_tile, k_tile, ratio):
+    rows = slice(q_tile * SIDE, (q_tile + 1) * SIDE)
+    keys = ki_ref[k, k_tile * SIDE : (k_tile + 1) * SIDE, :]
+    allowed = (keys <= qi_ref[0:1, rows]) & (keys >= qi_ref[1:2, rows])
+    bias = jnp.where(allowed, 0.0, masked_score)
+    return jnp.concatenate([bias] * ratio, axis=1)
+
+
+def flat_heads(ref, q_tile, group, ratio):
+    return jnp.concatenate(
+        [
+            ref[
+                q_tile * SIDE : (q_tile + 1) * SIDE,
+                (group * ratio + h) * HEAD_SIZE : (group * ratio + h + 1) * HEAD_SIZE,
+            ]
+            for h in range(ratio)
+        ],
+        axis=0,
+    )
+
+
+def head_lanes(g, offset=0):
+    return slice(offset + g * HEAD_SIZE, offset + (g + 1) * HEAD_SIZE)
+
+
+def dense_begin(q_ref, groups, ratio, qt_ref, top_ref, total_ref, att_ref):
+    for q_tile in range(q_ref.shape[0] // SIDE):
+        for g in range(groups):
+            flat = flat_heads(q_ref, q_tile, g, ratio)
+            qt_ref[q_tile * groups + g] = flat.astype(f32).T.astype(bf16)
+    top_ref[...] = jnp.full(top_ref.shape, masked_score, f32)
+    total_ref[...] = jnp.zeros(total_ref.shape, f32)
+    att_ref[...] = jnp.zeros(att_ref.shape, f32)
+
+
+def dense_piece(k, kv_ref, qi_ref, ki_ref, groups, ratio, qt_ref, top_ref, total_ref, att_ref):
+    width = groups * HEAD_SIZE
+    for q_tile in range(qi_ref.shape[1] // SIDE):
+        for k_tile in range(q_tile, -1, -1):
+            bias = tile_bias(qi_ref, ki_ref, k, q_tile, k_tile, ratio)
+            rows = slice(k_tile * SIDE, (k_tile + 1) * SIDE)
+            for g in range(groups):
+                i = q_tile * groups + g
+                raw = dot(kv_ref[k, rows, head_lanes(g)], qt_ref[i], NN) * SCALE2 + bias
+                top = top_ref[i]
+                new_top = jnp.maximum(top, jnp.max(raw, axis=0, keepdims=True))
+                weights = jnp.exp2(raw - new_top)
+                back = jnp.exp2(top - new_top)
+                top_ref[i] = new_top
+                total_ref[i] = total_ref[i] * back + jnp.sum(weights, axis=0, keepdims=True)
+                att_ref[i] = att_ref[i] * back + dot(
+                    kv_ref[k, rows, head_lanes(g, width)], weights.astype(bf16), TN
+                )
+
+
+def dense_end(groups, ratio, top_ref, total_ref, att_ref, sum_ref, low_ref):
+    for i in range(att_ref.shape[0]):
+        q_tile, g = divmod(i, groups)
+        out = att_ref[i] * (1.0 / total_ref[i])
+        att_ref[i] = out
+        sum_ref[i] = top_ref[i] + jnp.log2(total_ref[i])
+        flat = out.T.astype(bf16)
+        for h in range(ratio):
+            low_ref[q_tile * SIDE : (q_tile + 1) * SIDE, head_lanes(g * ratio + h)] = flat[
+                h * SIDE : (h + 1) * SIDE
+            ]
+
+
+def dense_kernel(q_ref, kv_ref, qi_ref, ki_ref, low_ref, att_ref, sum_ref, qt_ref, top_ref, total_ref):
+    groups = kv_ref.shape[2] // (2 * HEAD_SIZE)
+    ratio = q_ref.shape[1] // (groups * HEAD_SIZE)
+    dense_begin(q_ref, groups, ratio, qt_ref, top_ref, total_ref, att_ref)
+
+    def piece(k, unused):
+        dense_piece(k, kv_ref, qi_ref, ki_ref, groups, ratio, qt_ref, top_ref, total_ref, att_ref)
+        return unused
+
+    lax.fori_loop(0, kv_ref.shape[0], piece, 0)
+    dense_end(groups, ratio, top_ref, total_ref, att_ref, sum_ref, low_ref)
+
+
+def dense_shapes(rows, groups, ratio):
+    tiles = rows // SIDE * groups
+    return tiles, ratio * SIDE
+
+
+def dense_attend(queries, kv, qi, ki):
+    rows = queries.shape[0]
+    groups = kv.shape[2] // (2 * HEAD_SIZE)
+    tiles, lanes = dense_shapes(rows, groups, queries.shape[1] // (groups * HEAD_SIZE))
+    vmem = pl.BlockSpec(memory_space=pltpu.VMEM)
+    return pl.pallas_call(
+        dense_kernel,
+        in_specs=[vmem] * 4,
+        out_specs=[vmem] * 3,
+        out_shape=[
+            jax.ShapeDtypeStruct(queries.shape, bf16),
+            jax.ShapeDtypeStruct((tiles, HEAD_SIZE, lanes), f32),
+            jax.ShapeDtypeStruct((tiles, 1, lanes), f32),
+        ],
+        scratch_shapes=[
+            pltpu.VMEM((tiles, HEAD_SIZE, lanes), bf16),
+            pltpu.VMEM((tiles, 1, lanes), f32),
+            pltpu.VMEM((tiles, 1, lanes), f32),
+        ],
+        compiler_params=params(40),
+        cost_estimate=cost(8e9, 1e7),
+        name="dense_attend",
+    )(queries, kv, qi, ki)
+
+
+FEED_TILES = 12
+TILES = 17
+
+
+def back_kernel(
+    part_hbm, feed_hbm, cot_hbm, middle_hbm, gain_ref, act_hbm, mid_normed_hbm, x_hbm, normed_hbm,
+    low_ref, q_ref, kv_ref, att_ref, sum_ref, qi_ref, ki_ref, cos_ref, sin_ref, weight_hbm,
+    feed_other, back_middle, part2_out, part2_other, grads_ref, held_hbm, far_hbm,
+    lhs, mid, part, part_other, w_out, w_in, rhs, q2, q2t, d2, d2t, delta, bias_ref, dq_ref,
+    kv_sent, kv_got, cot, gain_rows, gain_other, gain_columns,
+    p_send, p_keep, c_got, s_one, own, y_got, z_got,
+    load_sem, act_sem, x_send, x_recv, c_send, c_recv, c_free, held_sem, y_send, y_recv, own_sem,
+    z_send, z_recv, k_send, k_recv,
+):
+    ctxs = lax.axis_size("ctx")
+    dp, ctx, tp = lax.axis_index("dp"), lax.axis_index("ctx"), lax.axis_index("tp")
+    pair_at, core_at = dp // 2, lax.rem(dp, 2)
+    far, core = (lax.rem(dp + 2, 4), ctx, tp), (dp + 1 - 2 * core_at, ctx, tp)
+    after, before = (dp, lax.rem(ctx + 1, ctxs), tp), (dp, lax.rem(ctx + ctxs - 1, ctxs), tp)
+    across = (dp, ctx, 1 - tp)
+    rows, width = mid.shape
+    section = width // 4
+    piece = section // ctxs
+    groups = kv_ref.shape[2] // (2 * HEAD_SIZE)
+    kv_width = groups * HEAD_SIZE
+    ratio = q_ref.shape[1] // kv_width
+    q_cols = q_ref.shape[1]
+
+    barrier = pltpu.get_barrier_semaphore()
+    for device in (after, before, far, core, across):
+        pl.semaphore_signal(barrier, inc=1, device_id=device, device_id_type=MESH)
+    pl.semaphore_wait(barrier, 5)
+
+    def remote(source, target, device, sent, got):
+        return pltpu.make_async_remote_copy(source, target, sent, got, device, MESH)
+
+    def load(source, target, index):
+        return pltpu.make_async_copy(source, target, load_sem.at[index])
+
+
+    def product(t, lhs_of, rhs_of):
+        slot = lax.rem(t, 2)
+
+        @pl.when(t >= 2)
+        def _():
+            core_copy(t - 2).wait_send()
+
+        for c, out in ((1, p_send), (0, p_keep)):
+            for y in range(2):
+                there = lax.rem(pair_at + y + 1, 2) * 2 + lax.rem(core_at + c, 2)
+                start = pl.multiple_of(there * section, LANES)
+                result = rhs_of(start, lhs_of(pl.ds(start, section)))
+                for z in range(ctxs):
+                    place = lax.rem(z + 2 * ctxs - ctx - 1, ctxs)
+                    target = pl.ds(pl.multiple_of(y * section + place * piece, piece), piece)
+                    out[slot, target, :] = result[z * piece : (z + 1) * piece]
+
+        @pl.when(t >= 4)
+        def _():
+            pl.semaphore_wait(c_free, 1)
+
+        core_copy(t).start()
+
+    def core_copy(t):
+        return remote(
+            p_send.at[lax.rem(t, 2)], c_got.at[lax.rem(t, 4)], core, c_send.at[t], c_recv.at[t]
+        )
+
+    def held_copy(t):
+        return pltpu.make_async_copy(s_one.at[lax.rem(t, 2)], held_hbm.at[t], held_sem.at[t])
+
+    def meet_core(t):
+        core_copy(t).wait_recv()
+        slot, got = lax.rem(t, 2), lax.rem(t, 4)
+
+        def add(i, unused):
+            part_rows = pl.ds(pl.multiple_of(i * piece, piece), piece)
+            total = p_keep[slot, part_rows, :].astype(f32) + c_got[got, part_rows, :].astype(f32)
+            s_one[slot, part_rows, :] = total.astype(bf16)
+            return unused
+
+        lax.fori_loop(0, 2 * section // piece, add, 0)
+
+        @pl.when(t + 4 < TILES)
+        def _():
+            pl.semaphore_signal(c_free, inc=1, device_id=core, device_id_type=MESH)
+
+        held_copy(t).start()
+
+    def far_copy(t):
+        return remote(
+            held_hbm.at[t, pl.ds(0, section)], far_hbm.at[t], far, y_send.at[t], y_recv.at[t]
+        )
+
+    def send_far(t):
+        held_copy(t).wait()
+        far_copy(t).start()
+
+    def own_copy(t):
+        return pltpu.make_async_copy(
+            held_hbm.at[t, pl.ds(section, section)], own.at[lax.rem(t, 6)], own_sem.at[t, 0]
+        )
+
+    def got_copy(t):
+        return pltpu.make_async_copy(far_hbm.at[t], y_got.at[lax.rem(t, 2)], own_sem.at[t, 1])
+
+    def ring_copy(t, step):
+        return remote(
+            own.at[lax.rem(t, 6), pl.ds((ctxs - 2 - step) * piece, piece)],
+            z_got.at[t, step], after, z_send.at[t, step], z_recv.at[t, step],
+        )
+
+    def ring_add(t, step):
+        ring_copy(t, step).wait_recv()
+        ring_copy(t, step).wait_send()
+        place = ctxs - 3 - step if step < ctxs - 2 else ctxs - 1
+        target = pl.ds(place * piece, piece)
+        total = own[lax.rem(t, 6), target, :].astype(f32) + z_got[t, step].astype(f32)
+        if step < ctxs - 2:
+            own[lax.rem(t, 6), target, :] = total.astype(bf16)
+            ring_copy(t, step + 1).start()
+        else:
+            grads_ref[t] = total
+
+    def tick(n):
+        for step in range(ctxs - 2, -1, -1):
+
+            @pl.when((n - 2 - step >= 0) & (n - 2 - step < TILES))
+            def _(step=step):
+                ring_add(n - 2 - step, step)
+
+        @pl.when((n >= 1) & (n - 1 < TILES))
+        def _():
+            t = n - 1
+            own_copy(t).wait()
+            got_copy(t).wait()
+            slot, got = lax.rem(t, 6), lax.rem(t, 2)
+            for z in range(ctxs):
+                target = pl.ds(z * piece, piece)
+                total = own[slot, target, :].astype(f32) + y_got[got, target, :].astype(f32)
+                own[slot, target, :] = total.astype(bf16)
+            ring_copy(t, 0).start()
+
+        @pl.when(n < TILES)
+        def _():
+            far_copy(n).wait_recv()
+            own_copy(n).start()
+            got_copy(n).start()
+
+
+    part_copy = remote(part_hbm, part_other, across, x_send.at[0], x_recv.at[0])
+    part_copy.start()
+    feed_copy = remote(feed_hbm, feed_other, across, x_send.at[1], x_recv.at[1])
+    feed_copy.start()
+
+    def act_copy(t):
+        columns = pl.ds(pl.multiple_of(lax.rem(t, 4) * TILE, TILE), TILE)
+        return pltpu.make_async_copy(
+            act_hbm.at[t // 4, :, columns], rhs.at[lax.rem(t, 2)], act_sem.at[t]
+        )
+
+    loads = [
+        load(mid_normed_hbm, lhs.at[0], 0),
+        load(cot_hbm, lhs.at[1], 1),
+        load(part_hbm, part, 2),
+        load(middle_hbm, mid, 3),
+        load(weight_hbm.at[:, pl.ds(2 * q_cols + LANES, q_cols)], w_out, 4),
+        load(weight_hbm.at[:, pl.ds(0, 2 * q_cols)], w_in, 5),
+    ]
+    act_copy(0).start()
+    for copy in loads:
+        copy.start()
+    loads[0].wait()
+    loads[1].wait()
+
+    def plain(t):
+        def times(start, left):
+            return dot(left, rhs[lax.rem(t, 2)], TN).astype(bf16)
+
+        return times
+
+    def feed_step(t, unused):
+        act_copy(t).wait()
+
+        @pl.when(t + 1 < FEED_TILES)
+        def _():
+            act_copy(t + 1).start()
+
+        product(t, lambda lanes: lhs[t // 8, :, lanes], plain(t))
+
+        @pl.when(t >= 1)
+        def _():
+            meet_core(t - 1)
+
+        @pl.when(t >= 2)
+        def _():
+            send_far(t - 2)
+
+        @pl.when((t >= 5) & (lax.rem(t, 3) == 2))
+        def _():
+            tick((t - 5) // 3)
+
+        return unused
+
+    lax.fori_loop(0, FEED_TILES, feed_step, 0)
+    meet_core(FEED_TILES - 1)
+    send_far(FEED_TILES - 2)
+    send_far(FEED_TILES - 1)
+
+    for q_tile in range(rows // SIDE):
+        for g in range(groups):
+            flat = flat_heads(q_ref, q_tile, g, ratio)
+            q2[q_tile * groups + g] = flat
+            q2t[q_tile * groups + g] = flat.astype(f32).T.astype(bf16)
+    dq_ref[...] = jnp.zeros(dq_ref.shape, f32)
+    kv_got[0] = jnp.zeros(kv_got.shape[1:], bf16)
+    gain_rows[...] = jnp.zeros(gain_rows.shape, f32)
+
+
+    loads[2].wait()
+    loads[3].wait()
+    part_copy.wait_recv()
+    few = 64
+
+    def norm_rows(i, unused):
+        here = pl.ds(pl.multiple_of(i * few, few), few)
+        field = mid[here, :]
+        scale = lax.rsqrt(jnp.mean(field * field, axis=1, keepdims=True) + epsilon)
+        unit = field * scale
+        back = part[here, :].astype(f32) + part_other[here, :].astype(f32)
+        gain_rows[1:2, :] += jnp.sum(back * unit, axis=0, keepdims=True)
+        inner = back * gain_ref[1:2, :]
+        out = lhs[1, here, :].astype(f32) + scale * (
+            inner - unit * jnp.mean(inner * unit, axis=1, keepdims=True)
+        )
+        mid[here, :] = out
+        lhs[0, here, :] = out.astype(bf16)
+        return unused
+
+    lax.fori_loop(0, rows // few, norm_rows, 0)
+    middle_copy = load(mid, back_middle, 6)
+    middle_copy.start()
+    normed_copy = load(normed_hbm, lhs.at[1], 7)
+    normed_copy.start()
+    x_copy = load(x_hbm, part, 8)
+    x_copy.start()
+    loads[4].wait()
+    cot[:, :q_cols] = dot(lhs[0], w_out[...], NN).astype(bf16)
+    for q_tile in range(rows // SIDE):
+        for g in range(groups):
+            i = q_tile * groups + g
+            flat = flat_heads(cot, q_tile, g, ratio)
+            turned_flat = flat.astype(f32).T
+            d2[i] = flat
+            d2t[i] = turned_flat.astype(bf16)
+            delta[i] = jnp.sum(turned_flat * att_ref[i], axis=0, keepdims=True)
+    tick(jnp.int32(3))
+
+    t_out = jnp.int32(FEED_TILES)
+    product(
+        t_out, lambda lanes: lhs[0, :, lanes], lambda start, left: dot(left, low_ref[:, :TILE], TN).astype(bf16)
+    )
+
+
+    def kv_copy(s):
+        return remote(kv_sent.at[s], kv_got.at[s + 1], after, k_send.at[s], k_recv.at[s])
+
+    def back_piece(s, unused):
+        k = lax.rem(s + 1, ctxs)
+        pairs = [(q, kk) for kk in range(rows // SIDE) for q in range(kk, rows // SIDE)]
+        for index, (q_tile, k_tile) in enumerate(pairs):
+            bias_ref[index] = tile_bias(qi_ref, ki_ref, k, q_tile, k_tile, ratio)
+        sums = []
+        for k_tile in range(rows // SIDE):
+            here = slice(k_tile * SIDE, (k_tile + 1) * SIDE)
+            for g in range(groups):
+                key, value = kv_ref[k, here, head_lanes(g)], kv_ref[k, here, head_lanes(g, kv_width)]
+                d_key = d_value = None
+                for index, (q_tile, which) in enumerate(pairs):
+                    if which != k_tile:
+                        continue
+                    i = q_tile * groups + g
+                    raw = dot(key, q2t[i], NN) * SCALE2 + bias_ref[index]
+                    share = jnp.exp2(raw - sum_ref[i])
+                    back_share = dot(value, d2t[i], NN)
+                    back = (share * (back_share - delta[i])).astype(bf16)
+                    one_value = dot(share.astype(bf16), d2[i], NN)
+                    one_key = dot(back, q2[i], NN)
+                    d_value = one_value if d_value is None else d_value + one_value
+                    d_key = one_key if d_key is None else d_key + one_key
+                    dq_ref[i] += dot(key, back, TN)
+                kv_sent[s, here, head_lanes(g)] = (d_key * SCALE).astype(bf16)
+                kv_sent[s, here, head_lanes(g, kv_width)] = d_value.astype(bf16)
+
+        @pl.when(s >= 1)
+        def _():
+            kv_copy(s - 1).wait_recv()
+
+            def add(i, unused):
+                here = pl.ds(pl.multiple_of(i * few, few), few)
+                total = kv_sent[s, here, :].astype(f32) + kv_got[s, here, :].astype(f32)
+                kv_sent[s, here, :] = total.astype(bf16)
+                return unused
+
+            lax.fori_loop(0, rows // few, add, 0)
+
+        @pl.when(s < ctxs - 1)
+        def _():
+            kv_copy(s).start()
+
+        @pl.when(s == 0)
+        def _():
+            meet_core(t_out)
+            send_far(t_out)
+
+        @pl.when(s < ctxs - 1)
+        def _():
+            tick(4 + 2 * s)
+            tick(5 + 2 * s)
+
+        return unused
+
+    lax.fori_loop(0, ctxs, back_piece, 0)
+
+
+    for i in range(dq_ref.shape[0]):
+        q_tile, g = divmod(i, groups)
+        here = slice(q_tile * SIDE, (q_tile + 1) * SIDE)
+        flat = dq_ref[i].T * SCALE
+        for h in range(ratio):
+            cot[here, head_lanes(g * ratio + h)] = turned(
+                flat[h * SIDE : (h + 1) * SIDE], cos_ref[here, :], sin_ref[here, :], -1
+            ).astype(bf16)
+    for g in range(groups):
+        cot[:, head_lanes(g, q_cols)] = turned(
+            kv_sent[ctxs - 1, :, head_lanes(g)].astype(f32), cos_ref[...], sin_ref[...], -1
+        ).astype(bf16)
+    cot[:, q_cols + kv_width :] = kv_sent[ctxs - 1, :, kv_width:]
+    loads[5].wait()
+    x_copy.wait()
+    x_rows = part[...].astype(f32)
+    scale = lax.rsqrt(jnp.mean(x_rows * x_rows, axis=1, keepdims=True) + epsilon)
+    for j in range(width // TILE):
+        lanes = slice(j * TILE, (j + 1) * TILE)
+        back = dot(cot[...], w_in[lanes, :], NT)
+        part_other[:, lanes] = back.astype(bf16)
+        gain_rows[0:1, lanes] += jnp.sum(back * (part[:, lanes].astype(f32) * scale), axis=0, keepdims=True)
+    gain_copy = remote(gain_rows.at[pl.ds(0, 8)], gain_other, across, x_send.at[2], x_recv.at[2])
+    gain_copy.start()
+    part2_copy = remote(part_other, part2_other, across, x_send.at[3], x_recv.at[3])
+    part2_copy.start()
+    part2_save = load(part_other, part2_out, 9)
+    part2_save.start()
+    normed_copy.wait()
+
+    def qkv_step(j, unused):
+        t = FEED_TILES + 1 + j
+
+        def times(start, left):
+            lanes = pl.ds(pl.multiple_of(j * TILE, TILE), TILE)
+            return dot(left, cot[:, lanes], TN).astype(bf16)
+
+        product(t, lambda lanes: lhs[1, :, lanes], times)
+
+        @pl.when(j >= 1)
+        def _():
+            meet_core(t - 1)
+
+        @pl.when(j >= 2)
+        def _():
+            send_far(t - 2)
+
+        return unused
+
+    lax.fori_loop(0, 3, qkv_step, 0)
+    gain_copy.wait_recv()
+    gain_copy.wait_send()
+    gain_rows[0:1, :] += gain_other[0:1, :]
+    gain_columns[...] = gain_rows[...].T
+    last = jnp.int32(TILES - 1)
+    tail = q_cols - TILE
+
+    def times_last(start, left):
+        some = dot(left, low_ref[:, TILE:], TN)
+        gains = gain_columns[pl.ds(start, section), :]
+        spare = jnp.zeros((section, TILE - tail - LANES), f32)
+        return jnp.concatenate([some, gains, spare], axis=1).astype(bf16)
+
+    product(last, lambda lanes: lhs[0, :, lanes], times_last)
+    meet_core(last - 1)
+    send_far(last - 2)
+    meet_core(last)
+    send_far(last - 1)
+    send_far(last)
+
+    def drain(n, unused):
+        tick(n)
+        return unused
+
+    lax.fori_loop(4 + 2 * (ctxs - 1), TILES + ctxs, drain, 0)
+
+    for t in (TILES - 2, TILES - 1):
+        core_copy(jnp.int32(t)).wait_send()
+
+    def far_done(t, unused):
+        far_copy(t).wait_send()
+        return unused
+
+    lax.fori_loop(0, TILES, far_done, 0)
+    for s in range(ctxs - 1):
+        kv_copy(s).wait_send()
+    part_copy.wait_send()
+    feed_copy.wait()
+    part2_copy.wait()
+    part2_save.wait()
+    middle_copy.wait()
+
+
+def back_all(part, feed, cotangent, middle, gains, act, mid_normed, x, normed, low, queries, kv, att, sums, qi, ki, cosine, sine, weights, ctxs):
+    rows, width = x.shape
+    q_cols = queries.shape[1]
+    groups = kv.shape[2] // (2 * HEAD_SIZE)
+    ratio = q_cols // (groups * HEAD_SIZE)
+    tiles, lanes = dense_shapes(rows, groups, ratio)
+    section = width // 4
+    piece = section // ctxs
+    vmem, hbm = pl.BlockSpec(memory_space=pltpu.VMEM), pl.BlockSpec(memory_space=pl.ANY)
+    full = jax.ShapeDtypeStruct((rows, width), bf16)
+    sems = lambda *n: pltpu.SemaphoreType.DMA(n)
+    space = lambda *shape: pltpu.VMEM(shape, bf16)
+    wide = lambda *shape: pltpu.VMEM(shape, f32)
+    pairs = (rows // SIDE) * (rows // SIDE + 1) // 2
+    return pl.pallas_call(
+        back_kernel,
+        in_specs=[hbm] * 4 + [vmem] + [hbm] * 4 + [vmem] * 9 + [hbm],
+        out_specs=[hbm] * 4 + [vmem] + [hbm] * 2,
+        out_shape=[
+            full,
+            jax.ShapeDtypeStruct((rows, width), f32),
+            full,
+            full,
+            jax.ShapeDtypeStruct((TILES, piece, TILE), f32),
+            jax.ShapeDtypeStruct((TILES, 2 * section, TILE), bf16),
+            jax.ShapeDtypeStruct((TILES, section, TILE), bf16),
+        ],
+        scratch_shapes=[
+            space(2, rows, width), wide(rows, width), space(rows, width), space(rows, width),
+            space(width, q_cols), space(width, 2 * q_cols), space(2, rows, TILE),
+            space(tiles, lanes, HEAD_SIZE), space(tiles, HEAD_SIZE, lanes),
+            space(tiles, lanes, HEAD_SIZE), space(tiles, HEAD_SIZE, lanes),
+            wide(tiles, 1, lanes), wide(pairs, SIDE, lanes), wide(tiles, HEAD_SIZE, lanes),
+            space(ctxs, rows, q_cols), space(ctxs, rows, q_cols), space(rows, 2 * q_cols),
+            wide(LANES, width), wide(8, width), wide(width, LANES),
+            space(2, 2 * section, TILE), space(2, 2 * section, TILE), space(4, 2 * section, TILE),
+            space(2, 2 * section, TILE), space(6, section, TILE), space(2, section, TILE),
+            space(TILES, ctxs - 1, piece, TILE),
+            sems(10), sems(FEED_TILES), sems(4), sems(4), sems(TILES), sems(TILES),
+            pltpu.SemaphoreType.REGULAR, sems(TILES), sems(TILES), sems(TILES), sems(TILES, 2),
+            sems(TILES, ctxs - 1), sems(TILES, ctxs - 1), sems(ctxs - 1), sems(ctxs - 1),
+        ],
+        compiler_params=pltpu.CompilerParams(
+            vmem_limit_bytes=63 * MIB, collective_id=1, has_side_effects=True
+        ),
+        cost_estimate=cost(4e10, 1e8),
+        name="back_all",
+    )(part, feed, cotangent, middle, gains, act, mid_normed, x, normed, low, queries, kv, att, sums, qi, ki, cosine, sine, weights)
+
+
 def output_kernel(a_ref, w_ref, o_ref):
     o_ref[...] = dot(a_ref[...], w_ref[...], NT).astype(bf16)
 
@@ -490,7 +1071,7 @@
 
 def feed_kernel(
     x_ref, mine_ref, other_ref, gain_ref, cot_ref, gate_ref, up_ref, down_ref,
-    middle_ref, normed_ref, mixed_ref, bg_ref, bu_ref, back_ref, total_ref,
+    middle_ref, normed_ref, act_ref, back_ref, feed_ref, total_ref, feed_total,
 ):
     step = pl.program_id(0)
 
@@ -508,73 +1089,55 @@
     back_mixed = dot(cot_ref[...], down_ref[...], NN)
     sigmoid = 1.0 / (1.0 + jnp.exp(-gate))
     activated = gate * sigmoid
-    mixed_ref[...] = (activated * upward).astype(bf16)
+    mixed = (activated * upward).astype(bf16)
     back_gate = (back_mixed * upward * sigmoid * (1.0 + gate * (1.0 - sigmoid))).astype(bf16)
     back_up = (back_mixed * activated).astype(bf16)
-    bg_ref[...] = back_gate
-    bu_ref[...] = back_up
+    act_ref[0] = back_gate
+    act_ref[1] = back_up
+    act_ref[2] = mixed
     part = dot(back_gate, gate_ref[...], NT) + dot(back_up, up_ref[...], NT)
+    feed = dot(mixed, down_ref[...], NT)
 
     @pl.when(step == 0)
     def _():
         total_ref[...] = part
+        feed_total[...] = feed
 
     @pl.when(step > 0)
     def _():
         total_ref[...] += part
+        feed_total[...] += feed
 
     @pl.when(step == pl.num_programs(0) - 1)
     def _():
         back_ref[...] = total_ref[...].astype(bf16)
+        feed_ref[...] = feed_total[...].astype(bf16)
 
 
 def feed_forward(x, mine, other, gains, cotangent, weights, hidden):
     rows, width = x.shape
     steps = hidden // TILE
     tile_of = lambda which: pl.BlockSpec((width, TILE), lambda j: (0, which * steps + j))
-    rows_of = pl.BlockSpec((rows, TILE), lambda j: (0, j))
+    acts_of = pl.BlockSpec((3, rows, TILE), lambda j: (0, 0, j))
     full = whole((rows, width))
     return pl.pallas_call(
         feed_kernel,
         grid=(steps,),
         in_specs=[full, full, full, whole(gains.shape), full]
         + [tile_of(0), tile_of(1), tile_of(2)],
-        out_specs=[full, full, rows_of, rows_of, rows_of, full],
+        out_specs=[full, full, acts_of, full, full],
         out_shape=[
             jax.ShapeDtypeStruct((rows, width), f32),
             jax.ShapeDtypeStruct((rows, width), bf16),
-            jax.ShapeDtypeStruct((rows, hidden), bf16),
-            jax.ShapeDtypeStruct((rows, hidden), bf16),
-            jax.ShapeDtypeStruct((rows, hidden), bf16),
+            jax.ShapeDtypeStruct((3, rows, hidden), bf16),
+            jax.ShapeDtypeStruct((rows, width), bf16),
             jax.ShapeDtypeStruct((rows, width), bf16),
         ],
-        scratch_shapes=[pltpu.VMEM((rows, width), f32)],
+        scratch_shapes=[pltpu.VMEM((rows, width), f32)] * 2,
         compiler_params=params(56),
-        cost_estimate=cost(10 * rows * width * hidden, 6 * width * hidden),
+        cost_estimate=cost(12 * rows * width * hidden, 6 * width * hidden),
         name="feed_forward",
     )(x, mine, other, gains, cotangent, weights, weights, weights)
-
-
-def down_kernel(mixed_ref, w_ref, o_ref):
-    o_ref[...] = dot(mixed_ref[...], w_ref[...], NT).astype(bf16)
-
-
-def down_product(mixed, weights, column):
-    rows, hidden = mixed.shape
-    width = weights.shape[0]
-    return pl.pallas_call(
-        down_kernel,
-        grid=(3,),
-        in_specs=[
-            whole(mixed.shape),
-            pl.BlockSpec((width // 3, hidden), lambda j: (j, column)),
-        ],
-        out_specs=pl.BlockSpec((rows, width // 3), lambda j: (0, j)),
-        out_shape=jax.ShapeDtypeStruct((rows, width), bf16),
-        compiler_params=params(40),
-        cost_estimate=cost(2 * rows * width * hidden, 2 * width * hidden),
-        name="down_product",
-    )(mixed, weights)
 
 
 def middle_kernel(cot_ref, mine_ref, other_ref, middle_ref, gain_ref, w_ref, bm_ref, bb_ref, ba_ref, grad_ref):
@@ -791,56 +1354,77 @@
     second = lax.all_gather(
         jnp.concatenate([gate_weight, up_weight, down_weight], axis=1), ROWS, axis=0, tiled=True
     )
-    cosine, sine = angles(own_places(starts, order, ctx, ctxs))
-    if pairs == 2 and shard.shape[0] % 16 == 0:
+    stream = streams(order, ctx)
+    lows = jnp.max(jnp.where(starts[None, :] <= stream[0][:, None], starts[None, :], 0), axis=1)
+    cosine, sine = angles(stream[0] - lows)
+    if pairs == 2 and shard.shape[0] % 32 == 0:
         first, queries, kv, normed, gains = gather_project(
             shard, tokens, cosine, sine, q_cols, ctxs
         )
-        pieces = [kv[k] for k in range(ctxs)]
+        qi = jnp.pad(jnp.stack([stream[0], lows]), ((0, 6), (0, 0)))
+        attended_low, att, sums = dense_attend(queries, kv, qi, stream[:, :, None])
+        output_weights = first[:, 2 * q_cols + LANES :]
+        branch = output_product(attended_low, output_weights, 0, features)
+        middle, mid_normed, act, back_part, feed = feed_forward(
+            tokens, branch, swapped(branch), gains, cotangent, second, hidden
+        )
+        feed_other, back_middle, part, part_other, grads, _, _ = back_all(
+            back_part, feed, cotangent, middle, gains, act, mid_normed, tokens, normed,
+            attended_low, queries, kv, att, sums, qi, stream[:, :, None], cosine, sine, first, ctxs,
+        )
+        result = (middle + feed.astype(f32) + feed_other.astype(f32)).astype(bf16)
+        token_gradient = final_back(back_middle, part, part_other, tokens, gains)
+        wide = lambda *tiles: jnp.concatenate([grads[t] for t in tiles], axis=1)
+        qkv_gradient = wide(13, 14, 15)
+        output_gradient = jnp.concatenate([grads[12], grads[16][:, : q_cols - TILE]], axis=1)
+        gain_sums = grads[16][:, q_cols - TILE :]
+        gate_gradient, up_gradient = wide(0, 1, 2, 3), wide(4, 5, 6, 7)
+        down_gradient = wide(8, 9, 10, 11)
     else:
         first = lax.all_gather(shard, ROWS, axis=0, tiled=True)
         gains = first[:, 2 * q_cols : 2 * q_cols + 8].T.astype(f32)
         queries, kv, normed = project(tokens, gains, cosine, sine, first, q_cols)
         pieces = [kv] + [shifted(kv, "ctx", k) for k in range(1, ctxs)]
-    output_weights = first[:, 2 * q_cols + LANES :]
-    attended_low, att, sums = attend(order, starts, place, queries, pieces)
-    branch = output_product(attended_low, output_weights, 0, features)
-    middle, mid_normed, mixed, back_gate, back_up, back_part = feed_forward(
-        tokens, branch, swapped(branch), gains, cotangent, second, hidden
-    )
-    back_other = swapped(back_part)
-    gate_parts = gradient(mid_normed, back_gate, pairs, ctxs)
-    up_parts = gradient(mid_normed, back_up, pairs, ctxs)
-    down_parts = gradient(cotangent, mixed, pairs, ctxs)
-    feed = down_product(mixed, second, 2)
-    result = (middle + feed.astype(f32) + swapped(feed).astype(f32)).astype(bf16)
-
-    back_middle, back_branch, back_attended, mid_grad = middle_back(
-        cotangent, back_part, back_other, middle, gains, output_weights, 0, q_cols
-    )
-    output_parts = gradient(back_branch, attended_low, pairs, ctxs)
-    back = attend_back(
-        order, starts, place, queries, back_attended, att, sums, cosine, sine, pieces
-    )
-    own_parts = [back[1]] + [shifted(back[1 + k], "ctx", -k) for k in range(1, ctxs)]
-    cot, normed_part, pre_grad = inputs_back(tokens, back[0], cosine, sine, first, own_parts)
-    normed_other = swapped(normed_part)
-    qkv_parts = gradient(normed, cot, pairs, ctxs)
-    token_gradient = final_back(back_middle, normed_part, normed_other, tokens, gains)
-
-    tp = lax.axis_index("tp")
-    mid_once = jnp.where(tp == 0, mid_grad, 0.0)
-    pair = jnp.concatenate([pre_grad, mid_once], axis=0).astype(bf16)
-    pair = jnp.pad(pair, ((0, 6), (0, 0))).T
-    ordered = relative(pair, pairs, ctxs)
-    gain_sums = sum_to_owner(ordered[: features // 2], ordered[features // 2 :], pairs, ctxs)
-    gain_sums = gain_sums + swapped(gain_sums)
-
-    gate_gradient = sum_to_owner(*gate_parts, pairs, ctxs)
-    up_gradient = sum_to_owner(*up_parts, pairs, ctxs)
-    down_gradient = sum_to_owner(*down_parts, pairs, ctxs)
-    output_gradient = sum_to_owner(*output_parts, pairs, ctxs)
-    qkv_gradient = sum_to_owner(*qkv_parts, pairs, ctxs)
+        output_weights = first[:, 2 * q_cols + LANES :]
+        attended_low, att, sums = attend(order, starts, place, queries, pieces)
+        branch = output_product(attended_low, output_weights, 0, features)
+        middle, mid_normed, act, back_part, feed = feed_forward(
+            tokens, branch, swapped(branch), gains, cotangent, second, hidden
+        )
+        back_other = swapped(back_part)
+        gate_parts = gradient(mid_normed, act[0], pairs, ctxs)
+        up_parts = gradient(mid_normed, act[1], pairs, ctxs)
+        down_parts = gradient(cotangent, act[2], pairs, ctxs)
+        result = (middle + feed.astype(f32) + swapped(feed).astype(f32)).astype(bf16)
+
+        back_middle, back_branch, back_attended, mid_grad = middle_back(
+            cotangent, back_part, back_other, middle, gains, output_weights, 0, q_cols
+        )
+        output_parts = gradient(back_branch, attended_low, pairs, ctxs)
+        back = attend_back(
+            order, starts, place, queries, back_attended, att, sums, cosine, sine, pieces
+        )
+        own_parts = [back[1]] + [shifted(back[1 + k], "ctx", -k) for k in range(1, ctxs)]
+        cot, normed_part, pre_grad = inputs_back(
+            tokens, back[0], cosine, sine, first, own_parts
+        )
+        normed_other = swapped(normed_part)
+        qkv_parts = gradient(normed, cot, pairs, ctxs)
+        token_gradient = final_back(back_middle, normed_part, normed_other, tokens, gains)
+
+        mid_once = jnp.where(lax.axis_index("tp") == 0, mid_grad, 0.0)
+        pair = jnp.concatenate([pre_grad, mid_once], axis=0).astype(bf16)
+        pair = jnp.pad(pair, ((0, 6), (0, 0))).T
+        ordered = relative(pair, pairs, ctxs)
+        gain_sums = sum_to_owner(
+            ordered[: features // 2], ordered[features // 2 :], pairs, ctxs
+        )
+        gain_sums = gain_sums + swapped(gain_sums)
+        gate_gradient = sum_to_owner(*gate_parts, pairs, ctxs)
+        up_gradient = sum_to_owner(*up_parts, pairs, ctxs)
+        down_gradient = sum_to_owner(*down_parts, pairs, ctxs)
+        output_gradient = sum_to_owner(*output_parts, pairs, ctxs)
+        qkv_gradient = sum_to_owner(*qkv_parts, pairs, ctxs)
     return (
         result,
         token_gradient,

time: 686 us -> 525 us (0.77)
  waiting for transfers between devices: 244 us -> 35.8 us
  Pallas kernels: 294 us -> 448 us
  starting transfers between devices: 73.8 us -> 1.64 us
  other arithmetic: 34.1 us -> 9.39 us
  local copies, waits for them, and re-layouts: 22 us -> 12.8 us
    ppermute x33 -> x0, waiting for transfers between devices: 182 us -> none  [the longest x27 181 us: shifted(): lax.ppermute(field, axis, [(i, (i + steps * stride) % count) for i in ran...]
    pallas_call x10 -> x2, Pallas kernels: 108 us -> 254 us  [the longest x1 236 us: back_all(): pl.pallas_call(back_kernel, in_specs=[hbm] * 4 + [vmem] + [hbm] * 4 + [vm...]
    ppermute x33 -> x0, starting transfers between devices: 68 us -> none  [the longest x27 58 us: shifted(): lax.ppermute(field, axis, [(i, (i + steps * stride) % count) for i in ran...]
    ppermute x5 -> x1, waiting for transfers between devices: 61.8 us -> 35.7 us  [swapped(): return lax.ppermute(field, 'tp', [(i, count - 1 - i) for i in range(count)])]
    convert_element_type x8 -> x1, other arithmetic: 14.6 us -> 1.76 us  [body(): result = (middle + feed.astype(f32) + feed_other.astype(f32)).astype(bf16)]
    unnamed x108 -> x66, local copies, waits for them, and re-layouts: 15.9 us -> 3.77 us
    another operation x10 -> x2, other arithmetic: 11.5 us -> 0.19 us
  transfers between devices with their start and end apart: 39 -> 2, of which waited for: 15 -> 1; matrix products, arithmetic and copies ran while one was open for 5% -> 1% of each run, Pallas kernels for 39% -> 34%
where the time goes in v3:
time: 525 us; the launch traced here: 522 us
  Pallas kernels  448 us (85%)
  waiting for transfers between devices  35.8 us (7%)
  between operations  14.7 us (3%)
  local copies, waits for them, and re-layouts  12.8 us (2%)
  other arithmetic  9.39 us (2%)
    pallas_call x1, Pallas kernels, back_all(): pl.pallas_call(back_kernel, in_specs=[hbm] * 4 + [vmem] + [hbm] * 4 + [vm...  236 us
    pallas_call x1, Pallas kernels, gather_project(): pl.pallas_call(gather_project_kernel, in_specs=[vmem] * 4, out_specs=[pl....  156 us
    ppermute x1, waiting for transfers between devices, swapped(): return lax.ppermute(field, 'tp', [(i, count - 1 - i) for i in range(count)])  35.7 us
    pallas_call x1, Pallas kernels, feed_forward(): pl.pallas_call(feed_kernel, grid=(steps,), in_specs=[full, full, full, wh...  33.6 us
    pallas_call x1, Pallas kernels, dense_attend(): pl.pallas_call(dense_kernel, in_specs=[vmem] * 4, out_specs=[vmem] * 3, o...  17.7 us
  transfers between devices with their start and end apart: 2, of which 1 were waited for; matrix products, arithmetic and copies ran while one was open for 1% of the time, Pallas kernels for 34%

profile of v3, /device:TPU:0, one launch (start us, length us, event | category | flops | bytes accessed | tf_op | source)
XLA Modules:
  0.0 522.1 jit_solution(10588126417844154395)
XLA Ops:
  7.2 0.0 copy-start
  7.2 0.0 all-gather.2.cloned.1.call-start
  7.3 2.3 pad_maximum_fusion
  9.6 0.0 all-gather.2.cloned.1.call-update
  9.6 0.0 copy-start.3
  9.7 0.6 gather_fusion
  10.3 0.1 iota_add_fusion
  10.4 0.1 squeeze.67
  10.4 0.1 slice.87
  10.5 0.1 add.78
  10.6 0.2 reduce-window_clone.1
  10.8 0.1 select_reduce_fusion
  10.9 0.0 copy-start.14
  10.9 0.1 copy.31
  11.1 0.1 add.73
  11.1 2.0 add.84
  13.3 1.0 multiply_sine_fusion
  14.3 0.0 copy-start.11
  14.3 155.8 %gather_project.1 = (bf16[1536,2432]{1,0:T(8,128)(2,1)}, bf16[512,768]{1,0:T(8,128)(2,1)S(1)}, bf16[4,512,768]{2,1,0:T(8,128)(2,1)}, bf16[512,1536]{1,0:T(8,128)(2,1)S(1)}, f32[8,1536]{1,0:T(8,128)S(1)}) custom-call(bf16[96,2432]{1,0:T(8,128)(2,1)S(1)} %constant_dynamic-update-slice_fusion.shard_ref, bf16[512,1536]{1,0:T(8,128)(2,1)S(1)} %copy-done.3, ...), custom_call_target="tpu_custom_call" | custom-call | flops 2415919104 | bytes 100000000 | tf_op jit(solution)/shard_map/gather_project/pallas_call | solution.py:230
  170.2 0.0 copy-start.12
  170.2 0.6 copy-done.12
  170.8 2.7 slice.88.w_ref
  173.6 0.1 copy-done.20
  173.6 0.1 broadcast_add_fusion.ki_ref
  173.8 0.9 copy-done.15
  174.7 17.7 %dense_attend.1 = (bf16[512,768]{1,0:T(8,128)(2,1)S(1)}, f32[8,96,512]{2,1,0:T(8,128)S(1)}, f32[8,1,512]{2,1,0:T(1,128)S(1)}) custom-call(bf16[512,768]{1,0:T(8,128)(2,1)S(1)} %get-tuple-element.29.q_ref, bf16[4,512,768]{2,1,0:T(8,128)(2,1)S(1)} %copy-done.15, s32[8,512]{1,0:T(8,128)S(1)} %pad.9.qi_ref, s32[4,512,1]{2,1,0:T(8,128)S(1)} %broadcast_add_fusion.ki_ref), custom_call_target="tpu_custom_call" | custom-call | flops 8000000000 | bytes 10000000 | tf_op jit(solution)/shard_map/dense_attend/pallas_call | solution.py:563
  192.4 0.0 copy-start.9
  192.5 0.0 copy-start.19
  192.5 1.7 output_product.1.mine_ref
  194.2 0.0 copy-start.7
  194.3 1.6 collective-permute-start
  195.9 35.7 %collective-permute-done.other_ref = bf16[512,1536]{1,0:T(8,128)(2,1)} collective-permute-done((bf16[512,1536]{1,0:T(8,128)(2,1)S(1)}, bf16[512,1536]{1,0:T(8,128)(2,1)}, u32[]{:S(2)}, u32[]{:S(2)}) %collective-permute-start) | collective-permute-done | bytes 1572896 | tf_op jit(solution)/shard_map/ppermute | solution.py:1321
  231.6 33.6 %feed_forward.1 = (f32[512,1536]{1,0:T(8,128)}, bf16[512,1536]{1,0:T(8,128)(2,1)}, bf16[3,512,2048]{2,1,0:T(8,128)(2,1)}, bf16[512,1536]{1,0:T(8,128)(2,1)}, bf16[512,1536]{1,0:T(8,128)(2,1)}) custom-call(bf16[512,1536]{1,0:T(8,128)(2,1)} %x_ref.5, bf16[512,1536]{1,0:T(8,128)(2,1)} %copy-done.7, bf16[512,1536]{1,0:T(8,128)(2,1)} %collective-permute-done.other_ref, ...), custom_call_target="tpu_custom_call" | custom-call | flops 19327352832 | bytes 18874368 | tf_op jit(solution)/shard_map/feed_forward/pallas_call | solution.py:1123
  265.2 236.2 %back_all.1 = (bf16[512,1536]{1,0:T(8,128)(2,1)}, f32[512,1536]{1,0:T(8,128)}, bf16[512,1536]{1,0:T(8,128)(2,1)}, bf16[512,1536]{1,0:T(8,128)(2,1)}, f32[17,96,5...) custom-call(bf16[512,1536]{1,0:T(8,128)(2,1)} %get-tuple-element.36.part_hbm, ...), custom_call_target="tpu_custom_call" | custom-call | flops 40000000000 | bytes 100000000 | tf_op jit(solution)/shard_map/back_all/pallas_call | solution.py:1015
  501.4 2.6 slice_bitcast_fusion.3
  504.0 0.7 slice_reduce_fusion
  504.8 0.1 copy-done.22
  504.8 0.5 copy-done.23
  505.3 0.0 copy-start.13
  505.3 1.8 add_convert_fusion
  507.1 0.7 fusion.2
  507.8 0.5 copy-done.4
  508.4 0.5 copy-done.5
  508.8 0.5 copy-done.6
  509.3 2.8 final_back.1
  512.1 0.9 pad_maximum_fusion.4
  512.9 0.9 pad_maximum_fusion.3
  513.9 1.3 pad_maximum_fusion.1
  (64 shorter events, 0.3 us)
Async XLA Ops:
  7.2 2.5 copy-start
  7.2 3.4 copy-start.28
  7.2 3.7 copy-start.29
  7.2 3.7 copy-start.30
  7.2 224.4 %all-gather.2.cloned.1.call-start = ((), (), s32[]{:S(2)}) async-start(), calls=%async_computation | async-start | bytes 20054016 | tf_op jit(solution)/shard_map/all_gather | solution.py:1354
  9.6 3.5 copy-start.24
  9.6 3.6 copy-start.26
  9.6 3.6 copy-start.27
  9.6 3.6 copy-start.25
  9.6 4.7 copy-start.3
  10.9 162.9 %copy-start.14 = (s32[8,512]{1,0:T(8,128)}, s32[8,512]{1,0:T(8,128)S(1)}, u32[]{:S(2)}) copy-start(s32[8,512]{1,0:T(8,128)S(1)} %pad.9.qi_ref) | copy-start | bytes 49156
  14.3 155.9 %copy-start.10 = (f32[512,48]{1,0:T(8,128)}, f32[512,48]{1,0:T(8,128)S(1)}, u32[]{:S(2)}) copy-start(f32[512,48]{1,0:T(8,128)S(1)} %get-tuple-element.68.sin_ref) | copy-start | bytes 294916
  14.3 155.9 %copy-start.11 = (f32[512,48]{1,0:T(8,128)}, f32[512,48]{1,0:T(8,128)S(1)}, u32[]{:S(2)}) copy-start(f32[512,48]{1,0:T(8,128)S(1)} %get-tuple-element.69.cos_ref) | copy-start | bytes 294916
  170.2 0.6 copy-start.12
  170.8 2.8 copy-start.16
  170.8 3.0 copy-start.17
  170.8 2.8 copy-start.20
  170.8 3.9 copy-start.15
  173.8 18.6 %copy-start.8 = (s32[4,512,1]{2,1,0:T(8,128)}, s32[4,512,1]{2,1,0:T(8,128)S(1)}, u32[]{:S(2)}) copy-start(s32[4,512,1]{2,1,0:T(8,128)S(1)} %broadcast_add_fusion.ki_ref) | copy-start | bytes 24580
  192.4 1.8 copy-start.9
  192.4 1.8 copy-start.18
  192.5 1.8 copy-start.19
  194.2 37.4 %copy-start.7 = (bf16[512,1536]{1,0:T(8,128)(2,1)}, bf16[512,1536]{1,0:T(8,128)(2,1)S(1)}, u32[]{:S(2)}) copy-start(bf16[512,1536]{1,0:T(8,128)(2,1)S(1)} %output_product.1.mine_ref) | copy-start | bytes 4718596
  194.3 37.3 %collective-permute-start = (bf16[512,1536]{1,0:T(8,128)(2,1)S(1)}, bf16[512,1536]{1,0:T(8,128)(2,1)}, u32[]{:S(2)}, u32[]{:S(2)}) collective-permute-start(bf16[512,1536]{1,0:T(8,128)(2,1)S(1)} %output_product.1.mine_ref), channel_id=1, source_target_pairs={{0,1},{1,0},{2,3},{3,2},{4,5},{5,4},{6,7},{7,6},{8,9},{9,8},{10,11... | collective-permute-start | bytes 4718600 | tf_op jit(solution)/shard_map/ppermute | solution.py:1321
  501.4 3.4 copy-start.21
  501.4 3.5 copy-start.22
  501.4 3.9 copy-start.23
  505.3 2.5 copy-start.2
  505.3 3.0 copy-start.4
  505.3 3.5 copy-start.5
  505.3 4.0 copy-start.6
  505.3 4.0 copy-start.13
  513.8 1.3 copy-start.1
Sparse Core Ops, SparseCore 0:
  10.2 188.1 all-gather.1

commit v4 on v3

--- a/solution.py
+++ b/solution.py
@@ -135,60 +135,110 @@
 MESH = pl.DeviceIdType.MESH
 
 
-def gather_project_kernel(
-    shard_ref, x_ref, cos_ref, sin_ref,
-    full_ref, q_ref, kv_ref, normed_ref, gain_ref,
-    w_ref, z_send, z_recv, y_send, y_recv, c_send, c_recv, k_send, k_recv, local,
+def forward_kernel(
+    shard_ref, gate_shard, up_shard, down_shard, x_ref, cos_ref, sin_ref, qi_ref, ki_ref,
+    full_ref, gate_ref, up_ref, down_ref, q_ref, kv_ref, normed_ref, gain_ref, low_ref, att_ref, sum_ref,
+    branch_ref, other_ref,
+    w_ref, qt_ref, top_ref, total_ref,
+    z_send, z_recv, y_send, y_recv, c_send, c_recv, k_send, k_recv, x_send, x_recv, local,
 ):
     ctxs = lax.axis_size("ctx")
     dp, ctx, tp = lax.axis_index("dp"), lax.axis_index("ctx"), lax.axis_index("tp")
     far, core = (lax.rem(dp + 2, 4), ctx, tp), (dp + 1 - 2 * lax.rem(dp, 2), ctx, tp)
     after, before = (dp, lax.rem(ctx + 1, ctxs), tp), (dp, lax.rem(ctx + ctxs - 1, ctxs), tp)
+    across = (dp, ctx, 1 - tp)
     barrier = pltpu.get_barrier_semaphore()
-    for device in (after, before, far, core):
+    for device in (after, before, far, core, across):
         pl.semaphore_signal(barrier, inc=1, device_id=device, device_id_type=MESH)
-    pl.semaphore_wait(barrier, 4)
+    pl.semaphore_wait(barrier, 5)
     piece = shard_ref.shape[0]
-
-    def block(pair, steps):
+    shards = (shard_ref, gate_shard, up_shard, down_shard)
+    wholes = (w_ref, gate_ref, up_ref, down_ref)
+    last = ctxs - 1
+
+
+    def place(group, pair, steps):
         owner = pair * ctxs + lax.rem(ctx - steps + ctxs, ctxs)
-        return w_ref.at[pl.ds(pl.multiple_of(owner * piece, piece), piece)]
-
-    def send(source, target, device, sent, got):
-        copy = pltpu.make_async_remote_copy(source, target, sent, got, device, MESH)
-        copy.start()
-        return copy
-
-    copies, y_copies, c_copies, z_copies = [], [], [], []
-    for s in range(ctxs):
-        place = block(dp, s)
-        source = place if s else shard_ref
-        if s:
-            z_copies[s - 1].wait_recv()
-        if s < ctxs - 1:
-            z_copies.append(send(source, place, after, z_send.at[s], z_recv.at[s]))
-        y_copies.append(send(source, place, far, y_send.at[s], y_recv.at[s]))
-        c_copies.append(send(source, place, core, c_send.at[s], c_recv.at[s]))
-        if s == 0:
-            own = pltpu.make_async_copy(shard_ref, place, local.at[0])
-            own.start()
-            x = x_ref[...].astype(f32)
-            unit = x * lax.rsqrt(jnp.mean(x * x, axis=1, keepdims=True) + epsilon)
-    for s in range(ctxs):
-        y_copies[s].wait_recv()
-        place = block(far[0], s)
-        c_copies.append(send(place, place, core, c_send.at[ctxs + s], c_recv.at[ctxs + s]))
-    own.wait()
-    for copy in c_copies:
-        copy.wait_recv()
-    full = pltpu.make_async_copy(w_ref, full_ref, local.at[1])
+        return wholes[group].at[pl.ds(pl.multiple_of(owner * piece, piece), piece)]
+
+    def source(group, steps):
+        return place(group, dp, steps) if steps else shards[group]
+
+    def remote(source, target, device, sent, got):
+        return pltpu.make_async_remote_copy(source, target, device_id=device, device_id_type=MESH, send_sem=sent, recv_sem=got)
+
+    def ring(group, s):
+        return remote(
+            source(group, s), place(group, dp, s), after, z_send.at[group, s], z_recv.at[group, s]
+        )
+
+    def over(group, s):
+        return remote(
+            source(group, s), place(group, dp, s), far, y_send.at[group, s], y_recv.at[group, s]
+        )
+
+    def aside(group, s):
+        return remote(
+            source(group, s), place(group, dp, s), core, c_send.at[group, s], c_recv.at[group, s]
+        )
+
+    def aside_far(group, s):
+        there = place(group, far[0], s)
+        return remote(
+            there, there, core, c_send.at[group, ctxs + s], c_recv.at[group, ctxs + s]
+        )
+
+    def own_copy(group):
+        return pltpu.make_async_copy(shards[group], place(group, dp, 0), local.at[group])
+
+    def begin(group):
+        over(group, 0).start()
+        aside(group, 0).start()
+        own_copy(group).start()
+
+    def along(group, s):
+        ring(group, s - 1).wait_recv()
+        if s < last:
+            ring(group, s).start()
+        over(group, s).start()
+        aside(group, s).start()
+
+    def came_over(group, s):
+        over(group, s).wait_recv()
+        aside_far(group, s).start()
+
+    def gathered(group):
+        own_copy(group).wait()
+        for s in range(ctxs):
+            aside(group, s).wait_recv()
+            aside_far(group, s).wait_recv()
+
+    first, gate, up, down = range(4)
+    ring(first, 0).start()
+    begin(first)
+    x = x_ref[...].astype(f32)
+    unit = x * lax.rsqrt(jnp.mean(x * x, axis=1, keepdims=True) + epsilon)
+    for s in range(1, ctxs):
+        along(first, s)
+        came_over(first, s - 1)
+    ring(gate, 0).start()
+    begin(gate)
+    came_over(first, last)
+    gathered(first)
+    full = pltpu.make_async_copy(w_ref, full_ref, local.at[4])
     full.start()
+    along(gate, 1)
 
     q_cols = q_ref.shape[1]
     tile = q_cols // 2
+    groups = kv_ref.shape[2] // (2 * HEAD_SIZE)
+    ratio = q_cols // (groups * HEAD_SIZE)
     gains = w_ref[:, 2 * q_cols : 2 * q_cols + LANES].astype(f32).T[:8]
     gain_ref[...] = gains
     normed_ref[...] = (unit * gains[0:1]).astype(bf16)
+
+    def product(step):
+        return dot(normed_ref[...], w_ref[:, step * tile : (step + 1) * tile], NN)
 
     def rotated(out, store):
         for h in range(tile // HEAD_SIZE):
@@ -198,58 +248,124 @@
     def key_store(lanes, value):
         kv_ref[0, :, lanes] = value
 
-    def product(step):
-        return dot(normed_ref[...], w_ref[:, step * tile : (step + 1) * tile], NN)
-
     rotated(product(2), key_store)
     kv_ref[0, :, tile:] = product(3).astype(bf16)
-    k_copies = [send(kv_ref.at[0], kv_ref.at[1], after, k_send.at[0], k_recv.at[0])]
-
+
+    def kv_copy(s):
+        return remote(kv_ref.at[s], kv_ref.at[s + 1], after, k_send.at[s], k_recv.at[s])
+
+    kv_copy(0).start()
+    begin(up)
     for step in range(2):
 
         def query_store(lanes, value):
             q_ref[:, step * tile + lanes.start : step * tile + lanes.stop] = value
 
         rotated(product(step), query_store)
-    for s in range(1, ctxs):
-        k_copies[s - 1].wait_recv()
-        if s < ctxs - 1:
-            k_copies.append(
-                send(kv_ref.at[s], kv_ref.at[s + 1], after, k_send.at[s], k_recv.at[s])
-            )
-    for copy in z_copies + y_copies + c_copies + k_copies:
-        copy.wait_send()
+
+    def attention(k):
+        dense_piece(k, kv_ref, qi_ref, ki_ref, groups, ratio, qt_ref, top_ref, total_ref, att_ref)
+
+    dense_begin(q_ref, groups, ratio, qt_ref, top_ref, total_ref, att_ref)
+    waits = [
+        [lambda: along(gate, 2), lambda: came_over(gate, 0), lambda: came_over(gate, 1)],
+        [lambda: ring(up, 0).start(), lambda: begin(down), lambda: along(gate, last), lambda: came_over(up, 0)],
+        [],
+    ]
+
+    def attention_step(k, unused):
+        for s in range(1, ctxs):
+
+            @pl.when(k == s)
+            def _(s=s):
+                kv_copy(s - 1).wait_recv()
+                if s < last:
+                    kv_copy(s).start()
+                for step in waits[s - 1] if s - 1 < len(waits) else []:
+                    step()
+
+        attention(k)
+        return unused
+
+    lax.fori_loop(0, ctxs, attention_step, 0)
+    ring(down, 0).start()
+    along(up, 1)
+    dense_end(groups, ratio, top_ref, total_ref, att_ref, sum_ref, low_ref)
+    branch_ref[...] = dot(low_ref[...], w_ref[:, 2 * q_cols + LANES :], NT).astype(bf16)
+    exchange = remote(branch_ref, other_ref, across, x_send.at[0], x_recv.at[0])
+    exchange.start()
+
+    for s in range(2, ctxs):
+        along(up, s)
+        came_over(gate, s)
+        along(down, s - 1)
+        came_over(up, s - 1)
+        came_over(down, s - 2)
+    along(down, last)
+    came_over(up, last)
+    came_over(down, last - 1)
+    came_over(down, last)
+    for group in (gate, up, down):
+        gathered(group)
+    for group in range(4):
+        for s in range(ctxs):
+            if s < last:
+                ring(group, s).wait_send()
+            over(group, s).wait_send()
+            aside(group, s).wait_send()
+            aside_far(group, s).wait_send()
+    for s in range(last):
+        kv_copy(s).wait_send()
+    exchange.wait()
     full.wait()
 
 
-def gather_project(shard, x, cosine, sine, q_cols, ctxs):
+def forward_all(shard, gate, up, down, x, cosine, sine, qi, ki, q_cols, ctxs):
     rows, width = x.shape
-    columns = shard.shape[1]
-    vmem = pl.BlockSpec(memory_space=pltpu.VMEM)
-    sems = lambda n: pltpu.SemaphoreType.DMA((n,))
+    columns, hidden = shard.shape[1], gate.shape[1]
+    groups = q_cols // 2 // HEAD_SIZE
+    tiles, lanes = dense_shapes(rows, groups, 2)
+    vmem, hbm = pl.BlockSpec(memory_space=pltpu.VMEM), pl.BlockSpec(memory_space=pl.ANY)
+    sems = lambda *n: pltpu.SemaphoreType.DMA(n)
+    shape = jax.ShapeDtypeStruct
+    full = shape((rows, width), bf16)
     return pl.pallas_call(
-        gather_project_kernel,
-        in_specs=[vmem] * 4,
-        out_specs=[pl.BlockSpec(memory_space=pl.ANY)] + [vmem] * 4,
+        forward_kernel,
+        in_specs=[vmem] + [hbm] * 3 + [vmem] * 5,
+        out_specs=[hbm] * 4 + [vmem] * 9,
         out_shape=[
-            jax.ShapeDtypeStruct((width, columns), bf16),
-            jax.ShapeDtypeStruct((rows, q_cols), bf16),
-            jax.ShapeDtypeStruct((ctxs, rows, q_cols), bf16),
-            jax.ShapeDtypeStruct((rows, width), bf16),
-            jax.ShapeDtypeStruct((8, width), f32),
+            shape((width, columns), bf16),
+            shape((width, hidden), bf16),
+            shape((width, hidden), bf16),
+            shape((width, hidden), bf16),
+            shape((rows, q_cols), bf16),
+            shape((ctxs, rows, q_cols), bf16),
+            full,
+            shape((8, width), f32),
+            shape((rows, q_cols), bf16),
+            shape((tiles, HEAD_SIZE, lanes), f32),
+            shape((tiles, 1, lanes), f32),
+            full,
+            full,
         ],
-        scratch_shapes=[pltpu.VMEM((width, columns), bf16)]
+        scratch_shapes=[
+            pltpu.VMEM((width, columns), bf16),
+            pltpu.VMEM((tiles, HEAD_SIZE, lanes), bf16),
+            pltpu.VMEM((tiles, 1, lanes), f32),
+            pltpu.VMEM((tiles, 1, lanes), f32),
+        ]
+        + [sems(4, ctxs - 1)] * 2
+        + [sems(4, ctxs)] * 2
+        + [sems(4, 2 * ctxs)] * 2
         + [sems(ctxs - 1)] * 2
-        + [sems(ctxs)] * 2
-        + [sems(2 * ctxs)] * 2
-        + [sems(ctxs - 1)] * 2
-        + [sems(2)],
+        + [sems(1)] * 2
+        + [sems(5)],
         compiler_params=pltpu.CompilerParams(
-            vmem_limit_bytes=48 * MIB, collective_id=0, has_side_effects=True
+            vmem_limit_bytes=56 * MIB, collective_id=0, has_side_effects=True
         ),
-        cost_estimate=cost(2 * rows * width * 2 * q_cols, 1e8),
-        name="gather_project",
-    )(shard, x, cosine, sine)
+        cost_estimate=cost(1e10, 1e8),
+        name="forward_all",
+    )(shard, gate, up, down, x, cosine, sine, qi, ki)
 
 
 def gather_stream(order, ctx, pieces, k_ref, v_ref):
@@ -537,51 +653,14 @@
             ]
 
 
-def dense_kernel(q_ref, kv_ref, qi_ref, ki_ref, low_ref, att_ref, sum_ref, qt_ref, top_ref, total_ref):
-    groups = kv_ref.shape[2] // (2 * HEAD_SIZE)
-    ratio = q_ref.shape[1] // (groups * HEAD_SIZE)
-    dense_begin(q_ref, groups, ratio, qt_ref, top_ref, total_ref, att_ref)
-
-    def piece(k, unused):
-        dense_piece(k, kv_ref, qi_ref, ki_ref, groups, ratio, qt_ref, top_ref, total_ref, att_ref)
-        return unused
-
-    lax.fori_loop(0, kv_ref.shape[0], piece, 0)
-    dense_end(groups, ratio, top_ref, total_ref, att_ref, sum_ref, low_ref)
-
-
 def dense_shapes(rows, groups, ratio):
     tiles = rows // SIDE * groups
     return tiles, ratio * SIDE
 
 
-def dense_attend(queries, kv, qi, ki):
-    rows = queries.shape[0]
-    groups = kv.shape[2] // (2 * HEAD_SIZE)
-    tiles, lanes = dense_shapes(rows, groups, queries.shape[1] // (groups * HEAD_SIZE))
-    vmem = pl.BlockSpec(memory_space=pltpu.VMEM)
-    return pl.pallas_call(
-        dense_kernel,
-        in_specs=[vmem] * 4,
-        out_specs=[vmem] * 3,
-        out_shape=[
-            jax.ShapeDtypeStruct(queries.shape, bf16),
-            jax.ShapeDtypeStruct((tiles, HEAD_SIZE, lanes), f32),
-            jax.ShapeDtypeStruct((tiles, 1, lanes), f32),
-        ],
-        scratch_shapes=[
-            pltpu.VMEM((tiles, HEAD_SIZE, lanes), bf16),
-            pltpu.VMEM((tiles, 1, lanes), f32),
-            pltpu.VMEM((tiles, 1, lanes), f32),
-        ],
-        compiler_params=params(40),
-        cost_estimate=cost(8e9, 1e7),
-        name="dense_attend",
-    )(queries, kv, qi, ki)
-
-
 FEED_TILES = 12
 TILES = 17
+SLOTS = 8
 
 
 def back_kernel(
@@ -680,7 +759,7 @@
 
     def own_copy(t):
         return pltpu.make_async_copy(
-            held_hbm.at[t, pl.ds(section, section)], own.at[lax.rem(t, 6)], own_sem.at[t, 0]
+            held_hbm.at[t, pl.ds(section, section)], own.at[lax.rem(t, SLOTS)], own_sem.at[t, 0]
         )
 
     def got_copy(t):
@@ -688,7 +767,7 @@
 
     def ring_copy(t, step):
         return remote(
-            own.at[lax.rem(t, 6), pl.ds((ctxs - 2 - step) * piece, piece)],
+            own.at[lax.rem(t, SLOTS), pl.ds((ctxs - 2 - step) * piece, piece)],
             z_got.at[t, step], after, z_send.at[t, step], z_recv.at[t, step],
         )
 
@@ -697,9 +776,9 @@
         ring_copy(t, step).wait_send()
         place = ctxs - 3 - step if step < ctxs - 2 else ctxs - 1
         target = pl.ds(place * piece, piece)
-        total = own[lax.rem(t, 6), target, :].astype(f32) + z_got[t, step].astype(f32)
+        total = own[lax.rem(t, SLOTS), target, :].astype(f32) + z_got[t, step].astype(f32)
         if step < ctxs - 2:
-            own[lax.rem(t, 6), target, :] = total.astype(bf16)
+            own[lax.rem(t, SLOTS), target, :] = total.astype(bf16)
             ring_copy(t, step + 1).start()
         else:
             grads_ref[t] = total
@@ -707,16 +786,18 @@
     def tick(n):
         for step in range(ctxs - 2, -1, -1):
 
-            @pl.when((n - 2 - step >= 0) & (n - 2 - step < TILES))
-            def _(step=step):
-                ring_add(n - 2 - step, step)
+            t = n - 3 - 2 * step
+
+            @pl.when((t >= 0) & (t < TILES))
+            def _(t=t, step=step):
+                ring_add(t, step)
 
         @pl.when((n >= 1) & (n - 1 < TILES))
         def _():
             t = n - 1
             own_copy(t).wait()
             got_copy(t).wait()
-            slot, got = lax.rem(t, 6), lax.rem(t, 2)
+            slot, got = lax.rem(t, SLOTS), lax.rem(t, 2)
             for z in range(ctxs):
                 target = pl.ds(z * piece, piece)
                 total = own[slot, target, :].astype(f32) + y_got[got, target, :].astype(f32)
@@ -897,11 +978,11 @@
 
         @pl.when(s < ctxs - 1)
         def _():
-            tick(4 + 2 * s)
-            tick(5 + 2 * s)
+            tick(5 + s)
 
         return unused
 
+    tick(jnp.int32(4))
     lax.fori_loop(0, ctxs, back_piece, 0)
 
 
@@ -952,6 +1033,7 @@
         def _():
             send_far(t - 2)
 
+        tick(4 + ctxs + j)
         return unused
 
     lax.fori_loop(0, 3, qkv_step, 0)
@@ -979,7 +1061,7 @@
         tick(n)
         return unused
 
-    lax.fori_loop(4 + 2 * (ctxs - 1), TILES + ctxs, drain, 0)
+    lax.fori_loop(7 + ctxs, TILES + 2 * ctxs - 1, drain, 0)
 
     for t in (TILES - 2, TILES - 1):
         core_copy(jnp.int32(t)).wait_send()
@@ -1034,7 +1116,7 @@
             space(ctxs, rows, q_cols), space(ctxs, rows, q_cols), space(rows, 2 * q_cols),
             wide(LANES, width), wide(8, width), wide(width, LANES),
             space(2, 2 * section, TILE), space(2, 2 * section, TILE), space(4, 2 * section, TILE),
-            space(2, 2 * section, TILE), space(6, section, TILE), space(2, section, TILE),
+            space(2, 2 * section, TILE), space(SLOTS, section, TILE), space(2, section, TILE),
             space(TILES, ctxs - 1, piece, TILE),
             sems(10), sems(FEED_TILES), sems(4), sems(4), sems(TILES), sems(TILES),
             pltpu.SemaphoreType.REGULAR, sems(TILES), sems(TILES), sems(TILES), sems(TILES, 2),
@@ -1114,17 +1196,18 @@
         feed_ref[...] = feed_total[...].astype(bf16)
 
 
-def feed_forward(x, mine, other, gains, cotangent, weights, hidden):
+def feed_forward(x, mine, other, gains, cotangent, gate, up, down):
     rows, width = x.shape
+    hidden = gate.shape[1]
     steps = hidden // TILE
-    tile_of = lambda which: pl.BlockSpec((width, TILE), lambda j: (0, which * steps + j))
+    tile_of = pl.BlockSpec((width, TILE), lambda j: (0, j))
     acts_of = pl.BlockSpec((3, rows, TILE), lambda j: (0, 0, j))
     full = whole((rows, width))
     return pl.pallas_call(
         feed_kernel,
         grid=(steps,),
         in_specs=[full, full, full, whole(gains.shape), full]
-        + [tile_of(0), tile_of(1), tile_of(2)],
+        + [tile_of] * 3,
         out_specs=[full, full, acts_of, full, full],
         out_shape=[
             jax.ShapeDtypeStruct((rows, width), f32),
@@ -1137,7 +1220,7 @@
         compiler_params=params(56),
         cost_estimate=cost(12 * rows * width * hidden, 6 * width * hidden),
         name="feed_forward",
-    )(x, mine, other, gains, cotangent, weights, weights, weights)
+    )(x, mine, other, gains, cotangent, gate, up, down)
 
 
 def middle_kernel(cot_ref, mine_ref, other_ref, middle_ref, gain_ref, w_ref, bm_ref, bb_ref, ba_ref, grad_ref):
@@ -1345,32 +1428,29 @@
     place = jnp.stack([ctx]).astype(jnp.int32)
     q_cols = query_weight.shape[1]
     features = tokens.shape[1]
-    hidden = gate_weight.shape[1]
 
     gain_columns = jnp.pad(jnp.stack([pre_gain, mid_gain], axis=1), ((0, 0), (0, LANES - 2)))
     shard = jnp.concatenate(
         [query_weight, key_weight, value_weight, gain_columns, output_weight], axis=1
     )
-    second = lax.all_gather(
-        jnp.concatenate([gate_weight, up_weight, down_weight], axis=1), ROWS, axis=0, tiled=True
-    )
     stream = streams(order, ctx)
     lows = jnp.max(jnp.where(starts[None, :] <= stream[0][:, None], starts[None, :], 0), axis=1)
     cosine, sine = angles(stream[0] - lows)
-    if pairs == 2 and shard.shape[0] % 32 == 0:
-        first, queries, kv, normed, gains = gather_project(
-            shard, tokens, cosine, sine, q_cols, ctxs
-        )
+    if pairs == 2 and ctxs == 4 and shard.shape[0] % 32 == 0:
         qi = jnp.pad(jnp.stack([stream[0], lows]), ((0, 6), (0, 0)))
-        attended_low, att, sums = dense_attend(queries, kv, qi, stream[:, :, None])
-        output_weights = first[:, 2 * q_cols + LANES :]
-        branch = output_product(attended_low, output_weights, 0, features)
+        ki = stream[:, :, None]
+        (
+            first, gate_full, up_full, down_full, queries, kv, normed, gains,
+            attended_low, att, sums, branch, branch_other,
+        ) = forward_all(
+            shard, gate_weight, up_weight, down_weight, tokens, cosine, sine, qi, ki, q_cols, ctxs
+        )
         middle, mid_normed, act, back_part, feed = feed_forward(
-            tokens, branch, swapped(branch), gains, cotangent, second, hidden
+            tokens, branch, branch_other, gains, cotangent, gate_full, up_full, down_full
         )
         feed_other, back_middle, part, part_other, grads, _, _ = back_all(
             back_part, feed, cotangent, middle, gains, act, mid_normed, tokens, normed,
-            attended_low, queries, kv, att, sums, qi, stream[:, :, None], cosine, sine, first, ctxs,
+            attended_low, queries, kv, att, sums, qi, ki, cosine, sine, first, ctxs,
         )
         result = (middle + feed.astype(f32) + feed_other.astype(f32)).astype(bf16)
         token_gradient = final_back(back_middle, part, part_other, tokens, gains)
@@ -1381,7 +1461,10 @@
         gate_gradient, up_gradient = wide(0, 1, 2, 3), wide(4, 5, 6, 7)
         down_gradient = wide(8, 9, 10, 11)
     else:
-        first = lax.all_gather(shard, ROWS, axis=0, tiled=True)
+        first, gate_full, up_full, down_full = (
+            lax.all_gather(field, ROWS, axis=0, tiled=True)
+            for field in (shard, gate_weight, up_weight, down_weight)
+        )
         gains = first[:, 2 * q_cols : 2 * q_cols + 8].T.astype(f32)
         queries, kv, normed = project(tokens, gains, cosine, sine, first, q_cols)
         pieces = [kv] + [shifted(kv, "ctx", k) for k in range(1, ctxs)]
@@ -1389,7 +1472,7 @@
         attended_low, att, sums = attend(order, starts, place, queries, pieces)
         branch = output_product(attended_low, output_weights, 0, features)
         middle, mid_normed, act, back_part, feed = feed_forward(
-            tokens, branch, swapped(branch), gains, cotangent, second, hidden
+            tokens, branch, swapped(branch), gains, cotangent, gate_full, up_full, down_full
         )
         back_other = swapped(back_part)
         gate_parts = gradient(mid_normed, act[0], pairs, ctxs)

time: 525 us -> 491 us (0.935)
  waiting for transfers between devices: 35.8 us -> 0 us
  between operations: 14.7 us -> 1.25 us
  Pallas kernels: 448 us -> 459 us
    ppermute x1 -> x0, waiting for transfers between devices: 35.7 us -> none  [swapped(): return lax.ppermute(field, 'tp', [(i, count - 1 - i) for i in range(count)])]
    pallas_call x3 -> x1, Pallas kernels: 175 us -> 201 us  [forward_all(): pl.pallas_call(forward_kernel, in_specs=[vmem] + [hbm] * 3 + [vmem] * 5,...]
    pallas_call x1, Pallas kernels: 236 us -> 221 us  [back_all(): pl.pallas_call(back_kernel, in_specs=[hbm] * 4 + [vmem] + [hbm] * 4 + [vm...]
  transfers between devices with their start and end apart: 2 -> 0, of which waited for: 1 -> 0; matrix products, arithmetic and copies ran while one was open for 1% -> 0% of each run, Pallas kernels for 34% -> 0%
where the time goes in v4:
time: 491 us; the launch traced here: 483 us
  Pallas kernels  459 us (93%)
  other arithmetic  13.9 us (3%)
  local copies, waits for them, and re-layouts  8.95 us (2%)
    pallas_call x1, Pallas kernels, back_all(): pl.pallas_call(back_kernel, in_specs=[hbm] * 4 + [vmem] + [hbm] * 4 + [vm...  221 us
    pallas_call x1, Pallas kernels, forward_all(): pl.pallas_call(forward_kernel, in_specs=[vmem] + [hbm] * 3 + [vmem] * 5,...  201 us
    pallas_call x1, Pallas kernels, feed_forward(): pl.pallas_call(feed_kernel, grid=(steps,), in_specs=[full, full, full, wh...  33.6 us

profile of v4, /device:TPU:0, one launch (start us, length us, event | category | flops | bytes accessed | tf_op | source)
XLA Modules:
  0.0 483.1 jit_solution(10830359079470123938)
XLA Ops:
  0.6 0.0 copy-start
  0.7 0.7 copy-done
  1.3 0.7 pad_maximum_fusion.6
  2.0 0.8 reduce-window_clone.1
  2.8 0.7 subtract_bitcast_fusion
  3.5 0.6 gather_fusion
  4.1 0.1 iota_add_fusion
  4.2 0.1 squeeze.67
  4.3 0.1 slice.84
  4.3 0.1 select_reduce_fusion
  4.5 0.1 add.78
  4.5 0.6 pad.9.qi_ref
  5.1 0.1 add.73
  5.2 0.1 copy.31
  5.3 0.9 constant_dynamic-update-slice_fusion.3
  6.3 0.9 constant_dynamic-update-slice_fusion.2
  7.2 0.9 constant_dynamic-update-slice_fusion.1
  8.1 0.9 constant_dynamic-update-slice_fusion.shard_ref
  9.0 0.0 copy-start.8
  9.0 1.8 multiply_sine_fusion
  10.8 1.0 add.84
  11.9 1.1 broadcast_add_fusion.ki_ref
  13.0 0.0 copy-done.8
  13.0 201.2 %forward_all.1 = (bf16[1536,2432]{1,0:T(8,128)(2,1)}, bf16[1536,2048]{1,0:T(8,128)(2,1)}, bf16[1536,2048]{1,0:T(8,128)(2,1)}, bf16[1536,2048]{1,0:T(8,128)(2,1)}...) custom-call(bf16[96,2432]{1,0:T(8,128)(2,1)} %copy-done.8, ...), custom_call_target="tpu_custom_call" | custom-call | flops 10000000000 | bytes 100000000 | tf_op jit(solution)/shard_map/forward_all/pallas_call | solution.py:332
  214.2 33.6 %feed_forward.1 = (f32[512,1536]{1,0:T(8,128)}, bf16[512,1536]{1,0:T(8,128)(2,1)}, bf16[3,512,2048]{2,1,0:T(8,128)(2,1)}, bf16[512,1536]{1,0:T(8,128)(2,1)}, bf16[512,1536]{1,0:T(8,128)(2,1)}) custom-call(bf16[512,1536]{1,0:T(8,128)(2,1)} %x_ref.5, bf16[512,1536]{1,0:T(8,128)(2,1)} %get-tuple-element.34.mine_ref, ...), custom_call_target="tpu_custom_call" | custom-call | flops 19327352832 | bytes 18874368 | tf_op jit(solution)/shard_map/feed_forward/pallas_call | solution.py:1206
  247.8 0.0 copy-start.6
  247.8 221.4 %back_all.1 = (bf16[512,1536]{1,0:T(8,128)(2,1)}, f32[512,1536]{1,0:T(8,128)}, bf16[512,1536]{1,0:T(8,128)(2,1)}, bf16[512,1536]{1,0:T(8,128)(2,1)}, f32[17,96,5...) custom-call(bf16[512,1536]{1,0:T(8,128)(2,1)} %get-tuple-element.42.part_hbm, ...), custom_call_target="tpu_custom_call" | custom-call | flops 40000000000 | bytes 100000000 | tf_op jit(solution)/shard_map/back_all/pallas_call | solution.py:1097
  469.2 0.0 copy-start.2
  469.2 0.0 copy-start.3
  469.2 0.0 copy-start.4
  469.2 0.0 copy-start.5
  469.2 4.7 add_convert_fusion
  474.0 0.0 copy-done.6
  474.0 0.0 copy-done.2
  474.0 0.0 copy-done.3
  474.0 0.1 copy-done.4
  474.1 0.8 copy-done.5
  474.9 0.0 copy-start.7
  474.9 2.9 final_back.1
  477.8 0.0 copy-done.7
  477.8 0.4 slice_bitcast_fusion.3
  478.1 0.0 copy-start.1
  478.2 0.9 pad_maximum_fusion.2
  479.1 0.7 slice_reduce_fusion
  479.8 0.9 pad_maximum_fusion.3
  480.7 0.7 fusion.2
  481.4 1.3 pad_maximum_fusion
  482.6 0.0 copy-done.1
  (11 shorter events, 0.1 us)
Async XLA Ops:
  0.6 0.7 copy-start
  9.0 4.0 copy-start.8
  247.8 226.2 %copy-start.6 = (f32[8,1536]{1,0:T(8,128)S(1)}, f32[8,1536]{1,0:T(8,128)}, u32[]{:S(2)}) copy-start(f32[8,1536]{1,0:T(8,128)} %get-tuple-element.36.gain_ref) | copy-start | bytes 147460
  469.2 4.8 copy-start.2
  469.2 4.8 copy-start.3
  469.2 4.9 %copy-start.4 = (bf16[512,1536]{1,0:T(8,128)(2,1)S(1)}, bf16[512,1536]{1,0:T(8,128)(2,1)}, u32[]{:S(2)}) copy-start(bf16[512,1536]{1,0:T(8,128)(2,1)} %get-tuple-element.54.mine_ref) | copy-start | bytes 4718596
  469.2 5.7 %copy-start.5 = (bf16[512,1536]{1,0:T(8,128)(2,1)S(1)}, bf16[512,1536]{1,0:T(8,128)(2,1)}, u32[]{:S(2)}) copy-start(bf16[512,1536]{1,0:T(8,128)(2,1)} %get-tuple-element.55.other_ref) | copy-start | bytes 4718596
  474.9 2.9 copy-start.7
  478.1 4.5 copy-start.1

commit v5 on v4

--- a/solution.py
+++ b/solution.py
@@ -136,7 +136,8 @@
 
 
 def forward_kernel(
-    shard_ref, gate_shard, up_shard, down_shard, x_ref, cos_ref, sin_ref, qi_ref, ki_ref,
+    query_shard, key_shard, value_shard, gain_shard, out_shard, gate_shard, up_shard, down_shard,
+    x_ref, cos_ref, sin_ref, qi_ref, ki_ref,
     full_ref, gate_ref, up_ref, down_ref, q_ref, kv_ref, normed_ref, gain_ref, low_ref, att_ref, sum_ref,
     branch_ref, other_ref,
     w_ref, qt_ref, top_ref, total_ref,
@@ -147,12 +148,19 @@
     far, core = (lax.rem(dp + 2, 4), ctx, tp), (dp + 1 - 2 * lax.rem(dp, 2), ctx, tp)
     after, before = (dp, lax.rem(ctx + 1, ctxs), tp), (dp, lax.rem(ctx + ctxs - 1, ctxs), tp)
     across = (dp, ctx, 1 - tp)
+    piece = query_shard.shape[0]
+    mine = pl.ds(pl.multiple_of((dp * ctxs + ctx) * piece, piece), piece)
+    packs, column = [], 0
+    for j, part in enumerate((query_shard, key_shard, value_shard, gain_shard, out_shard)):
+        target = w_ref.at[mine, pl.ds(column, part.shape[1])]
+        packs.append(pltpu.make_async_copy(part, target, local.at[5 + j]))
+        packs[-1].start()
+        column += part.shape[1]
     barrier = pltpu.get_barrier_semaphore()
     for device in (after, before, far, core, across):
         pl.semaphore_signal(barrier, inc=1, device_id=device, device_id_type=MESH)
     pl.semaphore_wait(barrier, 5)
-    piece = shard_ref.shape[0]
-    shards = (shard_ref, gate_shard, up_shard, down_shard)
+    shards = (w_ref.at[mine], gate_shard, up_shard, down_shard)
     wholes = (w_ref, gate_ref, up_ref, down_ref)
     last = ctxs - 1
 
@@ -194,7 +202,8 @@
     def begin(group):
         over(group, 0).start()
         aside(group, 0).start()
-        own_copy(group).start()
+        if group:
+            own_copy(group).start()
 
     def along(group, s):
         ring(group, s - 1).wait_recv()
@@ -208,12 +217,15 @@
         aside_far(group, s).start()
 
     def gathered(group):
-        own_copy(group).wait()
+        if group:
+            own_copy(group).wait()
         for s in range(ctxs):
             aside(group, s).wait_recv()
             aside_far(group, s).wait_recv()
 
     first, gate, up, down = range(4)
+    for copy in packs:
+        copy.wait()
     ring(first, 0).start()
     begin(first)
     x = x_ref[...].astype(f32)
@@ -223,7 +235,9 @@
         came_over(first, s - 1)
     ring(gate, 0).start()
     begin(gate)
+    ring(up, 0).start()
     came_over(first, last)
+    begin(up)
     gathered(first)
     full = pltpu.make_async_copy(w_ref, full_ref, local.at[4])
     full.start()
@@ -255,7 +269,7 @@
         return remote(kv_ref.at[s], kv_ref.at[s + 1], after, k_send.at[s], k_recv.at[s])
 
     kv_copy(0).start()
-    begin(up)
+    begin(down)
     for step in range(2):
 
         def query_store(lanes, value):
@@ -267,10 +281,12 @@
         dense_piece(k, kv_ref, qi_ref, ki_ref, groups, ratio, qt_ref, top_ref, total_ref, att_ref)
 
     dense_begin(q_ref, groups, ratio, qt_ref, top_ref, total_ref, att_ref)
+    along(gate, 2)
+    came_over(gate, 0)
     waits = [
-        [lambda: along(gate, 2), lambda: came_over(gate, 0), lambda: came_over(gate, 1)],
-        [lambda: ring(up, 0).start(), lambda: begin(down), lambda: along(gate, last), lambda: came_over(up, 0)],
-        [],
+        [lambda: along(up, 1), lambda: along(gate, last), lambda: came_over(gate, 1), lambda: came_over(up, 0)],
+        [lambda: ring(down, 0).start(), lambda: came_over(down, 0), lambda: came_over(gate, 2)],
+        [lambda: along(up, 2)],
     ]
 
     def attention_step(k, unused):
@@ -288,22 +304,21 @@
         return unused
 
     lax.fori_loop(0, ctxs, attention_step, 0)
-    ring(down, 0).start()
-    along(up, 1)
     dense_end(groups, ratio, top_ref, total_ref, att_ref, sum_ref, low_ref)
     branch_ref[...] = dot(low_ref[...], w_ref[:, 2 * q_cols + LANES :], NT).astype(bf16)
     exchange = remote(branch_ref, other_ref, across, x_send.at[0], x_recv.at[0])
     exchange.start()
 
-    for s in range(2, ctxs):
-        along(up, s)
-        came_over(gate, s)
-        along(down, s - 1)
-        came_over(up, s - 1)
-        came_over(down, s - 2)
+    along(down, 1)
+    came_over(gate, last)
+    came_over(up, 1)
+    along(up, last)
+    came_over(up, 2)
+    along(down, 2)
+    came_over(down, 1)
+    came_over(up, last)
     along(down, last)
-    came_over(up, last)
-    came_over(down, last - 1)
+    came_over(down, 2)
     came_over(down, last)
     for group in (gate, up, down):
         gathered(group)
@@ -320,9 +335,9 @@
     full.wait()
 
 
-def forward_all(shard, gate, up, down, x, cosine, sine, qi, ki, q_cols, ctxs):
+def forward_all(packed, gate, up, down, x, cosine, sine, qi, ki, q_cols, ctxs):
     rows, width = x.shape
-    columns, hidden = shard.shape[1], gate.shape[1]
+    columns, hidden = sum(part.shape[1] for part in packed), gate.shape[1]
     groups = q_cols // 2 // HEAD_SIZE
     tiles, lanes = dense_shapes(rows, groups, 2)
     vmem, hbm = pl.BlockSpec(memory_space=pltpu.VMEM), pl.BlockSpec(memory_space=pl.ANY)
@@ -331,7 +346,7 @@
     full = shape((rows, width), bf16)
     return pl.pallas_call(
         forward_kernel,
-        in_specs=[vmem] + [hbm] * 3 + [vmem] * 5,
+        in_specs=[hbm] * (len(packed) + 3) + [vmem] * 5,
         out_specs=[hbm] * 4 + [vmem] * 9,
         out_shape=[
             shape((width, columns), bf16),
@@ -359,13 +374,13 @@
         + [sems(4, 2 * ctxs)] * 2
         + [sems(ctxs - 1)] * 2
         + [sems(1)] * 2
-        + [sems(5)],
+        + [sems(5 + len(packed))],
         compiler_params=pltpu.CompilerParams(
             vmem_limit_bytes=56 * MIB, collective_id=0, has_side_effects=True
         ),
         cost_estimate=cost(1e10, 1e8),
         name="forward_all",
-    )(shard, gate, up, down, x, cosine, sine, qi, ki)
+    )(*packed, gate, up, down, x, cosine, sine, qi, ki)
 
 
 def gather_stream(order, ctx, pieces, k_ref, v_ref):
@@ -660,13 +675,14 @@
 
 FEED_TILES = 12
 TILES = 17
-SLOTS = 8
+EARLY = 5
+SLOTS = 6
 
 
 def back_kernel(
     part_hbm, feed_hbm, cot_hbm, middle_hbm, gain_ref, act_hbm, mid_normed_hbm, x_hbm, normed_hbm,
     low_ref, q_ref, kv_ref, att_ref, sum_ref, qi_ref, ki_ref, cos_ref, sin_ref, weight_hbm,
-    feed_other, back_middle, part2_out, part2_other, grads_ref, held_hbm, far_hbm,
+    feed_other, back_middle, part2_other, result_ref, token_ref, grads_ref, held_hbm, far_hbm,
     lhs, mid, part, part_other, w_out, w_in, rhs, q2, q2t, d2, d2t, delta, bias_ref, dq_ref,
     kv_sent, kv_got, cot, gain_rows, gain_other, gain_columns,
     p_send, p_keep, c_got, s_one, own, y_got, z_got,
@@ -678,6 +694,7 @@
     pair_at, core_at = dp // 2, lax.rem(dp, 2)
     far, core = (lax.rem(dp + 2, 4), ctx, tp), (dp + 1 - 2 * core_at, ctx, tp)
     after, before = (dp, lax.rem(ctx + 1, ctxs), tp), (dp, lax.rem(ctx + ctxs - 1, ctxs), tp)
+    beside, opposite = (dp, ctx + 1 - 2 * lax.rem(ctx, 2), tp), (dp, lax.rem(ctx + 2, 4), tp)
     across = (dp, ctx, 1 - tp)
     rows, width = mid.shape
     section = width // 4
@@ -688,9 +705,9 @@
     q_cols = q_ref.shape[1]
 
     barrier = pltpu.get_barrier_semaphore()
-    for device in (after, before, far, core, across):
+    for device in (after, before, opposite, far, core, across):
         pl.semaphore_signal(barrier, inc=1, device_id=device, device_id_type=MESH)
-    pl.semaphore_wait(barrier, 5)
+    pl.semaphore_wait(barrier, 6)
 
     def remote(source, target, device, sent, got):
         return pltpu.make_async_remote_copy(source, target, sent, got, device, MESH)
@@ -712,7 +729,8 @@
                 start = pl.multiple_of(there * section, LANES)
                 result = rhs_of(start, lhs_of(pl.ds(start, section)))
                 for z in range(ctxs):
-                    place = lax.rem(z + 2 * ctxs - ctx - 1, ctxs)
+                    odd, half = lax.rem(z + ctx, 2), lax.rem(z // 2 + ctx // 2, 2)
+                    place = 2 * (1 - odd) + odd * half + (1 - odd) * (1 - half)
                     target = pl.ds(pl.multiple_of(y * section + place * piece, piece), piece)
                     out[slot, target, :] = result[z * piece : (z + 1) * piece]
 
@@ -765,50 +783,60 @@
     def got_copy(t):
         return pltpu.make_async_copy(far_hbm.at[t], y_got.at[lax.rem(t, 2)], own_sem.at[t, 1])
 
-    def ring_copy(t, step):
+
+    def near_copy(t):
         return remote(
-            own.at[lax.rem(t, SLOTS), pl.ds((ctxs - 2 - step) * piece, piece)],
-            z_got.at[t, step], after, z_send.at[t, step], z_recv.at[t, step],
-        )
-
-    def ring_add(t, step):
-        ring_copy(t, step).wait_recv()
-        ring_copy(t, step).wait_send()
-        place = ctxs - 3 - step if step < ctxs - 2 else ctxs - 1
-        target = pl.ds(place * piece, piece)
-        total = own[lax.rem(t, SLOTS), target, :].astype(f32) + z_got[t, step].astype(f32)
-        if step < ctxs - 2:
-            own[lax.rem(t, SLOTS), target, :] = total.astype(bf16)
-            ring_copy(t, step + 1).start()
-        else:
-            grads_ref[t] = total
+            own.at[lax.rem(t, SLOTS), pl.ds(0, 2 * piece)],
+            z_got.at[t, pl.ds(0, 2 * piece)], beside, z_send.at[t, 0], z_recv.at[t, 0],
+        )
+
+    def last_copy(t):
+        return remote(
+            own.at[lax.rem(t, SLOTS), pl.ds(2 * piece, piece)],
+            z_got.at[t, pl.ds(2 * piece, piece)], opposite, z_send.at[t, 1], z_recv.at[t, 1],
+        )
+
+    def meet_near(t):
+        near_copy(t).wait_recv()
+        near_copy(t).wait_send()
+        slot = lax.rem(t, SLOTS)
+        for target, came in ((2, 1), (3, 0)):
+            here = pl.ds(target * piece, piece)
+            total = own[slot, here, :].astype(f32) + z_got[t, came * piece : (came + 1) * piece].astype(f32)
+            own[slot, here, :] = total.astype(bf16)
+        last_copy(t).start()
+
+    def meet_last(t):
+        last_copy(t).wait_recv()
+        last_copy(t).wait_send()
+        mine = own[lax.rem(t, SLOTS), 3 * piece :, :].astype(f32)
+        grads_ref[t] = mine + z_got[t, 2 * piece :].astype(f32)
+
+    def fetch(t):
+        far_copy(t).wait_recv()
+        own_copy(t).start()
+        got_copy(t).start()
+
+    def meet_far(t):
+        own_copy(t).wait()
+        got_copy(t).wait()
+        slot, got = lax.rem(t, SLOTS), lax.rem(t, 2)
+        for z in range(ctxs):
+            target = pl.ds(z * piece, piece)
+            total = own[slot, target, :].astype(f32) + y_got[got, target, :].astype(f32)
+            own[slot, target, :] = total.astype(bf16)
+        near_copy(t).start()
+
+    def when(test, step, t):
+        @pl.when(test)
+        def _():
+            step(t)
 
     def tick(n):
-        for step in range(ctxs - 2, -1, -1):
-
-            t = n - 3 - 2 * step
-
-            @pl.when((t >= 0) & (t < TILES))
-            def _(t=t, step=step):
-                ring_add(t, step)
-
-        @pl.when((n >= 1) & (n - 1 < TILES))
-        def _():
-            t = n - 1
-            own_copy(t).wait()
-            got_copy(t).wait()
-            slot, got = lax.rem(t, SLOTS), lax.rem(t, 2)
-            for z in range(ctxs):
-                target = pl.ds(z * piece, piece)
-                total = own[slot, target, :].astype(f32) + y_got[got, target, :].astype(f32)
-                own[slot, target, :] = total.astype(bf16)
-            ring_copy(t, 0).start()
-
-        @pl.when(n < TILES)
-        def _():
-            far_copy(n).wait_recv()
-            own_copy(n).start()
-            got_copy(n).start()
+        when((n - 1 > EARLY) & (n - 1 < TILES), meet_far, n - 1)
+        when((n - 3 >= EARLY) & (n - 3 < TILES), meet_near, n - 3)
+        when((n - 5 >= EARLY - 1) & (n - 5 < TILES), meet_last, n - 5)
+        when(n < TILES, fetch, n)
 
 
     part_copy = remote(part_hbm, part_other, across, x_send.at[0], x_recv.at[0])
@@ -859,9 +887,11 @@
         def _():
             send_far(t - 2)
 
-        @pl.when((t >= 5) & (lax.rem(t, 3) == 2))
-        def _():
-            tick((t - 5) // 3)
+        n, turn = (t - 4) // 3, lax.rem(t, 3)
+        when((t >= 4) & (turn == 1), fetch, n)
+        when((t >= 7) & (turn == 1), meet_near, n - 1)
+        when((t >= 4) & (turn == 2), meet_far, n)
+        when((t >= 7) & (turn == 0), meet_last, n - 1)
 
         return unused
 
@@ -876,12 +906,15 @@
             q2[q_tile * groups + g] = flat
             q2t[q_tile * groups + g] = flat.astype(f32).T.astype(bf16)
     dq_ref[...] = jnp.zeros(dq_ref.shape, f32)
-    kv_got[0] = jnp.zeros(kv_got.shape[1:], bf16)
     gain_rows[...] = jnp.zeros(gain_rows.shape, f32)
 
 
     loads[2].wait()
     loads[3].wait()
+    t_1, t_2, t_3, t_4, t_5 = (jnp.int32(j) for j in range(1, 6))
+    fetch(t_3)
+    meet_last(t_1)
+    meet_near(t_2)
     part_copy.wait_recv()
     few = 64
 
@@ -901,6 +934,9 @@
         return unused
 
     lax.fori_loop(0, rows // few, norm_rows, 0)
+    meet_far(t_3)
+    meet_last(t_2)
+    fetch(t_4)
     middle_copy = load(mid, back_middle, 6)
     middle_copy.start()
     normed_copy = load(normed_hbm, lhs.at[1], 7)
@@ -909,6 +945,9 @@
     x_copy.start()
     loads[4].wait()
     cot[:, :q_cols] = dot(lhs[0], w_out[...], NN).astype(bf16)
+    meet_far(t_4)
+    meet_near(t_3)
+    fetch(t_5)
     for q_tile in range(rows // SIDE):
         for g in range(groups):
             i = q_tile * groups + g
@@ -917,7 +956,9 @@
             d2[i] = flat
             d2t[i] = turned_flat.astype(bf16)
             delta[i] = jnp.sum(turned_flat * att_ref[i], axis=0, keepdims=True)
-    tick(jnp.int32(3))
+    meet_last(t_3)
+    meet_far(t_5)
+    meet_near(t_4)
 
     t_out = jnp.int32(FEED_TILES)
     product(
@@ -926,7 +967,7 @@
 
 
     def kv_copy(s):
-        return remote(kv_sent.at[s], kv_got.at[s + 1], after, k_send.at[s], k_recv.at[s])
+        return remote(kv_sent.at[s], kv_got.at[s], after, k_send.at[s], k_recv.at[s])
 
     def back_piece(s, unused):
         k = lax.rem(s + 1, ctxs)
@@ -955,37 +996,35 @@
                 kv_sent[s, here, head_lanes(g)] = (d_key * SCALE).astype(bf16)
                 kv_sent[s, here, head_lanes(g, kv_width)] = d_value.astype(bf16)
 
-        @pl.when(s >= 1)
-        def _():
-            kv_copy(s - 1).wait_recv()
-
-            def add(i, unused):
-                here = pl.ds(pl.multiple_of(i * few, few), few)
-                total = kv_sent[s, here, :].astype(f32) + kv_got[s, here, :].astype(f32)
-                kv_sent[s, here, :] = total.astype(bf16)
-                return unused
-
-            lax.fori_loop(0, rows // few, add, 0)
-
-        @pl.when(s < ctxs - 1)
-        def _():
-            kv_copy(s).start()
-
         @pl.when(s == 0)
         def _():
+            kv_copy(0).start()
             meet_core(t_out)
             send_far(t_out)
 
-        @pl.when(s < ctxs - 1)
+        @pl.when((s == 1) | (s == 3))
         def _():
-            tick(5 + s)
+            tick(6 + s // 2)
 
         return unused
 
-    tick(jnp.int32(4))
     lax.fori_loop(0, ctxs, back_piece, 0)
 
-
+    def kv_pass(s):
+        kv_copy(s).wait_recv()
+
+        def add(i, unused):
+            here = pl.ds(pl.multiple_of(i * few, few), few)
+            total = kv_sent[s + 1, here, :].astype(f32) + kv_got[s, here, :].astype(f32)
+            kv_sent[s + 1, here, :] = total.astype(bf16)
+            return unused
+
+        lax.fori_loop(0, rows // few, add, 0)
+        if s + 1 < ctxs - 1:
+            kv_copy(s + 1).start()
+
+
+    kv_pass(0)
     for i in range(dq_ref.shape[0]):
         q_tile, g = divmod(i, groups)
         here = slice(q_tile * SIDE, (q_tile + 1) * SIDE)
@@ -994,74 +1033,130 @@
             cot[here, head_lanes(g * ratio + h)] = turned(
                 flat[h * SIDE : (h + 1) * SIDE], cos_ref[here, :], sin_ref[here, :], -1
             ).astype(bf16)
+    normed_copy.wait()
+    tail = q_cols - TILE
+    t_query, t_both, t_key, t_last = (jnp.int32(FEED_TILES + 1 + j) for j in range(4))
+    product(
+        t_query, lambda lanes: lhs[1, :, lanes], lambda start, left: dot(left, cot[:, :TILE], TN).astype(bf16)
+    )
+
+    def times_both(start, left):
+        from_query = dot(left, cot[:, TILE:q_cols], TN)
+        from_output = dot(lhs[0, :, pl.ds(start, section)], low_ref[:, TILE:], TN)
+        return jnp.concatenate([from_query, from_output], axis=1).astype(bf16)
+
+    meet_core(t_query)
+    product(t_both, lambda lanes: lhs[1, :, lanes], times_both)
+    send_far(t_query)
+    tick(jnp.int32(8))
+    meet_core(t_both)
+    send_far(t_both)
+    feed_copy.wait_recv()
+    here_copies = [load(feed_hbm, lhs.at[0], 9), load(feed_other, part_other, 10)]
+    for copy in here_copies:
+        copy.start()
+    loads[5].wait()
+    middle_copy.wait()
+    for j in range(width // TILE):
+        lanes = slice(j * TILE, (j + 1) * TILE)
+        mid[:, lanes] = dot(cot[:, :q_cols], w_in[lanes, :q_cols], NT)
+    kv_pass(1)
+    tick(jnp.int32(9))
+
+
+    for copy in here_copies:
+        copy.wait()
+    for half in range(rows // SIDE):
+        here = slice(half * SIDE, (half + 1) * SIDE)
+        pieces = [
+            load(
+                middle_hbm.at[pl.ds(half * SIDE, SIDE), pl.ds(j * TILE, TILE)],
+                bias_ref.at[j], 11 + half * (width // TILE) + j,
+            )
+            for j in range(width // TILE)
+        ]
+        for copy in pieces:
+            copy.start()
+        for j, copy in enumerate(pieces):
+            copy.wait()
+            lanes = slice(j * TILE, (j + 1) * TILE)
+            total = bias_ref[j] + lhs[0, here, lanes].astype(f32)
+            lhs[0, here, lanes] = (total + part_other[here, lanes].astype(f32)).astype(bf16)
+    result_copy = load(lhs.at[0], result_ref, 17)
+    result_copy.start()
+    tick(jnp.int32(10))
+
+    kv_pass(2)
     for g in range(groups):
         cot[:, head_lanes(g, q_cols)] = turned(
             kv_sent[ctxs - 1, :, head_lanes(g)].astype(f32), cos_ref[...], sin_ref[...], -1
         ).astype(bf16)
     cot[:, q_cols + kv_width :] = kv_sent[ctxs - 1, :, kv_width:]
-    loads[5].wait()
     x_copy.wait()
     x_rows = part[...].astype(f32)
     scale = lax.rsqrt(jnp.mean(x_rows * x_rows, axis=1, keepdims=True) + epsilon)
     for j in range(width // TILE):
         lanes = slice(j * TILE, (j + 1) * TILE)
-        back = dot(cot[...], w_in[lanes, :], NT)
+        back = mid[:, lanes] + dot(cot[:, q_cols:], w_in[lanes, q_cols:], NT)
         part_other[:, lanes] = back.astype(bf16)
         gain_rows[0:1, lanes] += jnp.sum(back * (part[:, lanes].astype(f32) * scale), axis=0, keepdims=True)
     gain_copy = remote(gain_rows.at[pl.ds(0, 8)], gain_other, across, x_send.at[2], x_recv.at[2])
     gain_copy.start()
     part2_copy = remote(part_other, part2_other, across, x_send.at[3], x_recv.at[3])
     part2_copy.start()
-    part2_save = load(part_other, part2_out, 9)
-    part2_save.start()
-    normed_copy.wait()
-
-    def qkv_step(j, unused):
-        t = FEED_TILES + 1 + j
-
-        def times(start, left):
-            lanes = pl.ds(pl.multiple_of(j * TILE, TILE), TILE)
-            return dot(left, cot[:, lanes], TN).astype(bf16)
-
-        product(t, lambda lanes: lhs[1, :, lanes], times)
-
-        @pl.when(j >= 1)
-        def _():
-            meet_core(t - 1)
-
-        @pl.when(j >= 2)
-        def _():
-            send_far(t - 2)
-
-        tick(4 + ctxs + j)
-        return unused
-
-    lax.fori_loop(0, 3, qkv_step, 0)
+    middle_back_copy = load(back_middle, mid, 18)
+    middle_back_copy.start()
+    product(
+        t_key, lambda lanes: lhs[1, :, lanes], lambda start, left: dot(left, cot[:, q_cols : q_cols + TILE], TN).astype(bf16)
+    )
     gain_copy.wait_recv()
     gain_copy.wait_send()
     gain_rows[0:1, :] += gain_other[0:1, :]
     gain_columns[...] = gain_rows[...].T
-    last = jnp.int32(TILES - 1)
-    tail = q_cols - TILE
 
     def times_last(start, left):
-        some = dot(left, low_ref[:, TILE:], TN)
+        some = dot(left, cot[:, q_cols + TILE :], TN)
         gains = gain_columns[pl.ds(start, section), :]
         spare = jnp.zeros((section, TILE - tail - LANES), f32)
         return jnp.concatenate([some, gains, spare], axis=1).astype(bf16)
 
-    product(last, lambda lanes: lhs[0, :, lanes], times_last)
-    meet_core(last - 1)
-    send_far(last - 2)
-    meet_core(last)
-    send_far(last - 1)
-    send_far(last)
+    meet_core(t_key)
+    product(t_last, lambda lanes: lhs[1, :, lanes], times_last)
+    send_far(t_key)
+    meet_core(t_last)
+    send_far(t_last)
 
     def drain(n, unused):
         tick(n)
         return unused
 
-    lax.fori_loop(7 + ctxs, TILES + 2 * ctxs - 1, drain, 0)
+    lax.fori_loop(11, TILES, drain, 0)
+
+
+    result_copy.wait()
+    part2_copy.wait()
+    other_copy = load(part2_other, lhs.at[0], 19)
+    other_copy.start()
+    middle_back_copy.wait()
+    other_copy.wait()
+
+    def token_rows(i, unused):
+        here = pl.ds(pl.multiple_of(i * few, few), few)
+        field = part[here, :].astype(f32)
+        scale = lax.rsqrt(jnp.mean(field * field, axis=1, keepdims=True) + epsilon)
+        unit = field * scale
+        back = part_other[here, :].astype(f32) + lhs[0, here, :].astype(f32)
+        inner = back * gain_ref[0:1, :]
+        out = mid[here, :] + scale * (
+            inner - unit * jnp.mean(inner * unit, axis=1, keepdims=True)
+        )
+        part_other[here, :] = out.astype(bf16)
+        return unused
+
+    lax.fori_loop(0, rows // few, token_rows, 0)
+    token_copy = load(part_other, token_ref, 20)
+    token_copy.start()
+    lax.fori_loop(TILES, TILES + 5, drain, 0)
 
     for t in (TILES - 2, TILES - 1):
         core_copy(jnp.int32(t)).wait_send()
@@ -1074,10 +1169,8 @@
     for s in range(ctxs - 1):
         kv_copy(s).wait_send()
     part_copy.wait_send()
-    feed_copy.wait()
-    part2_copy.wait()
-    part2_save.wait()
-    middle_copy.wait()
+    feed_copy.wait_send()
+    token_copy.wait()
 
 
 def back_all(part, feed, cotangent, middle, gains, act, mid_normed, x, normed, low, queries, kv, att, sums, qi, ki, cosine, sine, weights, ctxs):
@@ -1097,10 +1190,11 @@
     return pl.pallas_call(
         back_kernel,
         in_specs=[hbm] * 4 + [vmem] + [hbm] * 4 + [vmem] * 9 + [hbm],
-        out_specs=[hbm] * 4 + [vmem] + [hbm] * 2,
+        out_specs=[hbm] * 5 + [vmem] + [hbm] * 2,
         out_shape=[
             full,
             jax.ShapeDtypeStruct((rows, width), f32),
+            full,
             full,
             full,
             jax.ShapeDtypeStruct((TILES, piece, TILE), f32),
@@ -1113,14 +1207,14 @@
             space(tiles, lanes, HEAD_SIZE), space(tiles, HEAD_SIZE, lanes),
             space(tiles, lanes, HEAD_SIZE), space(tiles, HEAD_SIZE, lanes),
             wide(tiles, 1, lanes), wide(pairs, SIDE, lanes), wide(tiles, HEAD_SIZE, lanes),
-            space(ctxs, rows, q_cols), space(ctxs, rows, q_cols), space(rows, 2 * q_cols),
+            space(ctxs, rows, q_cols), space(ctxs - 1, rows, q_cols), space(rows, 2 * q_cols),
             wide(LANES, width), wide(8, width), wide(width, LANES),
             space(2, 2 * section, TILE), space(2, 2 * section, TILE), space(4, 2 * section, TILE),
             space(2, 2 * section, TILE), space(SLOTS, section, TILE), space(2, section, TILE),
-            space(TILES, ctxs - 1, piece, TILE),
-            sems(10), sems(FEED_TILES), sems(4), sems(4), sems(TILES), sems(TILES),
+            space(TILES, (ctxs - 1) * piece, TILE),
+            sems(21), sems(FEED_TILES), sems(4), sems(4), sems(TILES), sems(TILES),
             pltpu.SemaphoreType.REGULAR, sems(TILES), sems(TILES), sems(TILES), sems(TILES, 2),
-            sems(TILES, ctxs - 1), sems(TILES, ctxs - 1), sems(ctxs - 1), sems(ctxs - 1),
+            sems(TILES, 2), sems(TILES, 2), sems(ctxs - 1), sems(ctxs - 1),
         ],
         compiler_params=pltpu.CompilerParams(
             vmem_limit_bytes=63 * MIB, collective_id=1, has_side_effects=True
@@ -1430,40 +1524,39 @@
     features = tokens.shape[1]
 
     gain_columns = jnp.pad(jnp.stack([pre_gain, mid_gain], axis=1), ((0, 0), (0, LANES - 2)))
-    shard = jnp.concatenate(
-        [query_weight, key_weight, value_weight, gain_columns, output_weight], axis=1
-    )
+    packed = (query_weight, key_weight, value_weight, gain_columns, output_weight)
     stream = streams(order, ctx)
     lows = jnp.max(jnp.where(starts[None, :] <= stream[0][:, None], starts[None, :], 0), axis=1)
     cosine, sine = angles(stream[0] - lows)
-    if pairs == 2 and ctxs == 4 and shard.shape[0] % 32 == 0:
+    if pairs == 2 and ctxs == 4 and query_weight.shape[0] % 32 == 0:
         qi = jnp.pad(jnp.stack([stream[0], lows]), ((0, 6), (0, 0)))
         ki = stream[:, :, None]
         (
             first, gate_full, up_full, down_full, queries, kv, normed, gains,
             attended_low, att, sums, branch, branch_other,
         ) = forward_all(
-            shard, gate_weight, up_weight, down_weight, tokens, cosine, sine, qi, ki, q_cols, ctxs
+            packed, gate_weight, up_weight, down_weight, tokens, cosine, sine, qi, ki, q_cols, ctxs
         )
         middle, mid_normed, act, back_part, feed = feed_forward(
             tokens, branch, branch_other, gains, cotangent, gate_full, up_full, down_full
         )
-        feed_other, back_middle, part, part_other, grads, _, _ = back_all(
+        _, _, _, result, token_gradient, grads, _, _ = back_all(
             back_part, feed, cotangent, middle, gains, act, mid_normed, tokens, normed,
             attended_low, queries, kv, att, sums, qi, ki, cosine, sine, first, ctxs,
         )
-        result = (middle + feed.astype(f32) + feed_other.astype(f32)).astype(bf16)
-        token_gradient = final_back(back_middle, part, part_other, tokens, gains)
         wide = lambda *tiles: jnp.concatenate([grads[t] for t in tiles], axis=1)
-        qkv_gradient = wide(13, 14, 15)
-        output_gradient = jnp.concatenate([grads[12], grads[16][:, : q_cols - TILE]], axis=1)
-        gain_sums = grads[16][:, q_cols - TILE :]
+        tail = q_cols - TILE
+        qkv_gradient = jnp.concatenate(
+            [grads[13], grads[14][:, :tail], grads[15], grads[16][:, :tail]], axis=1
+        )
+        output_gradient = jnp.concatenate([grads[12], grads[14][:, tail:]], axis=1)
+        gain_sums = grads[16][:, tail : tail + LANES]
         gate_gradient, up_gradient = wide(0, 1, 2, 3), wide(4, 5, 6, 7)
         down_gradient = wide(8, 9, 10, 11)
     else:
         first, gate_full, up_full, down_full = (
             lax.all_gather(field, ROWS, axis=0, tiled=True)
-            for field in (shard, gate_weight, up_weight, down_weight)
+            for field in (jnp.concatenate(packed, axis=1), gate_weight, up_weight, down_weight)
         )
         gains = first[:, 2 * q_cols : 2 * q_cols + 8].T.astype(f32)
         queries, kv, normed = project(tokens, gains, cosine, sine, first, q_cols)

time: 491 us -> 460 us (0.937)
  Pallas kernels: 459 us -> 431 us
    pallas_call x2 -> x1, Pallas kernels: 204 us -> 187 us  [forward_all(): pl.pallas_call(forward_kernel, in_specs=[hbm] * (len(packed) + 3) + [vmem...]
    pallas_call x1, Pallas kernels: 221 us -> 211 us  [back_all(): pl.pallas_call(back_kernel, in_specs=[hbm] * 4 + [vmem] + [hbm] * 4 + [vm...]
where the time goes in v5:
time: 460 us; the launch traced here: 452 us
  Pallas kernels  431 us (94%)
  local copies, waits for them, and re-layouts  10.8 us (2%)
  other arithmetic  9.05 us (2%)
    pallas_call x1, Pallas kernels, back_all(): pl.pallas_call(back_kernel, in_specs=[hbm] * 4 + [vmem] + [hbm] * 4 + [vm...  211 us
    pallas_call x1, Pallas kernels, forward_all(): pl.pallas_call(forward_kernel, in_specs=[hbm] * (len(packed) + 3) + [vmem...  187 us
    pallas_call x1, Pallas kernels, feed_forward(): pl.pallas_call(feed_kernel, grid=(steps,), in_specs=[full, full, full, wh...  33.6 us

profile of v5, /device:TPU:0, one launch (start us, length us, event | category | flops | bytes accessed | tf_op | source)
XLA Modules:
  0.0 451.9 jit_solution(12324900608097756321)
XLA Ops:
  0.6 0.0 copy-start
  0.7 0.7 copy-done
  1.3 0.7 pad_maximum_fusion.6
  2.0 0.8 reduce-window_clone.1
  2.8 0.7 subtract_bitcast_fusion
  3.5 0.6 gather_fusion
  4.1 0.1 iota_add_fusion
  4.2 0.1 squeeze.68
  4.3 0.1 slice.89
  4.3 0.1 select_reduce_fusion
  4.5 0.1 add.72
  4.5 0.6 pad.9.qi_ref
  5.1 0.1 add.67
  5.2 0.1 copy.31
  5.3 0.6 pad.8.gain_shard
  6.0 1.8 multiply_sine_fusion
  7.7 1.0 add.76
  8.8 1.1 broadcast_add_fusion.ki_ref
  9.9 186.9 %forward_all.1 = (bf16[1536,2432]{1,0:T(8,128)(2,1)}, bf16[1536,2048]{1,0:T(8,128)(2,1)}, bf16[1536,2048]{1,0:T(8,128)(2,1)}, bf16[1536,2048]{1,0:T(8,128)(2,1)}...) custom-call(bf16[96,768]{1,0:T(8,128)(2,1)} %query_shard.1, ...), custom_call_target="tpu_custom_call" | custom-call | flops 10000000000 | bytes 100000000 | tf_op jit(solution)/shard_map/forward_all/pallas_call | solution.py:347
  196.8 33.6 %feed_forward.1 = (f32[512,1536]{1,0:T(8,128)}, bf16[512,1536]{1,0:T(8,128)(2,1)}, bf16[3,512,2048]{2,1,0:T(8,128)(2,1)}, bf16[512,1536]{1,0:T(8,128)(2,1)}, bf16[512,1536]{1,0:T(8,128)(2,1)}) custom-call(bf16[512,1536]{1,0:T(8,128)(2,1)} %x_hbm.1, bf16[512,1536]{1,0:T(8,128)(2,1)} %get-tuple-element.32.mine_ref, ...), custom_call_target="tpu_custom_call" | custom-call | flops 19327352832 | bytes 18874368 | tf_op jit(solution)/shard_map/feed_forward/pallas_call | solution.py:1300
  230.3 210.7 %back_all.1 = (bf16[512,1536]{1,0:T(8,128)(2,1)}, f32[512,1536]{1,0:T(8,128)}, bf16[512,1536]{1,0:T(8,128)(2,1)}, bf16[512,1536]{1,0:T(8,128)(2,1)}, bf16[512,15...) custom-call(bf16[512,1536]{1,0:T(8,128)(2,1)} %get-tuple-element.38.part, ...), custom_call_target="tpu_custom_call" | custom-call | flops 40000000000 | bytes 100000000 | tf_op jit(solution)/shard_map/back_all/pallas_call | solution.py:1190
  441.0 2.4 slice_bitcast_fusion.3
  443.4 0.9 pad_maximum_fusion.2
  444.3 0.7 slice_reduce_fusion
  445.0 0.7 pad_maximum_fusion.5
  445.7 0.9 pad_maximum_fusion.3
  446.6 0.0 copy-start.3
  446.6 1.3 pad_maximum_fusion
  447.9 0.7 copy-done.3
  448.6 0.0 copy-start.2
  448.6 0.0 copy-start.1
  448.6 1.1 copy.35
  449.7 0.8 copy-done.2
  450.5 1.1 copy.36
  451.7 0.0 copy-done.1
  (11 shorter events, 0.1 us)
Async XLA Ops:
  0.6 0.7 copy-start
  446.6 2.0 copy-start.3
  448.6 2.0 copy-start.2
  448.6 3.1 copy-start.1

commit v6 on v5

--- a/solution.py
+++ b/solution.py
@@ -3,6 +3,7 @@
 
 import jax
 import jax.numpy as jnp
+import numpy as np
 from jax import lax
 from jax.experimental import pallas as pl
 from jax.experimental.pallas import tpu as pltpu
@@ -13,6 +14,7 @@
 BLOCK = 64
 SPAN = 256
 TILE = 512
+FEED_TILE = 512
 LANES = 128
 
 epsilon = 1e-05
@@ -51,9 +53,13 @@
 SCALARS = pl.BlockSpec(memory_space=pltpu.SMEM)
 
 
+def frequencies():
+    steps = np.arange(HALF, dtype=np.float64) * 2.0 / HEAD_SIZE
+    return jnp.asarray(rotary_base ** -steps, f32)[None, :]
+
+
 def angles(place):
-    frequency = rotary_base ** (-(jnp.arange(HALF, dtype=f32) * 2.0 / HEAD_SIZE))
-    turn = place.astype(f32)[:, None] * frequency[None, :]
+    turn = place.astype(f32)[:, None] * frequencies()
     return (jnp.cos(turn), jnp.sin(turn))
 
 
@@ -137,10 +143,10 @@
 
 def forward_kernel(
     query_shard, key_shard, value_shard, gain_shard, out_shard, gate_shard, up_shard, down_shard,
-    x_ref, cos_ref, sin_ref, qi_ref, ki_ref,
+    x_ref, frequency_ref, qi_ref,
     full_ref, gate_ref, up_ref, down_ref, q_ref, kv_ref, normed_ref, gain_ref, low_ref, att_ref, sum_ref,
-    branch_ref, other_ref,
-    w_ref, qt_ref, top_ref, total_ref,
+    middle_ref, mid_normed_ref, cos_ref, sin_ref, ki_ref,
+    branch_ref, other_ref, w_ref, qt_ref, top_ref, total_ref,
     z_send, z_recv, y_send, y_recv, c_send, c_recv, k_send, k_recv, x_send, x_recv, local,
 ):
     ctxs = lax.axis_size("ctx")
@@ -228,6 +234,12 @@
         copy.wait()
     ring(first, 0).start()
     begin(first)
+    columns = qi_ref[...].astype(f32).T
+    turn = (columns[:, 0:1] - columns[:, 1:2]) * frequency_ref[...]
+    cos_ref[...] = jnp.cos(turn)
+    sin_ref[...] = jnp.sin(turn)
+    for k in range(ctxs):
+        ki_ref[k] = columns[:, 2 + k : 3 + k].astype(jnp.int32)
     x = x_ref[...].astype(f32)
     unit = x * lax.rsqrt(jnp.mean(x * x, axis=1, keepdims=True) + epsilon)
     for s in range(1, ctxs):
@@ -319,6 +331,20 @@
     came_over(up, last)
     along(down, last)
     came_over(down, 2)
+    exchange.wait_recv()
+    few = 64
+
+    def middle_rows(i, unused):
+        here = pl.ds(pl.multiple_of(i * few, few), few)
+        middle = x_ref[here, :].astype(f32) + (
+            branch_ref[here, :].astype(f32) + other_ref[here, :].astype(f32)
+        )
+        middle_ref[here, :] = middle
+        scale = lax.rsqrt(jnp.mean(middle * middle, axis=1, keepdims=True) + epsilon)
+        mid_normed_ref[here, :] = (middle * scale * gain_ref[1:2, :]).astype(bf16)
+        return unused
+
+    lax.fori_loop(0, x_ref.shape[0] // few, middle_rows, 0)
     came_over(down, last)
     for group in (gate, up, down):
         gathered(group)
@@ -331,11 +357,11 @@
             aside_far(group, s).wait_send()
     for s in range(last):
         kv_copy(s).wait_send()
-    exchange.wait()
+    exchange.wait_send()
     full.wait()
 
 
-def forward_all(packed, gate, up, down, x, cosine, sine, qi, ki, q_cols, ctxs):
+def forward_all(packed, gate, up, down, x, frequency, qi, q_cols, ctxs):
     rows, width = x.shape
     columns, hidden = sum(part.shape[1] for part in packed), gate.shape[1]
     groups = q_cols // 2 // HEAD_SIZE
@@ -346,8 +372,8 @@
     full = shape((rows, width), bf16)
     return pl.pallas_call(
         forward_kernel,
-        in_specs=[hbm] * (len(packed) + 3) + [vmem] * 5,
-        out_specs=[hbm] * 4 + [vmem] * 9,
+        in_specs=[hbm] * (len(packed) + 3) + [vmem] * 3,
+        out_specs=[hbm] * 4 + [vmem] * 12,
         out_shape=[
             shape((width, columns), bf16),
             shape((width, hidden), bf16),
@@ -360,10 +386,15 @@
             shape((rows, q_cols), bf16),
             shape((tiles, HEAD_SIZE, lanes), f32),
             shape((tiles, 1, lanes), f32),
+            shape((rows, width), f32),
             full,
-            full,
+            shape((rows, HALF), f32),
+            shape((rows, HALF), f32),
+            shape((ctxs, rows, 1), jnp.int32),
         ],
         scratch_shapes=[
+            pltpu.VMEM((rows, width), bf16),
+            pltpu.VMEM((rows, width), bf16),
             pltpu.VMEM((width, columns), bf16),
             pltpu.VMEM((tiles, HEAD_SIZE, lanes), bf16),
             pltpu.VMEM((tiles, 1, lanes), f32),
@@ -380,7 +411,7 @@
         ),
         cost_estimate=cost(1e10, 1e8),
         name="forward_all",
-    )(*packed, gate, up, down, x, cosine, sine, qi, ki)
+    )(*packed, gate, up, down, x, frequency, qi)
 
 
 def gather_stream(order, ctx, pieces, k_ref, v_ref):
@@ -1246,20 +1277,10 @@
 
 
 def feed_kernel(
-    x_ref, mine_ref, other_ref, gain_ref, cot_ref, gate_ref, up_ref, down_ref,
-    middle_ref, normed_ref, act_ref, back_ref, feed_ref, total_ref, feed_total,
+    normed_ref, cot_ref, gate_ref, up_ref, down_ref,
+    act_ref, back_ref, feed_ref, total_ref, feed_total,
 ):
     step = pl.program_id(0)
-
-    @pl.when(step == 0)
-    def _():
-        middle = (
-            x_ref[...].astype(f32) + mine_ref[...].astype(f32) + other_ref[...].astype(f32)
-        )
-        middle_ref[...] = middle
-        scale = lax.rsqrt(jnp.mean(middle * middle, axis=1, keepdims=True) + epsilon)
-        normed_ref[...] = (middle * scale * gain_ref[1:2, :]).astype(bf16)
-
     gate = dot(normed_ref[...], gate_ref[...], NN)
     upward = dot(normed_ref[...], up_ref[...], NN)
     back_mixed = dot(cot_ref[...], down_ref[...], NN)
@@ -1290,22 +1311,19 @@
         feed_ref[...] = feed_total[...].astype(bf16)
 
 
-def feed_forward(x, mine, other, gains, cotangent, gate, up, down):
-    rows, width = x.shape
+def feed_forward(normed, cotangent, gate, up, down):
+    rows, width = normed.shape
     hidden = gate.shape[1]
-    steps = hidden // TILE
-    tile_of = pl.BlockSpec((width, TILE), lambda j: (0, j))
-    acts_of = pl.BlockSpec((3, rows, TILE), lambda j: (0, 0, j))
+    steps = hidden // FEED_TILE
+    tile_of = pl.BlockSpec((width, FEED_TILE), lambda j: (0, j))
+    acts_of = pl.BlockSpec((3, rows, FEED_TILE), lambda j: (0, 0, j))
     full = whole((rows, width))
     return pl.pallas_call(
         feed_kernel,
         grid=(steps,),
-        in_specs=[full, full, full, whole(gains.shape), full]
-        + [tile_of] * 3,
-        out_specs=[full, full, acts_of, full, full],
+        in_specs=[full, full] + [tile_of] * 3,
+        out_specs=[acts_of, full, full],
         out_shape=[
-            jax.ShapeDtypeStruct((rows, width), f32),
-            jax.ShapeDtypeStruct((rows, width), bf16),
             jax.ShapeDtypeStruct((3, rows, hidden), bf16),
             jax.ShapeDtypeStruct((rows, width), bf16),
             jax.ShapeDtypeStruct((rows, width), bf16),
@@ -1314,7 +1332,7 @@
         compiler_params=params(56),
         cost_estimate=cost(12 * rows * width * hidden, 6 * width * hidden),
         name="feed_forward",
-    )(x, mine, other, gains, cotangent, gate, up, down)
+    )(normed, cotangent, gate, up, down)
 
 
 def middle_kernel(cot_ref, mine_ref, other_ref, middle_ref, gain_ref, w_ref, bm_ref, bb_ref, ba_ref, grad_ref):
@@ -1527,19 +1545,16 @@
     packed = (query_weight, key_weight, value_weight, gain_columns, output_weight)
     stream = streams(order, ctx)
     lows = jnp.max(jnp.where(starts[None, :] <= stream[0][:, None], starts[None, :], 0), axis=1)
-    cosine, sine = angles(stream[0] - lows)
     if pairs == 2 and ctxs == 4 and query_weight.shape[0] % 32 == 0:
-        qi = jnp.pad(jnp.stack([stream[0], lows]), ((0, 6), (0, 0)))
-        ki = stream[:, :, None]
+        own = jnp.stack([stream[0], lows])
+        qi = jnp.concatenate([own, stream, jnp.zeros_like(own)], axis=0)
         (
             first, gate_full, up_full, down_full, queries, kv, normed, gains,
-            attended_low, att, sums, branch, branch_other,
+            attended_low, att, sums, middle, mid_normed, cosine, sine, ki,
         ) = forward_all(
-            packed, gate_weight, up_weight, down_weight, tokens, cosine, sine, qi, ki, q_cols, ctxs
-        )
-        middle, mid_normed, act, back_part, feed = feed_forward(
-            tokens, branch, branch_other, gains, cotangent, gate_full, up_full, down_full
-        )
+            packed, gate_weight, up_weight, down_weight, tokens, frequencies(), qi, q_cols, ctxs
+        )
+        act, back_part, feed = feed_forward(mid_normed, cotangent, gate_full, up_full, down_full)
         _, _, _, result, token_gradient, grads, _, _ = back_all(
             back_part, feed, cotangent, middle, gains, act, mid_normed, tokens, normed,
             attended_low, queries, kv, att, sums, qi, ki, cosine, sine, first, ctxs,
@@ -1558,15 +1573,17 @@
             lax.all_gather(field, ROWS, axis=0, tiled=True)
             for field in (jnp.concatenate(packed, axis=1), gate_weight, up_weight, down_weight)
         )
+        cosine, sine = angles(stream[0] - lows)
         gains = first[:, 2 * q_cols : 2 * q_cols + 8].T.astype(f32)
         queries, kv, normed = project(tokens, gains, cosine, sine, first, q_cols)
         pieces = [kv] + [shifted(kv, "ctx", k) for k in range(1, ctxs)]
         output_weights = first[:, 2 * q_cols + LANES :]
         attended_low, att, sums = attend(order, starts, place, queries, pieces)
         branch = output_product(attended_low, output_weights, 0, features)
-        middle, mid_normed, act, back_part, feed = feed_forward(
-            tokens, branch, swapped(branch), gains, cotangent, gate_full, up_full, down_full
-        )
+        middle = tokens.astype(f32) + (branch.astype(f32) + swapped(branch).astype(f32))
+        mid_scale = lax.rsqrt(jnp.mean(middle * middle, axis=1, keepdims=True) + epsilon)
+        mid_normed = (middle * mid_scale * gains[1:2]).astype(bf16)
+        act, back_part, feed = feed_forward(mid_normed, cotangent, gate_full, up_full, down_full)
         back_other = swapped(back_part)
         gate_parts = gradient(mid_normed, act[0], pairs, ctxs)
         up_parts = gradient(mid_normed, act[1], pairs, ctxs)

time: 460 us -> 453 us (0.985)
  no operation moved by 1% of the time
where the time goes in v6:
time: 453 us; the launch traced here: 445 us
  Pallas kernels  428 us (94%)
  local copies, waits for them, and re-layouts  9.34 us (2%)
  other arithmetic  6.8 us (2%)
    pallas_call x1, Pallas kernels, back_all(): pl.pallas_call(back_kernel, in_specs=[hbm] * 4 + [vmem] + [hbm] * 4 + [vm...  210 us
    pallas_call x1, Pallas kernels, forward_all(): pl.pallas_call(forward_kernel, in_specs=[hbm] * (len(packed) + 3) + [vmem...  187 us
    pallas_call x1, Pallas kernels, feed_forward(): pl.pallas_call(feed_kernel, grid=(steps,), in_specs=[full, full] + [tile_...  29.8 us

profile of v6, /device:TPU:0, one launch (start us, length us, event | category | flops | bytes accessed | tf_op | source)
XLA Modules:
  0.0 444.8 jit_solution(1749720725599848775)
XLA Ops:
  0.6 0.0 copy-start
  0.7 0.7 copy-done
  1.3 0.7 pad_maximum_fusion.6
  2.0 0.8 reduce-window_clone.1
  2.8 0.7 subtract_bitcast_fusion
  3.5 0.1 pad.26.clone
  3.6 0.6 gather_fusion
  4.2 0.1 iota_add_fusion
  4.2 0.1 slice.88
  4.3 0.1 le.19
  4.4 0.1 select_reduce_fusion
  4.5 0.1 add.64
  4.6 0.1 add.59
  4.6 0.1 add.62
  4.7 0.7 add_add_fusion.qi_ref
  5.4 0.1 copy.30
  5.5 0.6 pad.4.gain_shard
  6.1 187.4 %forward_all.1 = (bf16[1536,2432]{1,0:T(8,128)(2,1)}, bf16[1536,2048]{1,0:T(8,128)(2,1)}, bf16[1536,2048]{1,0:T(8,128)(2,1)}, bf16[1536,2048]{1,0:T(8,128)(2,1)}...) custom-call(bf16[96,768]{1,0:T(8,128)(2,1)} %query_shard.1, ...), custom_call_target="tpu_custom_call" | custom-call | flops 10000000000 | bytes 100000000 | tf_op jit(solution)/shard_map/forward_all/pallas_call | solution.py:373
  193.6 29.8 %feed_forward.1 = (bf16[3,512,2048]{2,1,0:T(8,128)(2,1)}, bf16[512,1536]{1,0:T(8,128)(2,1)}, bf16[512,1536]{1,0:T(8,128)(2,1)}) custom-call(bf16[512,1536]{1,0:T(8,128)(2,1)} %get-tuple-element.33.normed_ref.mid_normed_hbm, bf16[512,1536]{1,0:T(8,128)(2,1)} %cot_hbm.1, bf16[1536,2048]{1,0:T(8,128)(2,1)} %get-tuple-element.34.gate_ref, ...), custom_call_target="tpu_custom_call" | custom-call | flops 19327352832 | bytes 18874368 | tf_op jit(solution)/shard_map/feed_forward/pallas_call | solution.py:1321
  223.4 210.4 %back_all.1 = (bf16[512,1536]{1,0:T(8,128)(2,1)}, f32[512,1536]{1,0:T(8,128)}, bf16[512,1536]{1,0:T(8,128)(2,1)}, bf16[512,1536]{1,0:T(8,128)(2,1)}, bf16[512,15...) custom-call(bf16[512,1536]{1,0:T(8,128)(2,1)} %get-tuple-element.37.part, ...), custom_call_target="tpu_custom_call" | custom-call | flops 40000000000 | bytes 100000000 | tf_op jit(solution)/shard_map/back_all/pallas_call | solution.py:1221
  433.8 2.4 slice_bitcast_fusion.3
  436.2 0.9 pad_maximum_fusion.2
  437.1 0.7 slice_reduce_fusion
  437.8 0.7 pad_maximum_fusion.5
  438.6 0.9 pad_maximum_fusion.3
  439.4 0.0 copy-start.3
  439.4 1.3 pad_maximum_fusion
  440.7 0.7 copy-done.3
  441.4 0.0 copy-start.2
  441.4 0.0 copy-start.1
  441.4 1.1 copy.33
  442.6 0.8 copy-done.2
  443.4 1.1 copy.34
  444.5 0.0 copy-done.1
  (10 shorter events, 0.1 us)
Async XLA Ops:
  0.6 0.7 copy-start
  439.4 2.0 copy-start.3
  441.4 2.0 copy-start.2
  441.4 3.1 copy-start.1

commit v7 on v6

--- a/solution.py
+++ b/solution.py
@@ -144,10 +144,12 @@
 def forward_kernel(
     query_shard, key_shard, value_shard, gain_shard, out_shard, gate_shard, up_shard, down_shard,
     x_ref, frequency_ref, qi_ref,
-    full_ref, gate_ref, up_ref, down_ref, q_ref, kv_ref, normed_ref, gain_ref, low_ref, att_ref, sum_ref,
+    full_ref, gate_ref, up_ref, down_ref, q_out, kv_out, normed_out, gain_out, low_out, att_out, sum_out,
+    middle_out, mid_normed_out, cos_out, sin_out, ki_out,
+    q_ref, kv_ref, normed_ref, gain_ref, low_ref, att_ref, sum_ref,
     middle_ref, mid_normed_ref, cos_ref, sin_ref, ki_ref,
     branch_ref, other_ref, w_ref, qt_ref, top_ref, total_ref,
-    z_send, z_recv, y_send, y_recv, c_send, c_recv, k_send, k_recv, x_send, x_recv, local,
+    z_send, z_recv, y_send, y_recv, c_send, c_recv, k_send, k_recv, x_send, x_recv, local, save_sem,
 ):
     ctxs = lax.axis_size("ctx")
     dp, ctx, tp = lax.axis_index("dp"), lax.axis_index("ctx"), lax.axis_index("tp")
@@ -228,6 +230,13 @@
         for s in range(ctxs):
             aside(group, s).wait_recv()
             aside_far(group, s).wait_recv()
+
+    saves = []
+
+    def save(*pairs):
+        for have, out in pairs:
+            saves.append(pltpu.make_async_copy(have, out, save_sem.at[len(saves)]))
+            saves[-1].start()
 
     first, gate, up, down = range(4)
     for copy in packs:
@@ -262,6 +271,7 @@
     gains = w_ref[:, 2 * q_cols : 2 * q_cols + LANES].astype(f32).T[:8]
     gain_ref[...] = gains
     normed_ref[...] = (unit * gains[0:1]).astype(bf16)
+    save((gain_ref, gain_out), (normed_ref, normed_out), (cos_ref, cos_out), (sin_ref, sin_out), (ki_ref, ki_out))
 
     def product(step):
         return dot(normed_ref[...], w_ref[:, step * tile : (step + 1) * tile], NN)
@@ -316,7 +326,9 @@
         return unused
 
     lax.fori_loop(0, ctxs, attention_step, 0)
+    save((q_ref, q_out), (kv_ref, kv_out))
     dense_end(groups, ratio, top_ref, total_ref, att_ref, sum_ref, low_ref)
+    save((low_ref, low_out), (att_ref, att_out), (sum_ref, sum_out))
     branch_ref[...] = dot(low_ref[...], w_ref[:, 2 * q_cols + LANES :], NT).astype(bf16)
     exchange = remote(branch_ref, other_ref, across, x_send.at[0], x_recv.at[0])
     exchange.start()
@@ -345,6 +357,7 @@
         return unused
 
     lax.fori_loop(0, x_ref.shape[0] // few, middle_rows, 0)
+    save((middle_ref, middle_out), (mid_normed_ref, mid_normed_out))
     came_over(down, last)
     for group in (gate, up, down):
         gathered(group)
@@ -359,6 +372,8 @@
         kv_copy(s).wait_send()
     exchange.wait_send()
     full.wait()
+    for copy in saves:
+        copy.wait()
 
 
 def forward_all(packed, gate, up, down, x, frequency, qi, q_cols, ctxs):
@@ -370,29 +385,33 @@
     sems = lambda *n: pltpu.SemaphoreType.DMA(n)
     shape = jax.ShapeDtypeStruct
     full = shape((rows, width), bf16)
+    kept = [
+        shape((rows, q_cols), bf16),
+        shape((ctxs, rows, q_cols), bf16),
+        full,
+        shape((8, width), f32),
+        shape((rows, q_cols), bf16),
+        shape((tiles, HEAD_SIZE, lanes), f32),
+        shape((tiles, 1, lanes), f32),
+        shape((rows, width), f32),
+        full,
+        shape((rows, HALF), f32),
+        shape((rows, HALF), f32),
+        shape((ctxs, rows, 1), jnp.int32),
+    ]
     return pl.pallas_call(
         forward_kernel,
         in_specs=[hbm] * (len(packed) + 3) + [vmem] * 3,
-        out_specs=[hbm] * 4 + [vmem] * 12,
+        out_specs=[hbm] * 16,
         out_shape=[
             shape((width, columns), bf16),
             shape((width, hidden), bf16),
             shape((width, hidden), bf16),
             shape((width, hidden), bf16),
-            shape((rows, q_cols), bf16),
-            shape((ctxs, rows, q_cols), bf16),
-            full,
-            shape((8, width), f32),
-            shape((rows, q_cols), bf16),
-            shape((tiles, HEAD_SIZE, lanes), f32),
-            shape((tiles, 1, lanes), f32),
-            shape((rows, width), f32),
-            full,
-            shape((rows, HALF), f32),
-            shape((rows, HALF), f32),
-            shape((ctxs, rows, 1), jnp.int32),
-        ],
-        scratch_shapes=[
+        ]
+        + kept,
+        scratch_shapes=[pltpu.VMEM(part.shape, part.dtype) for part in kept]
+        + [
             pltpu.VMEM((rows, width), bf16),
             pltpu.VMEM((rows, width), bf16),
             pltpu.VMEM((width, columns), bf16),
@@ -405,7 +424,7 @@
         + [sems(4, 2 * ctxs)] * 2
         + [sems(ctxs - 1)] * 2
         + [sems(1)] * 2
-        + [sems(5 + len(packed))],
+        + [sems(5 + len(packed)), sems(len(kept))],
         compiler_params=pltpu.CompilerParams(
             vmem_limit_bytes=56 * MIB, collective_id=0, has_side_effects=True
         ),
@@ -712,8 +731,9 @@
 
 def back_kernel(
     part_hbm, feed_hbm, cot_hbm, middle_hbm, gain_ref, act_hbm, mid_normed_hbm, x_hbm, normed_hbm,
-    low_ref, q_ref, kv_ref, att_ref, sum_ref, qi_ref, ki_ref, cos_ref, sin_ref, weight_hbm,
+    low_hbm, q_hbm, kv_hbm, att_hbm, sum_hbm, qi_hbm, ki_hbm, cos_hbm, sin_hbm, weight_hbm,
     feed_other, back_middle, part2_other, result_ref, token_ref, grads_ref, held_hbm, far_hbm,
+    low_ref, q_ref, kv_ref, att_ref, sum_ref, qi_ref, ki_ref, cos_ref, sin_ref,
     lhs, mid, part, part_other, w_out, w_in, rhs, q2, q2t, d2, d2t, delta, bias_ref, dq_ref,
     kv_sent, kv_got, cot, gain_rows, gain_other, gain_columns,
     p_send, p_keep, c_got, s_one, own, y_got, z_got,
@@ -889,8 +909,13 @@
         load(weight_hbm.at[:, pl.ds(2 * q_cols + LANES, q_cols)], w_out, 4),
         load(weight_hbm.at[:, pl.ds(0, 2 * q_cols)], w_in, 5),
     ]
+    later = (
+        (low_hbm, low_ref), (q_hbm, q_ref), (kv_hbm, kv_ref), (att_hbm, att_ref), (sum_hbm, sum_ref),
+        (qi_hbm, qi_ref), (ki_hbm, ki_ref), (cos_hbm, cos_ref), (sin_hbm, sin_ref),
+    )
+    later = [load(have, into, 21 + j) for j, (have, into) in enumerate(later)]
     act_copy(0).start()
-    for copy in loads:
+    for copy in loads + later:
         copy.start()
     loads[0].wait()
     loads[1].wait()
@@ -930,6 +955,8 @@
     meet_core(FEED_TILES - 1)
     send_far(FEED_TILES - 2)
     send_far(FEED_TILES - 1)
+    for copy in later:
+        copy.wait()
 
     for q_tile in range(rows // SIDE):
         for g in range(groups):
@@ -1220,7 +1247,7 @@
     pairs = (rows // SIDE) * (rows // SIDE + 1) // 2
     return pl.pallas_call(
         back_kernel,
-        in_specs=[hbm] * 4 + [vmem] + [hbm] * 4 + [vmem] * 9 + [hbm],
+        in_specs=[hbm] * 4 + [vmem] + [hbm] * 14,
         out_specs=[hbm] * 5 + [vmem] + [hbm] * 2,
         out_shape=[
             full,
@@ -1232,7 +1259,8 @@
             jax.ShapeDtypeStruct((TILES, 2 * section, TILE), bf16),
             jax.ShapeDtypeStruct((TILES, section, TILE), bf16),
         ],
-        scratch_shapes=[
+        scratch_shapes=[pltpu.VMEM(part_in.shape, part_in.dtype) for part_in in (low, queries, kv, att, sums, qi, ki, cosine, sine)]
+        + [
             space(2, rows, width), wide(rows, width), space(rows, width), space(rows, width),
             space(width, q_cols), space(width, 2 * q_cols), space(2, rows, TILE),
             space(tiles, lanes, HEAD_SIZE), space(tiles, HEAD_SIZE, lanes),
@@ -1243,7 +1271,7 @@
             space(2, 2 * section, TILE), space(2, 2 * section, TILE), space(4, 2 * section, TILE),
             space(2, 2 * section, TILE), space(SLOTS, section, TILE), space(2, section, TILE),
             space(TILES, (ctxs - 1) * piece, TILE),
-            sems(21), sems(FEED_TILES), sems(4), sems(4), sems(TILES), sems(TILES),
+            sems(30), sems(FEED_TILES), sems(4), sems(4), sems(TILES), sems(TILES),
             pltpu.SemaphoreType.REGULAR, sems(TILES), sems(TILES), sems(TILES), sems(TILES, 2),
             sems(TILES, 2), sems(TILES, 2), sems(ctxs - 1), sems(ctxs - 1),
         ],

time: 453 us -> 448 us (0.989)
  Pallas kernels: 428 us -> 423 us
    pallas_call x1, Pallas kernels: 187 us -> 183 us  [forward_all(): pl.pallas_call(forward_kernel, in_specs=[hbm] * (len(packed) + 3) + [vmem...]
where the time goes in v7:
time: 448 us; the launch traced here: 440 us
  Pallas kernels  423 us (94%)
  local copies, waits for them, and re-layouts  9.34 us (2%)
  other arithmetic  6.8 us (2%)
    pallas_call x1, Pallas kernels, back_all(): pl.pallas_call(back_kernel, in_specs=[hbm] * 4 + [vmem] + [hbm] * 14, out...  210 us
    pallas_call x1, Pallas kernels, forward_all(): pl.pallas_call(forward_kernel, in_specs=[hbm] * (len(packed) + 3) + [vmem...  183 us
    pallas_call x1, Pallas kernels, feed_forward(): pl.pallas_call(feed_kernel, grid=(steps,), in_specs=[full, full] + [tile_...  29.8 us

profile of v7, /device:TPU:0, one launch (start us, length us, event | category | flops | bytes accessed | tf_op | source)
XLA Modules:
  0.0 439.8 jit_solution(8949774249882345513)
XLA Ops:
  0.6 0.0 copy-start
  0.7 0.7 copy-done
  1.3 0.7 pad_maximum_fusion.6
  2.0 0.8 reduce-window_clone.1
  2.8 0.7 subtract_bitcast_fusion
  3.5 0.1 pad.26.clone
  3.6 0.6 gather_fusion
  4.2 0.1 iota_add_fusion
  4.2 0.1 slice.88
  4.3 0.1 le.19
  4.4 0.1 select_reduce_fusion
  4.5 0.1 add.64
  4.6 0.1 add.59
  4.6 0.1 add.62
  4.7 0.7 add_add_fusion.qi_ref.qi_hbm
  5.4 0.1 copy.30
  5.5 0.6 pad.4.gain_shard
  6.1 182.5 %forward_all.1 = (bf16[1536,2432]{1,0:T(8,128)(2,1)}, bf16[1536,2048]{1,0:T(8,128)(2,1)}, bf16[1536,2048]{1,0:T(8,128)(2,1)}, bf16[1536,2048]{1,0:T(8,128)(2,1)}...) custom-call(bf16[96,768]{1,0:T(8,128)(2,1)} %query_shard.1, ...), custom_call_target="tpu_custom_call" | custom-call | flops 10000000000 | bytes 100000000 | tf_op jit(solution)/shard_map/forward_all/pallas_call | solution.py:402
  188.7 29.8 %feed_forward.1 = (bf16[3,512,2048]{2,1,0:T(8,128)(2,1)}, bf16[512,1536]{1,0:T(8,128)(2,1)}, bf16[512,1536]{1,0:T(8,128)(2,1)}) custom-call(bf16[512,1536]{1,0:T(8,128)(2,1)} %get-tuple-element.33.normed_ref.mid_normed_hbm, bf16[512,1536]{1,0:T(8,128)(2,1)} %cot_hbm.1, bf16[1536,2048]{1,0:T(8,128)(2,1)} %get-tuple-element.34.gate_ref, ...), custom_call_target="tpu_custom_call" | custom-call | flops 19327352832 | bytes 18874368 | tf_op jit(solution)/shard_map/feed_forward/pallas_call | solution.py:1349
  218.5 210.4 %back_all.1 = (bf16[512,1536]{1,0:T(8,128)(2,1)}, f32[512,1536]{1,0:T(8,128)}, bf16[512,1536]{1,0:T(8,128)(2,1)}, bf16[512,1536]{1,0:T(8,128)(2,1)}, bf16[512,15...) custom-call(bf16[512,1536]{1,0:T(8,128)(2,1)} %get-tuple-element.37.part, ...), custom_call_target="tpu_custom_call" | custom-call | flops 40000000000 | bytes 100000000 | tf_op jit(solution)/shard_map/back_all/pallas_call | solution.py:1248
  428.9 2.4 slice_bitcast_fusion.3
  431.2 0.9 pad_maximum_fusion.2
  432.2 0.7 slice_reduce_fusion
  432.9 0.7 pad_maximum_fusion.5
  433.6 0.9 pad_maximum_fusion.3
  434.5 0.0 copy-start.3
  434.5 1.3 pad_maximum_fusion
  435.7 0.7 copy-done.3
  436.4 0.0 copy-start.2
  436.4 0.0 copy-start.1
  436.4 1.1 copy.33
  437.6 0.8 copy-done.2
  438.4 1.1 copy.34
  439.6 0.0 copy-done.1
  (10 shorter events, 0.1 us)
Async XLA Ops:
  0.6 0.7 copy-start
  434.5 2.0 copy-start.3
  436.4 2.0 copy-start.2
  436.4 3.1 copy-start.1

commit v8 on v7

--- a/solution.py
+++ b/solution.py
@@ -725,7 +725,7 @@
 
 FEED_TILES = 12
 TILES = 17
-EARLY = 5
+EARLY = 4
 SLOTS = 6
 
 
@@ -935,11 +935,16 @@
 
         product(t, lambda lanes: lhs[t // 8, :, lanes], plain(t))
 
-        @pl.when(t >= 1)
+        @pl.when(t == 0)
+        def _():
+            meet_core(t)
+            send_far(t)
+
+        @pl.when(t >= 2)
         def _():
             meet_core(t - 1)
 
-        @pl.when(t >= 2)
+        @pl.when(t >= 3)
         def _():
             send_far(t - 2)
 
@@ -969,7 +974,7 @@
 
     loads[2].wait()
     loads[3].wait()
-    t_1, t_2, t_3, t_4, t_5 = (jnp.int32(j) for j in range(1, 6))
+    t_1, t_2, t_3, t_4 = (jnp.int32(j) for j in range(1, 5))
     fetch(t_3)
     meet_last(t_1)
     meet_near(t_2)
@@ -1005,7 +1010,6 @@
     cot[:, :q_cols] = dot(lhs[0], w_out[...], NN).astype(bf16)
     meet_far(t_4)
     meet_near(t_3)
-    fetch(t_5)
     for q_tile in range(rows // SIDE):
         for g in range(groups):
             i = q_tile * groups + g
@@ -1014,9 +1018,6 @@
             d2[i] = flat
             d2t[i] = turned_flat.astype(bf16)
             delta[i] = jnp.sum(turned_flat * att_ref[i], axis=0, keepdims=True)
-    meet_last(t_3)
-    meet_far(t_5)
-    meet_near(t_4)
 
     t_out = jnp.int32(FEED_TILES)
     product(
@@ -1060,9 +1061,9 @@
             meet_core(t_out)
             send_far(t_out)
 
-        @pl.when((s == 1) | (s == 3))
+        @pl.when((s == 0) | (s == 2))
         def _():
-            tick(6 + s // 2)
+            tick(5 + s // 2)
 
         return unused
 
@@ -1083,6 +1084,7 @@
 
 
     kv_pass(0)
+    tick(jnp.int32(7))
     for i in range(dq_ref.shape[0]):
         q_tile, g = divmod(i, groups)
         here = slice(q_tile * SIDE, (q_tile + 1) * SIDE)

time: 448 us -> 446 us (level)
  no operation moved by 1% of the time
where the time goes in v8:
time: 446 us; the launch traced here: 438 us
  Pallas kernels  421 us (94%)
  local copies, waits for them, and re-layouts  9.34 us (2%)
  other arithmetic  6.8 us (2%)
    pallas_call x1, Pallas kernels, back_all(): pl.pallas_call(back_kernel, in_specs=[hbm] * 4 + [vmem] + [hbm] * 14, out...  209 us
    pallas_call x1, Pallas kernels, forward_all(): pl.pallas_call(forward_kernel, in_specs=[hbm] * (len(packed) + 3) + [vmem...  183 us
    pallas_call x1, Pallas kernels, feed_forward(): pl.pallas_call(feed_kernel, grid=(steps,), in_specs=[full, full] + [tile_...  29.8 us

profile of v8, /device:TPU:0, one launch (start us, length us, event | category | flops | bytes accessed | tf_op | source)
XLA Modules:
  0.0 438.1 jit_solution(8007486262209269452)
XLA Ops:
  0.6 0.0 copy-start
  0.7 0.7 copy-done
  1.3 0.7 pad_maximum_fusion.6
  2.0 0.8 reduce-window_clone.1
  2.8 0.7 subtract_bitcast_fusion
  3.5 0.1 pad.26.clone
  3.6 0.6 gather_fusion
  4.2 0.1 iota_add_fusion
  4.2 0.1 slice.88
  4.3 0.1 le.19
  4.4 0.1 select_reduce_fusion
  4.5 0.1 add.64
  4.6 0.1 add.59
  4.6 0.1 add.62
  4.7 0.7 add_add_fusion.qi_ref.qi_hbm
  5.4 0.1 copy.30
  5.5 0.6 pad.4.gain_shard
  6.1 182.5 %forward_all.1 = (bf16[1536,2432]{1,0:T(8,128)(2,1)}, bf16[1536,2048]{1,0:T(8,128)(2,1)}, bf16[1536,2048]{1,0:T(8,128)(2,1)}, bf16[1536,2048]{1,0:T(8,128)(2,1)}...) custom-call(bf16[96,768]{1,0:T(8,128)(2,1)} %query_shard.1, ...), custom_call_target="tpu_custom_call" | custom-call | flops 10000000000 | bytes 100000000 | tf_op jit(solution)/shard_map/forward_all/pallas_call | solution.py:402
  188.7 29.8 %feed_forward.1 = (bf16[3,512,2048]{2,1,0:T(8,128)(2,1)}, bf16[512,1536]{1,0:T(8,128)(2,1)}, bf16[512,1536]{1,0:T(8,128)(2,1)}) custom-call(bf16[512,1536]{1,0:T(8,128)(2,1)} %get-tuple-element.33.normed_ref.mid_normed_hbm, bf16[512,1536]{1,0:T(8,128)(2,1)} %cot_hbm.1, bf16[1536,2048]{1,0:T(8,128)(2,1)} %get-tuple-element.34.gate_ref, ...), custom_call_target="tpu_custom_call" | custom-call | flops 19327352832 | bytes 18874368 | tf_op jit(solution)/shard_map/feed_forward/pallas_call | solution.py:1351
  218.5 208.7 %back_all.1 = (bf16[512,1536]{1,0:T(8,128)(2,1)}, f32[512,1536]{1,0:T(8,128)}, bf16[512,1536]{1,0:T(8,128)(2,1)}, bf16[512,1536]{1,0:T(8,128)(2,1)}, bf16[512,15...) custom-call(bf16[512,1536]{1,0:T(8,128)(2,1)} %get-tuple-element.37.part, ...), custom_call_target="tpu_custom_call" | custom-call | flops 40000000000 | bytes 100000000 | tf_op jit(solution)/shard_map/back_all/pallas_call | solution.py:1250
  427.2 2.4 slice_bitcast_fusion.3
  429.6 0.9 pad_maximum_fusion.2
  430.5 0.7 slice_reduce_fusion
  431.2 0.7 pad_maximum_fusion.5
  432.0 0.9 pad_maximum_fusion.3
  432.8 0.0 copy-start.3
  432.8 1.3 pad_maximum_fusion
  434.1 0.7 copy-done.3
  434.8 0.0 copy-start.2
  434.8 0.0 copy-start.1
  434.8 1.1 copy.33
  435.9 0.8 copy-done.2
  436.8 1.1 copy.34
  437.9 0.0 copy-done.1
  (10 shorter events, 0.1 us)
Async XLA Ops:
  0.6 0.7 copy-start
  432.8 2.0 copy-start.3
  434.8 2.0 copy-start.2
  434.8 3.1 copy-start.1

commit v9 on v8

--- a/solution.py
+++ b/solution.py
@@ -256,7 +256,6 @@
         came_over(first, s - 1)
     ring(gate, 0).start()
     begin(gate)
-    ring(up, 0).start()
     came_over(first, last)
     begin(up)
     gathered(first)
@@ -291,6 +290,7 @@
         return remote(kv_ref.at[s], kv_ref.at[s + 1], after, k_send.at[s], k_recv.at[s])
 
     kv_copy(0).start()
+    ring(up, 0).start()
     begin(down)
     for step in range(2):
 

time: 446 us -> 453 us (1.016)
  Pallas kernels: 421 us -> 427 us
    pallas_call x1, Pallas kernels: 183 us -> 188 us  [forward_all(): pl.pallas_call(forward_kernel, in_specs=[hbm] * (len(packed) + 3) + [vmem...]
where the time goes in v9:
time: 453 us; the launch traced here: 444 us
  Pallas kernels  427 us (94%)
  local copies, waits for them, and re-layouts  9.34 us (2%)
  other arithmetic  6.8 us (2%)
    pallas_call x1, Pallas kernels, back_all(): pl.pallas_call(back_kernel, in_specs=[hbm] * 4 + [vmem] + [hbm] * 14, out...  210 us
    pallas_call x1, Pallas kernels, forward_all(): pl.pallas_call(forward_kernel, in_specs=[hbm] * (len(packed) + 3) + [vmem...  188 us
    pallas_call x1, Pallas kernels, feed_forward(): pl.pallas_call(feed_kernel, grid=(steps,), in_specs=[full, full] + [tile_...  29.8 us

profile of v9, /device:TPU:0, one launch (start us, length us, event | category | flops | bytes accessed | tf_op | source)
XLA Modules:
  0.0 444.4 jit_solution(15869252546741443983)
XLA Ops:
  0.6 0.0 copy-start
  0.7 0.7 copy-done
  1.3 0.7 pad_maximum_fusion.6
  2.0 0.8 reduce-window_clone.1
  2.8 0.7 subtract_bitcast_fusion
  3.5 0.1 pad.26.clone
  3.6 0.6 gather_fusion
  4.2 0.1 iota_add_fusion
  4.2 0.1 slice.88
  4.3 0.1 le.19
  4.4 0.1 select_reduce_fusion
  4.5 0.1 add.64
  4.6 0.1 add.59
  4.6 0.1 add.62
  4.7 0.7 add_add_fusion.qi_ref.qi_hbm
  5.4 0.1 copy.30
  5.5 0.6 pad.4.gain_shard
  6.1 187.8 %forward_all.1 = (bf16[1536,2432]{1,0:T(8,128)(2,1)}, bf16[1536,2048]{1,0:T(8,128)(2,1)}, bf16[1536,2048]{1,0:T(8,128)(2,1)}, bf16[1536,2048]{1,0:T(8,128)(2,1)}...) custom-call(bf16[96,768]{1,0:T(8,128)(2,1)} %query_shard.1, ...), custom_call_target="tpu_custom_call" | custom-call | flops 10000000000 | bytes 100000000 | tf_op jit(solution)/shard_map/forward_all/pallas_call | solution.py:402
  193.9 29.8 %feed_forward.1 = (bf16[3,512,2048]{2,1,0:T(8,128)(2,1)}, bf16[512,1536]{1,0:T(8,128)(2,1)}, bf16[512,1536]{1,0:T(8,128)(2,1)}) custom-call(bf16[512,1536]{1,0:T(8,128)(2,1)} %get-tuple-element.33.normed_ref.mid_normed_hbm, bf16[512,1536]{1,0:T(8,128)(2,1)} %cot_hbm.1, bf16[1536,2048]{1,0:T(8,128)(2,1)} %get-tuple-element.34.gate_ref, ...), custom_call_target="tpu_custom_call" | custom-call | flops 19327352832 | bytes 18874368 | tf_op jit(solution)/shard_map/feed_forward/pallas_call | solution.py:1351
  223.7 209.7 %back_all.1 = (bf16[512,1536]{1,0:T(8,128)(2,1)}, f32[512,1536]{1,0:T(8,128)}, bf16[512,1536]{1,0:T(8,128)(2,1)}, bf16[512,1536]{1,0:T(8,128)(2,1)}, bf16[512,15...) custom-call(bf16[512,1536]{1,0:T(8,128)(2,1)} %get-tuple-element.37.part, ...), custom_call_target="tpu_custom_call" | custom-call | flops 40000000000 | bytes 100000000 | tf_op jit(solution)/shard_map/back_all/pallas_call | solution.py:1250
  433.4 2.4 slice_bitcast_fusion.3
  435.8 0.9 pad_maximum_fusion.2
  436.7 0.7 slice_reduce_fusion
  437.5 0.7 pad_maximum_fusion.5
  438.2 0.9 pad_maximum_fusion.3
  439.0 0.0 copy-start.3
  439.1 1.3 pad_maximum_fusion
  440.3 0.7 copy-done.3
  441.0 0.0 copy-start.2
  441.0 0.0 copy-start.1
  441.0 1.1 copy.33
  442.2 0.8 copy-done.2
  443.0 1.1 copy.34
  444.1 0.0 copy-done.1
  (10 shorter events, 0.1 us)
Async XLA Ops:
  0.6 0.7 copy-start
  439.0 2.0 copy-start.3
  441.0 2.0 copy-start.2
  441.0 3.1 copy-start.1
